TPU v7x, 32 devices: a whole 2x2x4 slice. The times are simulated.
32 devices in a mesh: groups: 2 (over x), adapter: 4 (over y, core), dp: 4 (over z).
Axes of the slice: x: 2, y: 2, z: 4, core: 2. Of those that a mesh axis runs over, the one named last changes fastest.
Arguments:
- acts: bfloat16 [16384, 8192], P(('groups', 'dp'), 'adapter'), parts along dimension 0, may hold values from -6 to 6
- out_grad: bfloat16 [16384, 2048], P(('groups', 'dp'), 'adapter'), parts along dimension 0, may hold values from -1.5 to 1.5
- tenant_ids: int32 [128, 1], P(('groups', 'dp')), parts along dimension 0, may hold values from 0 to 3
- slot_map: int32 [8], P('groups'), parts along dimension 0, may hold values from 0 to 3, each once
- down_pool: bfloat16 [8, 8192, 128], P(('groups', 'adapter')), parts along dimension 0, may hold values from -0.0625 to 0.0625
- up_pool: bfloat16 [8, 64, 2048], P(('groups', 'adapter')), parts along dimension 0, may hold values from -0.75 to 0.75
Outputs:
- acts_grad: bfloat16 [16384, 8192], P(('groups', 'dp'), 'adapter'), parts along dimension 0
- down_grad: bfloat16 [8, 8192, 128], P(('groups', 'adapter')), parts along dimension 0
- up_grad: bfloat16 [8, 64, 2048], P(('groups', 'adapter')), parts along dimension 0
There are 2 independent parts, one for each index of `groups`. A program takes and returns all parts, laid end to end along the dimension named above; each array names one. Nothing has to cross between parts.
Inputs may be any that keep to these rules, and one draw needn't show every extreme that they name: `tenant_ids`: every tenant owns at least one block. `slot_map`: each pool row belongs to exactly one tenant.
All inputs are finite; a program needn't handle non-finite values.
Results may differ from a plain program's by a relative error of at most 0.0052.
Values may be sent and summed in bfloat16 or wider, within the bound.
No kernel may reach another device: no remote copies, remote signals or barrier semaphores. Data moves between devices by JAX's collectives and lax.ppermute only.
A program may use at most 192 MiB of HBM per device.

v0:
```python
import jax
import jax.numpy as jnp
from jax import lax
from jax.sharding import PartitionSpec as P

DKV = 1024
R = 64
BLOCK = 128


def local(acts, out_grad, tenant_ids, slot_map, down_pool, up_pool):
    position = lax.axis_index("adapter")
    row_count, local_width = acts.shape
    col_count = out_grad.shape[1]
    block_count = row_count // BLOCK
    tenant_slot = slot_map[tenant_ids[:, 0]]
    down_slices = lax.all_to_all(down_pool, "adapter", split_axis=1, concat_axis=0, tiled=True)
    up_slices = lax.all_to_all(up_pool, "adapter", split_axis=2, concat_axis=0, tiled=True)
    tenant_count = down_slices.shape[0]
    acts_blocks = acts.reshape(block_count, BLOCK, local_width)
    grad_blocks = out_grad.reshape(block_count, BLOCK, col_count)
    down_blocks = down_slices[tenant_slot]
    up_blocks = up_slices[tenant_slot]
    shrunk_part = jnp.einsum(
        "bnd,bdr->bnr", acts_blocks, down_blocks, preferred_element_type=jnp.float32
    )
    back_part = jnp.einsum(
        "bnc,brc->bnr", grad_blocks, up_blocks, preferred_element_type=jnp.float32
    )
    is_key = position * col_count < DKV
    zero_part = jnp.zeros_like(back_part)
    d_part = jnp.where(
        is_key,
        jnp.concatenate([back_part, zero_part], axis=-1),
        jnp.concatenate([zero_part, back_part], axis=-1),
    )
    shrunk_sum, d_sum = lax.psum((shrunk_part, d_part), "adapter")
    shrunk = shrunk_sum.astype(jnp.bfloat16)
    d_shrunk = d_sum.astype(jnp.bfloat16)
    acts_grad = jnp.einsum(
        "bnr,bdr->bnd", d_shrunk, down_blocks, preferred_element_type=jnp.float32
    )
    acts_grad = acts_grad.astype(jnp.bfloat16).reshape(row_count, local_width)
    part_down = jnp.einsum(
        "bnd,bnr->bdr", acts_blocks, d_shrunk, preferred_element_type=jnp.float32
    )
    own_shrunk = jnp.where(is_key, shrunk[..., :R], shrunk[..., R:])
    part_up = jnp.einsum(
        "bnr,bnc->brc", own_shrunk, grad_blocks, preferred_element_type=jnp.float32
    )
    member = (tenant_slot[None, :] == jnp.arange(tenant_count, dtype=jnp.int32)[:, None]).astype(
        jnp.float32
    )
    grad_down = jnp.einsum("tb,bdr->tdr", member, part_down, precision=lax.Precision.HIGHEST)
    grad_up = jnp.einsum("tb,brc->trc", member, part_up, precision=lax.Precision.HIGHEST)
    owned_down = lax.all_to_all(grad_down, "adapter", split_axis=0, concat_axis=1, tiled=True)
    owned_up = lax.all_to_all(grad_up, "adapter", split_axis=0, concat_axis=2, tiled=True)
    total_down, total_up = lax.psum((owned_down, owned_up), "dp")
    down_grad = total_down.astype(jnp.bfloat16)
    up_grad = total_up.astype(jnp.bfloat16)
    return (acts_grad, down_grad, up_grad)


def solution(mesh):
    return jax.shard_map(
        local,
        mesh=mesh,
        in_specs=(
            P(("groups", "dp"), "adapter"),
            P(("groups", "dp"), "adapter"),
            P(("groups", "dp"), None),
            P("groups"),
            P(("groups", "adapter"), None, None),
            P(("groups", "adapter"), None, None),
        ),
        out_specs=(
            P(("groups", "dp"), "adapter"),
            P(("groups", "adapter"), None, None),
            P(("groups", "adapter"), None, None),
        ),
        check_vma=False,
    )
```

profile of v0, /device:TPU:0, one launch (start us, length us, event | category | flops | bytes accessed | tf_op | source)
XLA Modules:
  0.0 444.1 jit_solution(405307777434382479)
XLA Ops:
  0.6 0.0 copy-start
  0.6 2.4 copy.30
  3.0 0.5 broadcast.43
  3.6 12.3 %reduce.1 = bf16[2048,64]{1,0:T(8,128)(2,1)} reduce(bf16[2048,1,64]{2,1,0:T(2,128)(2,1)S(1)} %bitcast.56, bf16[]{:T(256)} %broadcast.43), dimensions={1}, to_apply=%bitcast.32.reduce_sub_computation | reduce | bytes 524290
  15.9 2.1 reshape.66
  18.0 4.2 all-to-all-start
  22.2 7.5 %copy.51 = bf16[1,8192,128]{2,0,1:T(2,128)(2,1)} copy(bf16[1,8192,128]{2,1,0:T(8,128)(2,1)} %param.10) | data formatting | bytes 4194304 | tf_op args[4]
  29.7 0.0 copy-start.4
  29.7 0.0 copy-start.2
  29.7 46.5 %reduce = bf16[8192,128]{1,0:T(8,128)(2,1)} reduce(bf16[8192,1,128]{2,1,0:T(2,128)(2,1)} %bitcast.51, bf16[]{:T(256)} %broadcast.43), dimensions={1}, to_apply=%bitcast.45.reduce_sub_computation | reduce | bytes 4194306
  76.2 4.0 reshape.64
  80.2 0.0 all-to-all-done
  80.2 4.6 %all-to-all-start.1 = ((bf16[4,2,131072]{2,1,0:T(2,128)(2,1)}), bf16[4,2,131072]{2,1,0:T(2,128)(2,1)}, u32[]{:S(2)}, u32[]{:S(2)}) async-start(bf16[4,2,131072]{2,1,0:T(2,128)(2,1)} %reshape.64), calls=%async_computation.1 | async-start | bytes 4194304 | tf_op jit(solution)/shard_map/all_to_all | solution.py:17
  84.8 0.0 copy-done.4
  84.8 0.0 copy-done.2
  84.8 0.7 gather_fusion
  85.5 0.6 reshape.67
  86.2 0.9 copy.45
  87.0 1.2 copy.32
  88.3 0.6 gather_fusion.1
  88.9 0.0 copy-done
  88.9 0.8 convolution_bitcast_fusion.2
  89.7 1.1 pad_select_fusion
  90.8 19.7 %all-to-all-done.1 = bf16[4,2,131072]{2,1,0:T(2,128)(2,1)} async-done(((bf16[4,2,131072]{2,1,0:T(2,128)(2,1)}), bf16[4,2,131072]{2,1,0:T(2,128)(2,1)}, u32[]{:S(2)}, u32[]{:S(2)}) %all-to-all-start.1) | async-done | bytes 2097184 | tf_op jit(solution)/shard_map/all_to_all | solution.py:17
  110.6 4.9 %reshape.65 = bf16[8192,1,128]{2,1,0:T(2,128)(2,1)} reshape(bf16[4,2,131072]{2,1,0:T(2,128)(2,1)} %all-to-all-done.1) | data formatting | bytes 4194304
  115.5 3.8 copy.46
  119.3 6.3 %gather_fusion.2 = bf16[16,2048,128]{2,1,0:T(8,128)(2,1)} fusion(bf16[4,2048,128]{2,1,0:T(8,128)(2,1)} %bitcast.48, s32[1024]{0:T(1024)S(1)} %pad_clamp_fusion), kind=kCustom, calls=%fused_computation.2 | custom fusion | bytes 16777280 | tf_op jit(solution)/shard_map/gather | solution.py:22
  125.5 8.2 %convolution_bitcast_fusion.1 = f32[16,128,128]{1,2,0:T(8,128)S(1)} fusion(bf16[16,2048,128]{2,1,0:T(8,128)(2,1)} %gather_fusion.2, bf16[16,128,2048]{2,1,0:T(8,128)(2,1)} %bitcast.49), kind=kOutput, calls=%fused_computation.7 | convolution fusion | flops 1073741824 | bytes 17825792 | tf_op jit(solution)/shard_map/bnd,bdr->bnr/dot_general | solution.py:24
  133.8 41.2 %all-reduce.6 = (bf16[16,128,128]{1,2,0:T(8,128)(2,1)}, bf16[16,128,128]{1,2,0:T(8,128)(2,1)}) all-reduce(f32[16,128,128]{1,2,0:T(8,128)} %pad_select_fusion, f32[16,128,128]{1,2,0:T(8,128)S(1)} %convolution_bitcast_fusion.1), channel_id=1, replica_groups=mesh['groups'=2,'adapter'=4,'dp'=4] {'adapter'}, use_global_device_ids=true, to_apply=%region_0.1 | all-reduce | flops 524288 | bytes 3145728 | tf_op jit(solution)/shard_map/psum | solution.py:37
  175.0 0.0 copy-start.3
  175.0 1.5 fusion.2
  176.6 2.0 fusion
  178.5 1.0 copy.39
  179.5 3.7 all-to-all-start.3
  183.2 0.0 copy-done.3
  183.2 11.4 %convolution_bitcast_fusion = f32[16,2048,128]{1,2,0:T(8,128)} fusion(bf16[16,128,2048]{2,1,0:T(8,128)(2,1)} %bitcast.50, bf16[16,128,128]{1,2,0:T(8,128)(2,1)S(1)} %copy-done.3), kind=kOutput, calls=%fused_computation.3 | convolution fusion | flops 1073741824 | bytes 25690112 | tf_op jit(solution)/shard_map/bnd,bnr->bdr/dot_general | solution.py:44
  194.7 17.7 %copy.35 = f32[16,2048,128]{2,0,1:T(8,128)} copy(f32[16,2048,128]{1,2,0:T(8,128)} %convolution_bitcast_fusion) | data formatting | bytes 33554432 | tf_op jit(solution)/shard_map/bnd,bnr->bdr/dot_general | solution.py:44
  212.3 9.8 %fusion.9 = f32[4,2048,128]{2,0,1:T(4,128)S(1)} fusion(f32[16,2048,128]{2,0,1:T(8,128)} %copy.35, s32[16]{0:T(128)S(1)} %gather_fusion), kind=kOutput, calls=%fused_computation.22 | convolution fusion | flops 201326656 | bytes 20971584 | tf_op jit(solution)/shard_map/tb,bdr->tdr/dot_general | solution.py:54
  222.2 2.2 copy.36
  224.4 0.0 all-to-all-done.3
  224.4 4.8 %all-to-all-start.2 = ((f32[4,2048,128]{2,1,0:T(8,128)}), f32[4,2048,128]{2,1,0:T(8,128)}, u32[]{:S(2)}, u32[]{:S(2)}) async-start(f32[4,2048,128]{2,1,0:T(8,128)} %copy.36), calls=%async_computation.2 | async-start | bytes 8388608 | tf_op jit(solution)/shard_map/all_to_all | solution.py:56
  229.3 0.0 copy-start.1
  229.3 9.3 %convolution_convert_fusion = bf16[16,128,2048]{2,1,0:T(8,128)(2,1)} fusion(bf16[16,2048,128]{2,1,0:T(8,128)(2,1)} %gather_fusion.2, bf16[16,128,128]{1,2,0:T(8,128)(2,1)S(1)} %copy-done.3), kind=kOutput, calls=%fused_computation.4 | convolution fusion | flops 1077936128 | bytes 17301504 | tf_op jit(solution)/shard_map/bnr,bdr->bnd/dot_general | solution.py:40
  238.6 38.9 %all-to-all-done.2 = f32[4,2048,128]{2,1,0:T(8,128)} async-done(((f32[4,2048,128]{2,1,0:T(8,128)}), f32[4,2048,128]{2,1,0:T(8,128)}, u32[]{:S(2)}, u32[]{:S(2)}) %all-to-all-start.2) | async-done | bytes 4194336 | tf_op jit(solution)/shard_map/all_to_all | solution.py:56
  277.5 166.6 %all-reduce.7 = (bf16[1,8192,128]{2,1,0:T(8,128)(2,1)}, bf16[1,64,2048]{2,1,0:T(8,128)(2,1)}) all-reduce(f32[1,8192,128]{2,1,0:T(8,128)} %bitcast.11, f32[1,64,2048]{2,1,0:T(8,128)S(1)} %bitcast.57), channel_id=1, replica_groups=mesh['groups'=2,'adapter'=4,'dp'=4] {'dp'}, use_global_device_ids=true, to_apply=%region_1.2 | all-reduce | flops 1179648 | bytes 7077888 | tf_op jit(solution)/shard_map/psum | solution.py:58
  444.1 0.0 copy-done.1
  (5 shorter events, 0.1 us)
Async XLA Ops:
  0.6 88.3 %copy-start = (bf16[2048,512]{1,0:T(8,128)(2,1)S(1)}, bf16[2048,512]{1,0:T(8,128)(2,1)}, u32[]{:S(2)}) copy-start(bf16[2048,512]{1,0:T(8,128)(2,1)} %param.7) | copy-start | bytes 6291460
  18.0 62.2 %all-to-all-start = ((bf16[4,2,16384]{2,1,0:T(2,128)(2,1)}), bf16[4,2,16384]{2,1,0:T(2,128)(2,1)S(1)}, u32[]{:S(2)}, u32[]{:S(2)}) async-start(bf16[4,2,16384]{2,1,0:T(2,128)(2,1)} %reshape.66), calls=%async_computation | async-start | bytes 524288 | tf_op jit(solution)/shard_map/all_to_all | solution.py:18
  29.7 55.1 %copy-start.4 = (s32[16,1]{0,1:T(1,128)S(1)}, s32[16,1]{0,1:T(1,128)}, u32[]{:S(2)}) copy-start(s32[16,1]{0,1:T(1,128)} %param.8) | copy-start | bytes 196
  29.7 55.2 %copy-start.2 = (s32[4]{0:T(128)S(1)}, s32[4]{0:T(128)}, u32[]{:S(2)}) copy-start(s32[4]{0:T(128)} %param.9) | copy-start | bytes 52
  80.2 30.4 %all-to-all-start.1 = ((bf16[4,2,131072]{2,1,0:T(2,128)(2,1)}), bf16[4,2,131072]{2,1,0:T(2,128)(2,1)}, u32[]{:S(2)}, u32[]{:S(2)}) async-start(bf16[4,2,131072]{2,1,0:T(2,128)(2,1)} %reshape.64), calls=%async_computation.1 | async-start | bytes 4194304 | tf_op jit(solution)/shard_map/all_to_all | solution.py:17
  175.0 8.2 %copy-start.3 = (bf16[16,128,128]{1,2,0:T(8,128)(2,1)S(1)}, bf16[16,128,128]{1,2,0:T(8,128)(2,1)}, u32[]{:S(2)}) copy-start(bf16[16,128,128]{1,2,0:T(8,128)(2,1)} %get-tuple-element.5) | copy-start | bytes 1572868
  179.5 44.9 %all-to-all-start.3 = ((f32[4,64,512]{2,1,0:T(8,128)}), f32[4,64,512]{2,1,0:T(8,128)S(1)}, u32[]{:S(2)}, u32[]{:S(2)}) async-start(f32[4,64,512]{2,1,0:T(8,128)} %copy.39), calls=%async_computation.3 | async-start | bytes 1048576 | tf_op jit(solution)/shard_map/all_to_all | solution.py:57
  224.4 53.1 %all-to-all-start.2 = ((f32[4,2048,128]{2,1,0:T(8,128)}), f32[4,2048,128]{2,1,0:T(8,128)}, u32[]{:S(2)}, u32[]{:S(2)}) async-start(f32[4,2048,128]{2,1,0:T(8,128)} %copy.36), calls=%async_computation.2 | async-start | bytes 8388608 | tf_op jit(solution)/shard_map/all_to_all | solution.py:56
  229.3 214.8 %copy-start.1 = (bf16[2048,512]{1,0:T(8,128)(2,1)S(1)}, bf16[2048,512]{1,0:T(8,128)(2,1)}, u32[]{:S(2)}) copy-start(bf16[2048,512]{1,0:T(8,128)(2,1)} %param.7) | copy-start | bytes 6291460
where the time goes:
time: 445 us; the launch traced here: 444 us
  blocking collectives  208 us (47%)
  other arithmetic  59.9 us (13%)
  waiting for transfers between devices  58.6 us (13%)
  local copies, waits for them, and re-layouts  56.4 us (13%)
  matrix products  43.1 us (10%)
  starting transfers between devices  17.4 us (4%)
    psum x1, blocking collectives, local(): total_down, total_up = lax.psum((owned_down, owned_up), 'dp')  167 us
    unnamed x2, other arithmetic  58.8 us
    psum x1, blocking collectives, local(): shrunk_sum, d_sum = lax.psum((shrunk_part, d_part), 'adapter')  41.2 us
    all_to_all x1, waiting for transfers between devices, local(): lax.all_to_all(grad_down, 'adapter', split_axis=0, concat_axis=1, tiled=T...  38.9 us
    unnamed x19, local copies, waits for them, and re-layouts  26.7 us
    all_to_all x1, waiting for transfers between devices, local(): lax.all_to_all(down_pool, 'adapter', split_axis=1, concat_axis=0, tiled=T...  19.7 us
    dot_general x1, local copies, waits for them, and re-layouts, local(): jnp.einsum('bnd,bnr->bdr', acts_blocks, d_shrunk, preferred_element_type=...  17.7 us
    dot_general x1, matrix products, local(): jnp.einsum('bnd,bnr->bdr', acts_blocks, d_shrunk, preferred_element_type=...  11.4 us
  transfers between devices with their start and end apart: 4, of which 2 were waited for; matrix products, arithmetic and copies ran while one was open for 26% of the time, Pallas kernels for 0%

commit v1 on v0

--- a/solution.py
+++ b/solution.py
@@ -1,14 +1,312 @@
+import functools
+
 import jax
 import jax.numpy as jnp
 from jax import lax
+from jax.experimental import pallas as pl
+from jax.experimental.pallas import tpu as pltpu
 from jax.sharding import PartitionSpec as P
 
 DKV = 1024
 R = 64
 BLOCK = 128
+BF = jnp.bfloat16
+F32 = jnp.float32
+VMEM_BYTES = 40 * 1024 * 1024
+
+
+def params():
+    return pltpu.CompilerParams(vmem_limit_bytes=VMEM_BYTES)
+
+
+def cost(flops, moved):
+    return pl.CostEstimate(flops=flops, bytes_accessed=moved, transcendentals=0)
+
+
+def back_kernel(pool_count, rel_ref, up_ref, grad_ref, out_ref):
+    wide = lax.dot_general(
+        up_ref[...], grad_ref[...], (((1,), (1,)), ((), ())), preferred_element_type=F32
+    )
+    rel = rel_ref[...]
+    total = jnp.zeros(out_ref.shape, F32)
+    for m in range(pool_count):
+        total += jnp.where(rel == m, wide[m * R : (m + 1) * R], 0.0)
+    out_ref[...] = total
+
+
+def back_call(rel_rows, up_stack, out_grad, tile=512):
+    rows, cols = out_grad.shape
+    wide = up_stack.shape[0]
+    return pl.pallas_call(
+        functools.partial(back_kernel, wide // R),
+        grid=(rows // tile,),
+        out_shape=jax.ShapeDtypeStruct((R, rows), F32),
+        in_specs=[
+            pl.BlockSpec((1, tile), lambda i: (0, i)),
+            pl.BlockSpec((wide, cols), lambda i: (0, 0)),
+            pl.BlockSpec((tile, cols), lambda i: (i, 0)),
+        ],
+        out_specs=pl.BlockSpec((R, tile), lambda i: (0, i)),
+        compiler_params=params(),
+        cost_estimate=cost(2 * rows * cols * wide, rows * cols * 2),
+    )(rel_rows, up_stack, out_grad)
+
+
+def outer_kernel(pool_count, rel_ref, rank_ref, wide_ref, out_ref, lhs):
+    @pl.when(pl.program_id(0) == 0)
+    def _():
+        rel = rel_ref[...]
+        rank = rank_ref[...].astype(F32)
+        for m in range(pool_count):
+            lhs[m * R : (m + 1) * R, :] = jnp.where(rel == m, rank, 0.0).astype(BF)
+
+    out_ref[...] = jnp.dot(lhs[...], wide_ref[...], preferred_element_type=F32).astype(BF)
+
+
+def outer_call(rel_rows, rank_t, wide, pool_count, start, width, tile=256):
+    rows = wide.shape[0]
+    first = start // tile
+    return pl.pallas_call(
+        functools.partial(outer_kernel, pool_count),
+        grid=(width // tile,),
+        out_shape=jax.ShapeDtypeStruct((pool_count * R, width), BF),
+        in_specs=[
+            pl.BlockSpec((1, rows), lambda i: (0, 0)),
+            pl.BlockSpec((R, rows), lambda i: (0, 0)),
+            pl.BlockSpec((rows, tile), lambda i: (0, first + i)),
+        ],
+        out_specs=pl.BlockSpec((pool_count * R, tile), lambda i: (0, i)),
+        scratch_shapes=[pltpu.VMEM((pool_count * R, rows), BF)],
+        compiler_params=params(),
+        cost_estimate=cost(2 * rows * pool_count * R * width, rows * width * 2),
+    )(rel_rows, rank_t, wide)
+
+
+def load_pool(pools, held, sems):
+    copies = [pltpu.make_async_copy(p, held.at[m], sems.at[m]) for m, p in enumerate(pools)]
+    for c in copies:
+        c.start()
+    for c in copies:
+        c.wait()
+
+
+def shrink_kernel(pool_count, per, rel_ref, *refs):
+    pools = refs[:pool_count]
+    acts_ref, out_ref, held, sems = refs[pool_count:]
+    i = pl.program_id(0)
+
+    @pl.when(i == 0)
+    def _():
+        load_pool(pools, held, sems)
+
+    for b in range(per):
+        part = jnp.dot(
+            acts_ref[b * BLOCK : (b + 1) * BLOCK, :],
+            held[rel_ref[i * per + b]],
+            preferred_element_type=F32,
+        )
+        out_ref[:, b * BLOCK : (b + 1) * BLOCK] = part.T
+
+
+def shrink_call(rel, pools, acts, per=4):
+    rows, width = acts.shape
+    count = len(pools)
+    return pl.pallas_call(
+        functools.partial(shrink_kernel, count, per),
+        grid_spec=pltpu.PrefetchScalarGridSpec(
+            num_scalar_prefetch=1,
+            grid=(rows // (BLOCK * per),),
+            in_specs=[pl.BlockSpec(memory_space=pl.ANY)] * count
+            + [pl.BlockSpec((per * BLOCK, width), lambda i, rel: (i, 0))],
+            out_specs=pl.BlockSpec((2 * R, per * BLOCK), lambda i, rel: (0, i)),
+            scratch_shapes=[
+                pltpu.VMEM((count, width, 2 * R), BF),
+                pltpu.SemaphoreType.DMA((count,)),
+            ],
+        ),
+        out_shape=jax.ShapeDtypeStruct((2 * R, rows), F32),
+        compiler_params=params(),
+        cost_estimate=cost(4 * rows * width * 2 * R, rows * width * 2),
+    )(rel, *pools, acts)
+
+
+def expand_kernel(pool_count, per, rel_ref, *refs):
+    pools = refs[:pool_count]
+    rank_ref, out_ref, held, sems = refs[pool_count:]
+    i = pl.program_id(0)
+
+    @pl.when(i == 0)
+    def _():
+        load_pool(pools, held, sems)
+
+    for b in range(per):
+        rank = rank_ref[:, b * BLOCK : (b + 1) * BLOCK].astype(F32).T.astype(BF)
+        out_ref[b * BLOCK : (b + 1) * BLOCK, :] = lax.dot_general(
+            rank, held[rel_ref[i * per + b]], (((1,), (1,)), ((), ())), preferred_element_type=F32
+        ).astype(BF)
+
+
+def expand_call(rel, pools, rank_t, width, per=4):
+    rows = rank_t.shape[1]
+    count = len(pools)
+    return pl.pallas_call(
+        functools.partial(expand_kernel, count, per),
+        grid_spec=pltpu.PrefetchScalarGridSpec(
+            num_scalar_prefetch=1,
+            grid=(rows // (BLOCK * per),),
+            in_specs=[pl.BlockSpec(memory_space=pl.ANY)] * count
+            + [pl.BlockSpec((2 * R, per * BLOCK), lambda i, rel: (0, i))],
+            out_specs=pl.BlockSpec((per * BLOCK, width), lambda i, rel: (i, 0)),
+            scratch_shapes=[
+                pltpu.VMEM((count, width, 2 * R), BF),
+                pltpu.SemaphoreType.DMA((count,)),
+            ],
+        ),
+        out_shape=jax.ShapeDtypeStruct((rows, width), BF),
+        compiler_params=params(),
+        cost_estimate=cost(4 * rows * width * 2 * R, rows * width * 2),
+    )(rel, *pools, rank_t)
+
+
+def place_kernel(count, start, has_input, pos_ref, *refs):
+    first, second = refs[:count], refs[count : 2 * count]
+    rest = refs[2 * count + (1 if has_input else 0) :]
+    out_ref, turned, sems = rest
+    width = first[0].shape[1]
+    copies = []
+    for m in range(count):
+        sender = pos_ref[0] ^ m
+        swap = sender >= count // 2
+        a, b = first[m][...].astype(F32), second[m][...].astype(F32)
+        turned[m, :, :] = jnp.concatenate(
+            [jnp.where(swap, b, a), jnp.where(swap, a, b)], axis=0
+        ).T.astype(BF)
+        row = pl.multiple_of(sender * (out_ref.shape[0] // count) + start, 128)
+        copy = pltpu.make_async_copy(turned.at[m], out_ref.at[pl.ds(row, width), :], sems.at[m])
+        copy.start()
+        copies.append(copy)
+    for copy in copies:
+        copy.wait()
+
+
+def place_call(position, first, second, start, total_rows, held):
+    count = len(first)
+    width = first[0].shape[1]
+    whole = pl.BlockSpec(memory_space=pltpu.VMEM)
+    extra = [] if held is None else [held]
+    return pl.pallas_call(
+        functools.partial(place_kernel, count, start, held is not None),
+        out_shape=jax.ShapeDtypeStruct((total_rows, 2 * R), BF),
+        in_specs=[pl.BlockSpec(memory_space=pltpu.SMEM)]
+        + [whole] * (2 * count)
+        + [pl.BlockSpec(memory_space=pl.ANY)] * len(extra),
+        out_specs=pl.BlockSpec(memory_space=pl.ANY),
+        scratch_shapes=[
+            pltpu.VMEM((count, width, 2 * R), BF),
+            pltpu.SemaphoreType.DMA((count,)),
+        ],
+        input_output_aliases={} if held is None else {1 + 2 * count: 0},
+        compiler_params=params(),
+        cost_estimate=cost(0, 4 * count * width * 2 * R * 2),
+    )(position.reshape(1), *first, *second, *extra)
 
 
 def local(acts, out_grad, tenant_ids, slot_map, down_pool, up_pool):
+    count = lax.axis_size("adapter")
+    j = lax.axis_index("adapter")
+    z = lax.axis_index("dp")
+    rows, width = acts.shape
+    cols = out_grad.shape[1]
+    total_rows = down_pool.shape[1]
+    upper = j >= count // 2
+
+    def swap(x, m):
+        return lax.ppermute(x, "adapter", [(i, i ^ m) for i in range(count)])
+
+    rel = jnp.bitwise_xor(slot_map[tenant_ids[:, 0]], j).astype(jnp.int32)
+    rel_rows = jnp.repeat(rel, BLOCK)[None, :]
+
+    def up_piece(m):
+        return lax.dynamic_slice(up_pool[0], (0, (j ^ m) * cols), (R, cols))
+
+    def down_piece(m):
+        return lax.dynamic_slice(down_pool[0], ((j ^ m) * width, 0), (width, 2 * R))
+
+    ups = [up_piece(0)] + [swap(up_piece(m), m) for m in range(1, count)]
+    pools = [down_piece(0)] + [swap(down_piece(m), m) for m in range(1, count)]
+    up_stack = jnp.concatenate(ups, axis=0)
+
+    back_part = back_call(rel_rows, up_stack, out_grad)
+    d_own = (back_part + swap(back_part, 1)).astype(BF)
+    d_other = swap(d_own, 2)
+
+    chunk = 512
+    pieces = width // chunk
+    own = [outer_call(rel_rows, d_own, acts, count, c * chunk, chunk) for c in range(pieces)]
+    other = [outer_call(rel_rows, d_other, acts, count, c * chunk, chunk) for c in range(pieces)]
+
+    shrunk_part = shrink_call(rel, pools, acts)
+    shrunk_sum = shrunk_part + swap(shrunk_part, 1)
+    key, value = shrunk_sum[:R], shrunk_sum[R:]
+    came = swap(jnp.where(upper, key, value).astype(BF), 2)
+    shrunk_own = (jnp.where(upper, value, key) + came.astype(F32)).astype(BF)
+    up_part = outer_call(rel_rows, shrunk_own, out_grad, count, 0, cols)
+
+    d_full = jnp.where(
+        upper,
+        jnp.concatenate([d_other, d_own], axis=0),
+        jnp.concatenate([d_own, d_other], axis=0),
+    )
+    acts_grad = expand_call(rel, pools, d_full, width)
+
+    names = [("own", c) for c in range(pieces)] + [("other", c) for c in range(pieces - 1)]
+    names += [("up", 0), ("other", pieces - 1)]
+    stream = {("own", c): own[c] for c in range(pieces)}
+    stream.update({("other", c): other[c] for c in range(pieces)})
+    stream[("up", 0)] = up_part
+    parts = [stream[n] for n in names]
+    n_parts = len(parts)
+    edge = (z == 0) | (z == 3)
+    lag = 4
+    inner, total, final = {}, {}, {}
+    for t in range(n_parts + lag):
+        back = t - lag
+        if back >= 0:
+            came = lax.ppermute(inner[back], "dp", [(1, 2), (2, 1)])
+            total[back] = (inner[back].astype(F32) + came.astype(F32)).astype(BF)
+        if t < n_parts and back >= 0:
+            payload = jnp.where(edge, parts[t], total[back])
+        elif t < n_parts:
+            payload = parts[t]
+        else:
+            payload = total[back]
+        got = lax.ppermute(payload, "dp", [(0, 1), (1, 0), (2, 3), (3, 2)])
+        if t < n_parts:
+            inner[t] = (parts[t].astype(F32) + got.astype(F32)).astype(BF)
+        if back >= 0:
+            final[names[back]] = jnp.where(edge, got, total[back])
+
+    def to_owner(x):
+        return [x[:R]] + [swap(x[m * R : (m + 1) * R], m) for m in range(1, count)]
+
+    down_grad = None
+    own_pairs = [
+        to_owner(jnp.concatenate([final[("own", c)], final[("own", c + 1)]], axis=1))
+        for c in range(0, pieces, 2)
+    ]
+    for c in range(pieces):
+        first = [p[:, (c % 2) * chunk : (c % 2 + 1) * chunk] for p in own_pairs[c // 2]]
+        second = to_owner(final[("other", c)])
+        down_grad = place_call(j, first, second, c * chunk, total_rows, down_grad)
+
+    up_pieces = to_owner(final[("up", 0)])
+    up_grad = jnp.zeros((R, cols * count), BF)
+    for m in range(count):
+        up_grad = lax.dynamic_update_slice(up_grad, up_pieces[m], (0, (j ^ m) * cols))
+    return acts_grad, down_grad[None], up_grad[None]
+
+
+def local_any(acts, out_grad, tenant_ids, slot_map, down_pool, up_pool):
     position = lax.axis_index("adapter")
     row_count, local_width = acts.shape
     col_count = out_grad.shape[1]
@@ -62,8 +360,9 @@
 
 
 def solution(mesh):
+    small = mesh.shape["adapter"] == 4 and mesh.shape["dp"] == 4
     return jax.shard_map(
-        local,
+        local if small else local_any,
         mesh=mesh,
         in_specs=(
             P(("groups", "dp"), "adapter"),

time: 445 us -> 185 us (0.42)
  blocking collectives: 208 us -> 0 us
  other arithmetic: 59.9 us -> 3.2 us
  matrix products: 43.1 us -> 0 us
  local copies, waits for them, and re-layouts: 56.4 us -> 13.7 us
  starting transfers between devices: 17.4 us -> 56.5 us
  Pallas kernels: 0 us -> 27.3 us
  waiting for transfers between devices: 58.6 us -> 82.1 us
    psum x2 -> x0, blocking collectives: 208 us -> none  [the longest x1 167 us: local(): total_down, total_up = lax.psum((owned_down, owned_up), 'dp')]
    ppermute x0 -> x53, waiting for transfers between devices: none -> 82.1 us  [the longest x31 44.4 us: swap(): return lax.ppermute(x, 'adapter', [(i, i ^ m) for i in range(count)])]
    unnamed x2 -> x1, other arithmetic: 58.8 us -> 0.01 us
    all_to_all x4 -> x0, waiting for transfers between devices: 58.6 us -> none  [the longest x1 38.9 us: local(): lax.all_to_all(grad_down, 'adapter', split_axis=0, concat_axis=1, tiled=T...]
    ppermute x0 -> x53, starting transfers between devices: none -> 56.5 us  [the longest x13 29.7 us: local(): got = lax.ppermute(payload, 'dp', [(0, 1), (1, 0), (2, 3), (3, 2)])]
    dot_general x7 -> x0, matrix products: 43.1 us -> none  [the longest x1 11.4 us: local(): jnp.einsum('bnd,bnr->bdr', acts_blocks, d_shrunk, preferred_element_type=...]
    pallas_call x0 -> x16, Pallas kernels: none -> 27.3 us  [the longest x9 12.5 us: outer_call(): pl.pallas_call(functools.partial(outer_kernel, pool_count), grid=(width /...]
    dot_general x3 -> x0, local copies, waits for them, and re-layouts: 20.9 us -> none  [the longest x1 17.7 us: local(): jnp.einsum('bnd,bnr->bdr', acts_blocks, d_shrunk, preferred_element_type=...]
  transfers between devices with their start and end apart: 4 -> 53, of which waited for: 2 -> 21; matrix products, arithmetic and copies ran while one was open for 26% -> 4% of each run, Pallas kernels for 0% -> 14%
where the time goes in v1:
time: 185 us; the launch traced here: 184 us
  waiting for transfers between devices  82.1 us (44%)
  starting transfers between devices  56.5 us (31%)
  Pallas kernels  27.3 us (15%)
  local copies, waits for them, and re-layouts  13.7 us (7%)
  other arithmetic  3.2 us (2%)
    ppermute x31, waiting for transfers between devices, swap(): return lax.ppermute(x, 'adapter', [(i, i ^ m) for i in range(count)])  44.4 us
    ppermute x13, waiting for transfers between devices, local(): got = lax.ppermute(payload, 'dp', [(0, 1), (1, 0), (2, 3), (3, 2)])  37.7 us
    ppermute x13, starting transfers between devices, local(): got = lax.ppermute(payload, 'dp', [(0, 1), (1, 0), (2, 3), (3, 2)])  29.7 us
    ppermute x31, starting transfers between devices, swap(): return lax.ppermute(x, 'adapter', [(i, i ^ m) for i in range(count)])  20.6 us
    pallas_call x9, Pallas kernels, outer_call(): pl.pallas_call(functools.partial(outer_kernel, pool_count), grid=(width /...  12.5 us
    unnamed x16, local copies, waits for them, and re-layouts  9.07 us
    ppermute x9, starting transfers between devices, local(): came = lax.ppermute(inner[back], 'dp', [(1, 2), (2, 1)])  6.22 us
    pallas_call x1, Pallas kernels, expand_call(): pl.pallas_call(functools.partial(expand_kernel, count, per), grid_spec=pl...  5.71 us
  transfers between devices with their start and end apart: 53, of which 21 were waited for; matrix products, arithmetic and copies ran while one was open for 4% of the time, Pallas kernels for 14%

profile of v1, /device:TPU:0, one launch (start us, length us, event | category | flops | bytes accessed | tf_op | source)
XLA Modules:
  0.0 184.3 jit_solution(17168120938794708665)
XLA Ops:
  2.2 2.6 %collective-permute-start.5 = (bf16[64,512]{1,0:T(8,128)(2,1)S(1)}, bf16[64,512]{1,0:T(8,128)(2,1)S(1)}, u32[]{:S(2)}, u32[]{:S(2)}) collective-permute-start(bf16[64,512]{1,0:T(8,128)(2,1)S(1)} %get-tuple-element.34), channel_id=1, source_target_pairs={{0,12},{4,8},{8,4},{12,0},{1,13},{5,9},{9,5},{13,1},{2,14},{6,10},... | collective-permute-start | bytes 196616 | tf_op jit(solution)/shard_map/ppermute | solution.py:224
  7.2 1.8 collective-permute-done.4
  9.2 1.6 copy-done.3
  10.8 1.4 shard_map.85
  12.3 2.7 %dynamic-slice_bitcast_fusion = (bf16[2048,128]{1,0:T(8,128)(2,1)}, bf16[2048,128]{1,0:T(8,128)(2,1)}, bf16[2048,128]{1,0:T(8,128)(2,1)S(1)}, bf16[2048,128]{1,0:T(8,128)(2,1)}) fusion(bf16[1,8192,128]{2,1,0:T(8,128)(2,1)} %param.10, s32[]{:T(128)S(6)} %select_n.116, s32[]{:T(128)S(6)} %select_n.114, s32[]{:T(128)S(6)} %select_n.113, s32[]{:T(128)S(6)} %select_n.115), kind=kLoop, calls=%fused_computation.23 | loop fusion | bytes 4194320 | tf_op jit(solution)/shard_map/dynamic_slice | solution.py:233
  15.0 1.6 collective-permute-start.2
  17.2 3.4 %copy-done.1 = bf16[2048,2048]{1,0:T(8,128)(2,1)S(1)} copy-done((bf16[2048,2048]{1,0:T(8,128)(2,1)S(1)}, bf16[2048,2048]{1,0:T(8,128)(2,1)}, u32[]{:S(2)}) %copy-start.1) | copy-done | bytes 8388632
  20.6 1.4 shard_map.96
  22.0 1.6 collective-permute-start.34
  23.7 5.5 %collective-permute-done.2.refs_3_ = bf16[2048,128]{1,0:T(8,128)(2,1)S(1)} collective-permute-done((bf16[2048,128]{1,0:T(8,128)(2,1)}, bf16[2048,128]{1,0:T(8,128)(2,1)S(1)}, u32[]{:S(2)}, u32[]{:S(2)}) %collective-permute-start.2) | collective-permute-done | bytes 524320 | tf_op jit(solution)/shard_map/ppermute | solution.py:224
  29.2 11.5 %collective-permute-done.1.refs_2_ = bf16[2048,128]{1,0:T(8,128)(2,1)S(1)} collective-permute-done((bf16[2048,128]{1,0:T(8,128)(2,1)}, bf16[2048,128]{1,0:T(8,128)(2,1)S(1)}, u32[]{:S(2)}, u32[]{:S(2)}) %collective-permute-start.1) | collective-permute-done | bytes 524320 | tf_op jit(solution)/shard_map/ppermute | solution.py:224
  40.7 3.4 %copy-done.2 = bf16[2048,2048]{1,0:T(8,128)(2,1)S(1)} copy-done((bf16[2048,2048]{1,0:T(8,128)(2,1)S(1)}, bf16[2048,2048]{1,0:T(8,128)(2,1)}, u32[]{:S(2)}) %copy-start.2) | copy-done | bytes 8388632
  44.1 3.9 %shard_map.87 = f32[128,2048]{1,0:T(8,128)S(1)} custom-call(s32[16]{0:T(128)S(1)} %broadcast_xor_fusion.rel_ref, bf16[2048,128]{1,0:T(8,128)(2,1)S(1)} %get-tuple-element.5.refs_0_, bf16[2048,128]{1,0:T(8,128)(2,1)S(1)} %collective-permute-done.refs_1_, bf16[2048,128]{1,0:T(8,128)(2,1)S(1)} %collective-permute-done.1.refs_2_, ...), custom_call_target="tpu_custom_call" | custom-call | flops 2147483648 | bytes 8388608 | tf_op jit(solution)/shard_map/pallas_call | solution.py:114
  48.1 1.4 shard_map.89
  49.5 1.6 collective-permute-start.10
  51.2 1.4 shard_map.94
  52.6 1.4 shard_map.91
  54.0 1.6 collective-permute-start.7
  56.0 1.6 collective-permute-start.19
  59.2 5.5 %collective-permute-done.13 = bf16[256,512]{1,0:T(8,128)(2,1)S(1)} collective-permute-done((bf16[256,512]{1,0:T(8,128)(2,1)S(1)}, bf16[256,512]{1,0:T(8,128)(2,1)S(1)}, u32[]{:S(2)}, u32[]{:S(2)}) %collective-permute-start.13) | collective-permute-done | bytes 262176 | tf_op jit(solution)/shard_map/ppermute | solution.py:283
  65.5 4.0 %collective-permute-done.19 = bf16[256,512]{1,0:T(8,128)(2,1)S(1)} collective-permute-done((bf16[256,512]{1,0:T(8,128)(2,1)S(1)}, bf16[256,512]{1,0:T(8,128)(2,1)S(1)}, u32[]{:S(2)}, u32[]{:S(2)}) %collective-permute-start.19) | collective-permute-done | bytes 262176 | tf_op jit(solution)/shard_map/ppermute | solution.py:283
  70.9 1.4 shard_map.93
  72.3 1.4 shard_map.92
  73.9 1.4 shard_map.90
  75.3 5.7 %shard_map.86 = bf16[2048,2048]{1,0:T(8,128)(2,1)} custom-call(s32[16]{0:T(128)S(1)} %broadcast_xor_fusion.rel_ref, bf16[2048,128]{1,0:T(8,128)(2,1)S(1)} %get-tuple-element.5.refs_0_, bf16[2048,128]{1,0:T(8,128)(2,1)S(1)} %collective-permute-done.refs_1_, bf16[2048,128]{1,0:T(8,128)(2,1)S(1)} %collective-permute-done.1.refs_2_, ...), custom_call_target="tpu_custom_call" | custom-call | flops 2147483648 | bytes 8388608 | tf_op jit(solution)/shard_map/pallas_call | solution.py:152
  81.0 1.4 shard_map.95
  82.5 6.1 %collective-permute-start.21 = (bf16[256,512]{1,0:T(8,128)(2,1)S(1)}, bf16[256,512]{1,0:T(8,128)(2,1)S(1)}, u32[]{:S(2)}, u32[]{:S(2)}) collective-permute-start(bf16[256,512]{1,0:T(8,128)(2,1)S(1)} %broadcast_select_fusion.9), channel_id=1, source_target_pairs={{0,1},{1,0},{2,3},{3,2},{4,5},{5,4},{6,7},{7,6},{8,9},{9,8},{10,11... | collective-permute-start | bytes 786440 | tf_op jit(solution)/shard_map/ppermute | solution.py:283
  89.0 2.1 %collective-permute-start.36 = (bf16[256,512]{1,0:T(8,128)(2,1)S(1)}, bf16[256,512]{1,0:T(8,128)(2,1)S(1)}, u32[]{:S(2)}, u32[]{:S(2)}) collective-permute-start(bf16[256,512]{1,0:T(8,128)(2,1)S(1)} %broadcast_select_fusion.5), channel_id=1, source_target_pairs={{0,1},{1,0},{2,3},{3,2},{4,5},{5,4},{6,7},{7,6},{8,9},{9,8},{10,11... | collective-permute-start | bytes 786440 | tf_op jit(solution)/shard_map/ppermute | solution.py:283
  91.0 4.9 %collective-permute-done.21 = bf16[256,512]{1,0:T(8,128)(2,1)S(1)} collective-permute-done((bf16[256,512]{1,0:T(8,128)(2,1)S(1)}, bf16[256,512]{1,0:T(8,128)(2,1)S(1)}, u32[]{:S(2)}, u32[]{:S(2)}) %collective-permute-start.21) | collective-permute-done | bytes 262176 | tf_op jit(solution)/shard_map/ppermute | solution.py:283
  96.8 4.7 %collective-permute-done.15 = bf16[256,512]{1,0:T(8,128)(2,1)S(1)} collective-permute-done((bf16[256,512]{1,0:T(8,128)(2,1)S(1)}, bf16[256,512]{1,0:T(8,128)(2,1)S(1)}, u32[]{:S(2)}, u32[]{:S(2)}) %collective-permute-start.15) | collective-permute-done | bytes 262176 | tf_op jit(solution)/shard_map/ppermute | solution.py:283
  102.4 3.1 %collective-permute-done.36 = bf16[256,512]{1,0:T(8,128)(2,1)S(1)} collective-permute-done((bf16[256,512]{1,0:T(8,128)(2,1)S(1)}, bf16[256,512]{1,0:T(8,128)(2,1)S(1)}, u32[]{:S(2)}, u32[]{:S(2)}) %collective-permute-start.36) | collective-permute-done | bytes 262176 | tf_op jit(solution)/shard_map/ppermute | solution.py:283
  105.8 5.7 %collective-permute-done.39 = bf16[64,1024]{1,0:T(8,128)(2,1)S(1)} collective-permute-done((bf16[64,1024]{1,0:T(8,128)(2,1)S(1)}, bf16[64,1024]{1,0:T(8,128)(2,1)S(1)}, u32[]{:S(2)}, u32[]{:S(2)}) %collective-permute-start.39) | collective-permute-done | bytes 131104 | tf_op jit(solution)/shard_map/ppermute | solution.py:224
  112.1 4.9 %collective-permute-done.38 = bf16[64,1024]{1,0:T(8,128)(2,1)S(1)} collective-permute-done((bf16[64,1024]{1,0:T(8,128)(2,1)S(1)}, bf16[64,1024]{1,0:T(8,128)(2,1)S(1)}, u32[]{:S(2)}, u32[]{:S(2)}) %collective-permute-start.38) | collective-permute-done | bytes 131104 | tf_op jit(solution)/shard_map/ppermute | solution.py:224
  117.0 1.3 collective-permute-done.37
  119.9 4.0 %collective-permute-start.23 = (bf16[256,512]{1,0:T(8,128)(2,1)S(1)}, bf16[256,512]{1,0:T(8,128)(2,1)S(1)}, u32[]{:S(2)}, u32[]{:S(2)}) collective-permute-start(bf16[256,512]{1,0:T(8,128)(2,1)S(1)} %broadcast_select_fusion.8), channel_id=1, source_target_pairs={{0,1},{1,0},{2,3},{3,2},{4,5},{5,4},{6,7},{7,6},{8,9},{9,8},{10,11... | collective-permute-start | bytes 786440 | tf_op jit(solution)/shard_map/ppermute | solution.py:283
  124.1 6.3 %collective-permute-start.41 = (bf16[256,512]{1,0:T(8,128)(2,1)S(1)}, bf16[256,512]{1,0:T(8,128)(2,1)S(1)}, u32[]{:S(2)}, u32[]{:S(2)}) collective-permute-start(bf16[256,512]{1,0:T(8,128)(2,1)S(1)} %add_convert_fusion.2), channel_id=1, source_target_pairs={{0,1},{1,0},{2,3},{3,2},{4,5},{5,4},{6,7},{7,6},{8,9},{9,8},{10,11... | collective-permute-start | bytes 786440 | tf_op jit(solution)/shard_map/ppermute | solution.py:283
  133.6 8.7 %collective-permute-done.41 = bf16[256,512]{1,0:T(8,128)(2,1)S(1)} collective-permute-done((bf16[256,512]{1,0:T(8,128)(2,1)S(1)}, bf16[256,512]{1,0:T(8,128)(2,1)S(1)}, u32[]{:S(2)}, u32[]{:S(2)}) %collective-permute-start.41) | collective-permute-done | bytes 262176 | tf_op jit(solution)/shard_map/ppermute | solution.py:283
  142.5 1.9 %collective-permute-start.44 = (bf16[64,512]{1,0:T(8,128)(2,1)S(1)}, bf16[64,512]{1,0:T(8,128)(2,1)S(1)}, u32[]{:S(2)}, u32[]{:S(2)}) collective-permute-start(bf16[64,512]{1,0:T(8,128)(2,1)S(1)} %get-tuple-element.20), channel_id=1, source_target_pairs={{0,12},{4,8},{8,4},{12,0},{1,13},{5,9},{9,5},{13,1},{2,14},{6,10},... | collective-permute-start | bytes 196616 | tf_op jit(solution)/shard_map/ppermute | solution.py:224
  146.8 1.9 %collective-permute-start.33 = (bf16[64,512]{1,0:T(8,128)(2,1)S(1)}, bf16[64,512]{1,0:T(8,128)(2,1)S(1)}, u32[]{:S(2)}, u32[]{:S(2)}) collective-permute-start(bf16[64,512]{1,0:T(8,128)(2,1)S(1)} %get-tuple-element.24), channel_id=1, source_target_pairs={{0,12},{4,8},{8,4},{12,0},{1,13},{5,9},{9,5},{13,1},{2,14},{6,10},... | collective-permute-start | bytes 196616 | tf_op jit(solution)/shard_map/ppermute | solution.py:224
  152.1 1.4 collective-permute-start.17
  153.6 2.8 %collective-permute-done.18 = bf16[64,1024]{1,0:T(8,128)(2,1)S(1)} collective-permute-done((bf16[64,1024]{1,0:T(8,128)(2,1)S(1)}, bf16[64,1024]{1,0:T(8,128)(2,1)S(1)}, u32[]{:S(2)}, u32[]{:S(2)}) %collective-permute-start.18) | collective-permute-done | bytes 131104 | tf_op jit(solution)/shard_map/ppermute | solution.py:224
  157.1 2.8 %collective-permute-done.17 = bf16[64,1024]{1,0:T(8,128)(2,1)S(1)} collective-permute-done((bf16[64,1024]{1,0:T(8,128)(2,1)S(1)}, bf16[64,1024]{1,0:T(8,128)(2,1)S(1)}, u32[]{:S(2)}, u32[]{:S(2)}) %collective-permute-start.17) | collective-permute-done | bytes 131104 | tf_op jit(solution)/shard_map/ppermute | solution.py:224
  159.8 2.8 %collective-permute-start.25 = (bf16[256,512]{1,0:T(8,128)(2,1)S(1)}, bf16[256,512]{1,0:T(8,128)(2,1)S(1)}, u32[]{:S(2)}, u32[]{:S(2)}) collective-permute-start(bf16[256,512]{1,0:T(8,128)(2,1)S(1)} %add_convert_fusion.8), channel_id=1, source_target_pairs={{0,1},{1,0},{2,3},{3,2},{4,5},{5,4},{6,7},{7,6},{8,9},{9,8},{10,11... | collective-permute-start | bytes 786440 | tf_op jit(solution)/shard_map/ppermute | solution.py:283
  162.8 6.0 %collective-permute-done.25 = bf16[256,512]{1,0:T(8,128)(2,1)S(1)} collective-permute-done((bf16[256,512]{1,0:T(8,128)(2,1)S(1)}, bf16[256,512]{1,0:T(8,128)(2,1)S(1)}, u32[]{:S(2)}, u32[]{:S(2)}) %collective-permute-start.25) | collective-permute-done | bytes 262176 | tf_op jit(solution)/shard_map/ppermute | solution.py:283
  168.8 1.7 collective-permute-start.49
  173.5 1.3 collective-permute-done.28.refs_7_
  174.9 1.6 collective-permute-done.27.refs_6_
  179.8 3.7 %collective-permute-done.51 = bf16[64,512]{1,0:T(8,128)(2,1)S(1)} collective-permute-done((bf16[64,512]{1,0:T(8,128)(2,1)S(1)}, bf16[64,512]{1,0:T(8,128)(2,1)S(1)}, u32[]{:S(2)}, u32[]{:S(2)}) %collective-permute-start.51) | collective-permute-done | bytes 65568 | tf_op jit(solution)/shard_map/ppermute | solution.py:224
  (153 shorter events, 30.8 us)
Async XLA Ops:
  1.6 4.5 %collective-permute-start.3 = (bf16[64,512]{1,0:T(8,128)(2,1)S(1)}, bf16[64,512]{1,0:T(8,128)(2,1)S(1)}, u32[]{:S(2)}, u32[]{:S(2)}) collective-permute-start(bf16[64,512]{1,0:T(8,128)(2,1)S(1)} %get-tuple-element.33), channel_id=1, source_target_pairs={{0,4},{4,0},{8,12},{12,8},{1,5},{5,1},{9,13},{13,9},{2,6},{6,2},{1... | collective-permute-start | bytes 196616 | tf_op jit(solution)/shard_map/ppermute | solution.py:224
  2.2 5.1 %collective-permute-start.5 = (bf16[64,512]{1,0:T(8,128)(2,1)S(1)}, bf16[64,512]{1,0:T(8,128)(2,1)S(1)}, u32[]{:S(2)}, u32[]{:S(2)}) collective-permute-start(bf16[64,512]{1,0:T(8,128)(2,1)S(1)} %get-tuple-element.34), channel_id=1, source_target_pairs={{0,12},{4,8},{8,4},{12,0},{1,13},{5,9},{9,5},{13,1},{2,14},{6,10},... | collective-permute-start | bytes 196616 | tf_op jit(solution)/shard_map/ppermute | solution.py:224
  12.2 5.0 %collective-permute-start.6 = (f32[64,2048]{1,0:T(8,128)S(1)}, f32[64,2048]{1,0:T(8,128)S(1)}, u32[]{:S(2)}, u32[]{:S(2)}) collective-permute-start(f32[64,2048]{1,0:T(8,128)S(1)} %shard_map.85), channel_id=1, source_target_pairs={{0,4},{4,0},{8,12},{12,8},{1,5},{5,1},{9,13},{13,9},{2,6},{6,2},{1... | collective-permute-start | bytes 1572872 | tf_op jit(solution)/shard_map/ppermute | solution.py:224
  15.0 14.1 %collective-permute-start.2 = (bf16[2048,128]{1,0:T(8,128)(2,1)}, bf16[2048,128]{1,0:T(8,128)(2,1)S(1)}, u32[]{:S(2)}, u32[]{:S(2)}) collective-permute-start(bf16[2048,128]{1,0:T(8,128)(2,1)} %get-tuple-element.3), channel_id=1, source_target_pairs={{0,12},{4,8},{8,4},{12,0},{1,13},{5,9},{9,5},{13,1},{2,14},{6,10},... | collective-permute-start | bytes 1572872 | tf_op jit(solution)/shard_map/ppermute | solution.py:224
  16.6 12.6 %collective-permute-start = (bf16[2048,128]{1,0:T(8,128)(2,1)}, bf16[2048,128]{1,0:T(8,128)(2,1)S(1)}, u32[]{:S(2)}, u32[]{:S(2)}) collective-permute-start(bf16[2048,128]{1,0:T(8,128)(2,1)} %get-tuple-element.4), channel_id=1, source_target_pairs={{0,4},{4,0},{8,12},{12,8},{1,5},{5,1},{9,13},{13,9},{2,6},{6,2},{1... | collective-permute-start | bytes 1572872 | tf_op jit(solution)/shard_map/ppermute | solution.py:224
  16.6 24.1 %collective-permute-start.1 = (bf16[2048,128]{1,0:T(8,128)(2,1)}, bf16[2048,128]{1,0:T(8,128)(2,1)S(1)}, u32[]{:S(2)}, u32[]{:S(2)}) collective-permute-start(bf16[2048,128]{1,0:T(8,128)(2,1)} %get-tuple-element.6), channel_id=1, source_target_pairs={{0,8},{4,12},{8,0},{12,4},{1,9},{5,13},{9,1},{13,5},{2,10},{6,14},... | collective-permute-start | bytes 1572872 | tf_op jit(solution)/shard_map/ppermute | solution.py:224
  22.0 34.0 %collective-permute-start.34 = (bf16[256,512]{1,0:T(8,128)(2,1)S(1)}, bf16[256,512]{1,0:T(8,128)(2,1)S(1)}, u32[]{:S(2)}, u32[]{:S(2)}) collective-permute-start(bf16[256,512]{1,0:T(8,128)(2,1)S(1)} %shard_map.96), channel_id=1, source_target_pairs={{0,1},{1,0},{2,3},{3,2},{4,5},{5,4},{6,7},{7,6},{8,9},{9,8},{10,11... | collective-permute-start | bytes 786440 | tf_op jit(solution)/shard_map/ppermute | solution.py:283
  48.0 71.2 %collective-permute-start.8 = (f32[128,2048]{1,0:T(8,128)S(1)}, f32[128,2048]{1,0:T(8,128)S(1)}, u32[]{:S(2)}, u32[]{:S(2)}) collective-permute-start(f32[128,2048]{1,0:T(8,128)S(1)} %shard_map.87), channel_id=1, source_target_pairs={{0,4},{4,0},{8,12},{12,8},{1,5},{5,1},{9,13},{13,9},{2,6},{6,2},{1... | collective-permute-start | bytes 3145736 | tf_op jit(solution)/shard_map/ppermute | solution.py:224
  49.5 8.9 %collective-permute-start.10 = (bf16[256,512]{1,0:T(8,128)(2,1)S(1)}, bf16[256,512]{1,0:T(8,128)(2,1)S(1)}, u32[]{:S(2)}, u32[]{:S(2)}) collective-permute-start(bf16[256,512]{1,0:T(8,128)(2,1)S(1)} %shard_map.89), channel_id=1, source_target_pairs={{0,1},{1,0},{2,3},{3,2},{4,5},{5,4},{6,7},{7,6},{8,9},{9,8},{10,11... | collective-permute-start | bytes 786440 | tf_op jit(solution)/shard_map/ppermute | solution.py:283
  54.0 16.3 %collective-permute-start.7 = (bf16[64,2048]{1,0:T(8,128)(2,1)S(1)}, bf16[64,2048]{1,0:T(8,128)(2,1)S(1)}, u32[]{:S(2)}, u32[]{:S(2)}) collective-permute-start(bf16[64,2048]{1,0:T(8,128)(2,1)S(1)} %add_convert_fusion.19.rank_ref), channel_id=1, source_target_pairs={{0,8},{4,12},{8,0},{12,4},{1,9},{5,13},{9,1},{13,5},{2,10},{6,14},... | collective-permute-start | bytes 786440 | tf_op jit(solution)/shard_map/ppermute | solution.py:224
  55.5 9.2 %collective-permute-start.13 = (bf16[256,512]{1,0:T(8,128)(2,1)S(1)}, bf16[256,512]{1,0:T(8,128)(2,1)S(1)}, u32[]{:S(2)}, u32[]{:S(2)}) collective-permute-start(bf16[256,512]{1,0:T(8,128)(2,1)S(1)} %shard_map.91), channel_id=1, source_target_pairs={{0,1},{1,0},{2,3},{3,2},{4,5},{5,4},{6,7},{7,6},{8,9},{9,8},{10,11... | collective-permute-start | bytes 786440 | tf_op jit(solution)/shard_map/ppermute | solution.py:283
  56.0 13.5 %collective-permute-start.19 = (bf16[256,512]{1,0:T(8,128)(2,1)S(1)}, bf16[256,512]{1,0:T(8,128)(2,1)S(1)}, u32[]{:S(2)}, u32[]{:S(2)}) collective-permute-start(bf16[256,512]{1,0:T(8,128)(2,1)S(1)} %shard_map.94), channel_id=1, source_target_pairs={{0,1},{1,0},{2,3},{3,2},{4,5},{5,4},{6,7},{7,6},{8,9},{9,8},{10,11... | collective-permute-start | bytes 786440 | tf_op jit(solution)/shard_map/ppermute | solution.py:283
  58.4 30.4 %collective-permute-start.35 = (bf16[256,512]{1,0:T(8,128)(2,1)S(1)}, bf16[256,512]{1,0:T(8,128)(2,1)S(1)}, u32[]{:S(2)}, u32[]{:S(2)}) collective-permute-start(bf16[256,512]{1,0:T(8,128)(2,1)S(1)} %add_convert_fusion.5), channel_id=1, source_target_pairs={{1,2},{2,1},{5,6},{6,5},{9,10},{10,9},{13,14},{14,13},{17,18},{18,... | collective-permute-start | bytes 786440 | tf_op jit(solution)/shard_map/ppermute | solution.py:275
  64.7 67.1 %collective-permute-start.11 = (bf16[256,512]{1,0:T(8,128)(2,1)S(1)}, bf16[256,512]{1,0:T(8,128)(2,1)S(1)}, u32[]{:S(2)}, u32[]{:S(2)}) collective-permute-start(bf16[256,512]{1,0:T(8,128)(2,1)S(1)} %add_convert_fusion.17), channel_id=1, source_target_pairs={{1,2},{2,1},{5,6},{6,5},{9,10},{10,9},{13,14},{14,13},{17,18},{18,... | collective-permute-start | bytes 786440 | tf_op jit(solution)/shard_map/ppermute | solution.py:275
  69.5 19.2 %collective-permute-start.14 = (bf16[256,512]{1,0:T(8,128)(2,1)S(1)}, bf16[256,512]{1,0:T(8,128)(2,1)S(1)}, u32[]{:S(2)}, u32[]{:S(2)}) collective-permute-start(bf16[256,512]{1,0:T(8,128)(2,1)S(1)} %add_convert_fusion.15), channel_id=1, source_target_pairs={{1,2},{2,1},{5,6},{6,5},{9,10},{10,9},{13,14},{14,13},{17,18},{18,... | collective-permute-start | bytes 786440 | tf_op jit(solution)/shard_map/ppermute | solution.py:275
  70.3 12.2 %collective-permute-start.20 = (bf16[256,512]{1,0:T(8,128)(2,1)S(1)}, bf16[256,512]{1,0:T(8,128)(2,1)S(1)}, u32[]{:S(2)}, u32[]{:S(2)}) collective-permute-start(bf16[256,512]{1,0:T(8,128)(2,1)S(1)} %add_convert_fusion.13), channel_id=1, source_target_pairs={{1,2},{2,1},{5,6},{6,5},{9,10},{10,9},{13,14},{14,13},{17,18},{18,... | collective-permute-start | bytes 786440 | tf_op jit(solution)/shard_map/ppermute | solution.py:275
  82.5 13.3 %collective-permute-start.21 = (bf16[256,512]{1,0:T(8,128)(2,1)S(1)}, bf16[256,512]{1,0:T(8,128)(2,1)S(1)}, u32[]{:S(2)}, u32[]{:S(2)}) collective-permute-start(bf16[256,512]{1,0:T(8,128)(2,1)S(1)} %broadcast_select_fusion.9), channel_id=1, source_target_pairs={{0,1},{1,0},{2,3},{3,2},{4,5},{5,4},{6,7},{7,6},{8,9},{9,8},{10,11... | collective-permute-start | bytes 786440 | tf_op jit(solution)/shard_map/ppermute | solution.py:283
  88.8 12.7 %collective-permute-start.15 = (bf16[256,512]{1,0:T(8,128)(2,1)S(1)}, bf16[256,512]{1,0:T(8,128)(2,1)S(1)}, u32[]{:S(2)}, u32[]{:S(2)}) collective-permute-start(bf16[256,512]{1,0:T(8,128)(2,1)S(1)} %broadcast_select_fusion.11), channel_id=1, source_target_pairs={{0,1},{1,0},{2,3},{3,2},{4,5},{5,4},{6,7},{7,6},{8,9},{9,8},{10,11... | collective-permute-start | bytes 786440 | tf_op jit(solution)/shard_map/ppermute | solution.py:283
  89.0 16.5 %collective-permute-start.36 = (bf16[256,512]{1,0:T(8,128)(2,1)S(1)}, bf16[256,512]{1,0:T(8,128)(2,1)S(1)}, u32[]{:S(2)}, u32[]{:S(2)}) collective-permute-start(bf16[256,512]{1,0:T(8,128)(2,1)S(1)} %broadcast_select_fusion.5), channel_id=1, source_target_pairs={{0,1},{1,0},{2,3},{3,2},{4,5},{5,4},{6,7},{7,6},{8,9},{9,8},{10,11... | collective-permute-start | bytes 786440 | tf_op jit(solution)/shard_map/ppermute | solution.py:283
  96.1 23.7 %collective-permute-start.22 = (bf16[256,512]{1,0:T(8,128)(2,1)S(1)}, bf16[256,512]{1,0:T(8,128)(2,1)S(1)}, u32[]{:S(2)}, u32[]{:S(2)}) collective-permute-start(bf16[256,512]{1,0:T(8,128)(2,1)S(1)} %add_convert_fusion.11), channel_id=1, source_target_pairs={{1,2},{2,1},{5,6},{6,5},{9,10},{10,9},{13,14},{14,13},{17,18},{18,... | collective-permute-start | bytes 786440 | tf_op jit(solution)/shard_map/ppermute | solution.py:275
  101.7 22.2 %collective-permute-start.29 = (bf16[256,512]{1,0:T(8,128)(2,1)S(1)}, bf16[256,512]{1,0:T(8,128)(2,1)S(1)}, u32[]{:S(2)}, u32[]{:S(2)}) collective-permute-start(bf16[256,512]{1,0:T(8,128)(2,1)S(1)} %add_convert_fusion.7), channel_id=1, source_target_pairs={{1,2},{2,1},{5,6},{6,5},{9,10},{10,9},{13,14},{14,13},{17,18},{18,... | collective-permute-start | bytes 786440 | tf_op jit(solution)/shard_map/ppermute | solution.py:275
  105.7 5.8 %collective-permute-start.39 = (bf16[64,1024]{1,0:T(8,128)(2,1)S(1)}, bf16[64,1024]{1,0:T(8,128)(2,1)S(1)}, u32[]{:S(2)}, u32[]{:S(2)}) collective-permute-start(bf16[64,1024]{1,0:T(8,128)(2,1)S(1)} %get-tuple-element.7), channel_id=1, source_target_pairs={{0,12},{4,8},{8,4},{12,0},{1,13},{5,9},{9,5},{13,1},{2,14},{6,10},... | collective-permute-start | bytes 393224 | tf_op jit(solution)/shard_map/ppermute | solution.py:224
  111.5 5.5 %collective-permute-start.38 = (bf16[64,1024]{1,0:T(8,128)(2,1)S(1)}, bf16[64,1024]{1,0:T(8,128)(2,1)S(1)}, u32[]{:S(2)}, u32[]{:S(2)}) collective-permute-start(bf16[64,1024]{1,0:T(8,128)(2,1)S(1)} %get-tuple-element.8), channel_id=1, source_target_pairs={{0,8},{4,12},{8,0},{12,4},{1,9},{5,13},{9,1},{13,5},{2,10},{6,14},... | collective-permute-start | bytes 393224 | tf_op jit(solution)/shard_map/ppermute | solution.py:224
  118.3 5.7 %collective-permute-start.40 = (bf16[256,512]{1,0:T(8,128)(2,1)S(1)}, bf16[256,512]{1,0:T(8,128)(2,1)S(1)}, u32[]{:S(2)}, u32[]{:S(2)}) collective-permute-start(bf16[256,512]{1,0:T(8,128)(2,1)S(1)} %add_convert_fusion.3), channel_id=1, source_target_pairs={{1,2},{2,1},{5,6},{6,5},{9,10},{10,9},{13,14},{14,13},{17,18},{18,... | collective-permute-start | bytes 786440 | tf_op jit(solution)/shard_map/ppermute | solution.py:275
  119.4 11.0 %collective-permute-start.9 = (bf16[64,2048]{1,0:T(8,128)(2,1)S(1)}, bf16[64,2048]{1,0:T(8,128)(2,1)S(1)}, u32[]{:S(2)}, u32[]{:S(2)}) collective-permute-start(bf16[64,2048]{1,0:T(8,128)(2,1)S(1)} %select_convert_fusion), channel_id=1, source_target_pairs={{0,8},{4,12},{8,0},{12,4},{1,9},{5,13},{9,1},{13,5},{2,10},{6,14},... | collective-permute-start | bytes 786440 | tf_op jit(solution)/shard_map/ppermute | solution.py:224
  119.9 13.1 %collective-permute-start.23 = (bf16[256,512]{1,0:T(8,128)(2,1)S(1)}, bf16[256,512]{1,0:T(8,128)(2,1)S(1)}, u32[]{:S(2)}, u32[]{:S(2)}) collective-permute-start(bf16[256,512]{1,0:T(8,128)(2,1)S(1)} %broadcast_select_fusion.8), channel_id=1, source_target_pairs={{0,1},{1,0},{2,3},{3,2},{4,5},{5,4},{6,7},{7,6},{8,9},{9,8},{10,11... | collective-permute-start | bytes 786440 | tf_op jit(solution)/shard_map/ppermute | solution.py:283
  124.0 18.5 %collective-permute-start.30 = (bf16[256,512]{1,0:T(8,128)(2,1)S(1)}, bf16[256,512]{1,0:T(8,128)(2,1)S(1)}, u32[]{:S(2)}, u32[]{:S(2)}) collective-permute-start(bf16[256,512]{1,0:T(8,128)(2,1)S(1)} %add_convert_fusion.6), channel_id=1, source_target_pairs={{0,1},{1,0},{2,3},{3,2},{4,5},{5,4},{6,7},{7,6},{8,9},{9,8},{10,11... | collective-permute-start | bytes 786440 | tf_op jit(solution)/shard_map/ppermute | solution.py:283
  124.1 18.2 %collective-permute-start.41 = (bf16[256,512]{1,0:T(8,128)(2,1)S(1)}, bf16[256,512]{1,0:T(8,128)(2,1)S(1)}, u32[]{:S(2)}, u32[]{:S(2)}) collective-permute-start(bf16[256,512]{1,0:T(8,128)(2,1)S(1)} %add_convert_fusion.2), channel_id=1, source_target_pairs={{0,1},{1,0},{2,3},{3,2},{4,5},{5,4},{6,7},{7,6},{8,9},{9,8},{10,11... | collective-permute-start | bytes 786440 | tf_op jit(solution)/shard_map/ppermute | solution.py:283
  131.9 19.0 %collective-permute-start.12 = (bf16[256,512]{1,0:T(8,128)(2,1)S(1)}, bf16[256,512]{1,0:T(8,128)(2,1)S(1)}, u32[]{:S(2)}, u32[]{:S(2)}) collective-permute-start(bf16[256,512]{1,0:T(8,128)(2,1)S(1)} %broadcast_select_fusion.13), channel_id=1, source_target_pairs={{0,1},{1,0},{2,3},{3,2},{4,5},{5,4},{6,7},{7,6},{8,9},{9,8},{10,11... | collective-permute-start | bytes 786440 | tf_op jit(solution)/shard_map/ppermute | solution.py:283
  133.1 11.2 %collective-permute-start.47 = (bf16[64,512]{1,0:T(8,128)(2,1)S(1)}, bf16[64,512]{1,0:T(8,128)(2,1)S(1)}, u32[]{:S(2)}, u32[]{:S(2)}) collective-permute-start(bf16[64,512]{1,0:T(8,128)(2,1)S(1)} %get-tuple-element.16), channel_id=1, source_target_pairs={{0,12},{4,8},{8,4},{12,0},{1,13},{5,9},{9,5},{13,1},{2,14},{6,10},... | collective-permute-start | bytes 196616 | tf_op jit(solution)/shard_map/ppermute | solution.py:224
  133.2 11.5 %collective-permute-start.46 = (bf16[64,512]{1,0:T(8,128)(2,1)S(1)}, bf16[64,512]{1,0:T(8,128)(2,1)S(1)}, u32[]{:S(2)}, u32[]{:S(2)}) collective-permute-start(bf16[64,512]{1,0:T(8,128)(2,1)S(1)} %get-tuple-element.17), channel_id=1, source_target_pairs={{0,8},{4,12},{8,0},{12,4},{1,9},{5,13},{9,1},{13,5},{2,10},{6,14},... | collective-permute-start | bytes 196616 | tf_op jit(solution)/shard_map/ppermute | solution.py:224
  142.5 4.3 %collective-permute-start.44 = (bf16[64,512]{1,0:T(8,128)(2,1)S(1)}, bf16[64,512]{1,0:T(8,128)(2,1)S(1)}, u32[]{:S(2)}, u32[]{:S(2)}) collective-permute-start(bf16[64,512]{1,0:T(8,128)(2,1)S(1)} %get-tuple-element.20), channel_id=1, source_target_pairs={{0,12},{4,8},{8,4},{12,0},{1,13},{5,9},{9,5},{13,1},{2,14},{6,10},... | collective-permute-start | bytes 196616 | tf_op jit(solution)/shard_map/ppermute | solution.py:224
  144.4 4.3 %collective-permute-start.43 = (bf16[64,512]{1,0:T(8,128)(2,1)S(1)}, bf16[64,512]{1,0:T(8,128)(2,1)S(1)}, u32[]{:S(2)}, u32[]{:S(2)}) collective-permute-start(bf16[64,512]{1,0:T(8,128)(2,1)S(1)} %get-tuple-element.21), channel_id=1, source_target_pairs={{0,8},{4,12},{8,0},{12,4},{1,9},{5,13},{9,1},{13,5},{2,10},{6,14},... | collective-permute-start | bytes 196616 | tf_op jit(solution)/shard_map/ppermute | solution.py:224
  144.8 5.3 %collective-permute-start.42 = (bf16[64,512]{1,0:T(8,128)(2,1)S(1)}, bf16[64,512]{1,0:T(8,128)(2,1)S(1)}, u32[]{:S(2)}, u32[]{:S(2)}) collective-permute-start(bf16[64,512]{1,0:T(8,128)(2,1)S(1)} %get-tuple-element.22), channel_id=1, source_target_pairs={{0,4},{4,0},{8,12},{12,8},{1,5},{5,1},{9,13},{13,9},{2,6},{6,2},{1... | collective-permute-start | bytes 196616 | tf_op jit(solution)/shard_map/ppermute | solution.py:224
  144.8 7.3 %collective-permute-start.24 = (bf16[256,512]{1,0:T(8,128)(2,1)S(1)}, bf16[256,512]{1,0:T(8,128)(2,1)S(1)}, u32[]{:S(2)}, u32[]{:S(2)}) collective-permute-start(bf16[256,512]{1,0:T(8,128)(2,1)S(1)} %add_convert_fusion.9), channel_id=1, source_target_pairs={{1,2},{2,1},{5,6},{6,5},{9,10},{10,9},{13,14},{14,13},{17,18},{18,... | collective-permute-start | bytes 786440 | tf_op jit(solution)/shard_map/ppermute | solution.py:275
  146.8 23.8 %collective-permute-start.33 = (bf16[64,512]{1,0:T(8,128)(2,1)S(1)}, bf16[64,512]{1,0:T(8,128)(2,1)S(1)}, u32[]{:S(2)}, u32[]{:S(2)}) collective-permute-start(bf16[64,512]{1,0:T(8,128)(2,1)S(1)} %get-tuple-element.24), channel_id=1, source_target_pairs={{0,12},{4,8},{8,4},{12,0},{1,13},{5,9},{9,5},{13,1},{2,14},{6,10},... | collective-permute-start | bytes 196616 | tf_op jit(solution)/shard_map/ppermute | solution.py:224
  148.7 22.8 %collective-permute-start.32 = (bf16[64,512]{1,0:T(8,128)(2,1)S(1)}, bf16[64,512]{1,0:T(8,128)(2,1)S(1)}, u32[]{:S(2)}, u32[]{:S(2)}) collective-permute-start(bf16[64,512]{1,0:T(8,128)(2,1)S(1)} %get-tuple-element.25), channel_id=1, source_target_pairs={{0,8},{4,12},{8,0},{12,4},{1,9},{5,13},{9,1},{13,5},{2,10},{6,14},... | collective-permute-start | bytes 196616 | tf_op jit(solution)/shard_map/ppermute | solution.py:224
  150.0 22.5 %collective-permute-start.31 = (bf16[64,512]{1,0:T(8,128)(2,1)S(1)}, bf16[64,512]{1,0:T(8,128)(2,1)S(1)}, u32[]{:S(2)}, u32[]{:S(2)}) collective-permute-start(bf16[64,512]{1,0:T(8,128)(2,1)S(1)} %get-tuple-element.26), channel_id=1, source_target_pairs={{0,4},{4,0},{8,12},{12,8},{1,5},{5,1},{9,13},{13,9},{2,6},{6,2},{1... | collective-permute-start | bytes 196616 | tf_op jit(solution)/shard_map/ppermute | solution.py:224
  151.2 5.2 %collective-permute-start.18 = (bf16[64,1024]{1,0:T(8,128)(2,1)S(1)}, bf16[64,1024]{1,0:T(8,128)(2,1)S(1)}, u32[]{:S(2)}, u32[]{:S(2)}) collective-permute-start(bf16[64,1024]{1,0:T(8,128)(2,1)S(1)} %get-tuple-element.10), channel_id=1, source_target_pairs={{0,12},{4,8},{8,4},{12,0},{1,13},{5,9},{9,5},{13,1},{2,14},{6,10},... | collective-permute-start | bytes 393224 | tf_op jit(solution)/shard_map/ppermute | solution.py:224
  152.1 7.7 %collective-permute-start.17 = (bf16[64,1024]{1,0:T(8,128)(2,1)S(1)}, bf16[64,1024]{1,0:T(8,128)(2,1)S(1)}, u32[]{:S(2)}, u32[]{:S(2)}) collective-permute-start(bf16[64,1024]{1,0:T(8,128)(2,1)S(1)} %get-tuple-element.11), channel_id=1, source_target_pairs={{0,8},{4,12},{8,0},{12,4},{1,9},{5,13},{9,1},{13,5},{2,10},{6,14},... | collective-permute-start | bytes 393224 | tf_op jit(solution)/shard_map/ppermute | solution.py:224
  156.4 6.3 %collective-permute-start.48 = (bf16[256,512]{1,0:T(8,128)(2,1)S(1)}, bf16[256,512]{1,0:T(8,128)(2,1)S(1)}, u32[]{:S(2)}, u32[]{:S(2)}) collective-permute-start(bf16[256,512]{1,0:T(8,128)(2,1)S(1)} %add_convert_fusion.1), channel_id=1, source_target_pairs={{1,2},{2,1},{5,6},{6,5},{9,10},{10,9},{13,14},{14,13},{17,18},{18,... | collective-permute-start | bytes 786440 | tf_op jit(solution)/shard_map/ppermute | solution.py:275
  159.8 9.0 %collective-permute-start.25 = (bf16[256,512]{1,0:T(8,128)(2,1)S(1)}, bf16[256,512]{1,0:T(8,128)(2,1)S(1)}, u32[]{:S(2)}, u32[]{:S(2)}) collective-permute-start(bf16[256,512]{1,0:T(8,128)(2,1)S(1)} %add_convert_fusion.8), channel_id=1, source_target_pairs={{0,1},{1,0},{2,3},{3,2},{4,5},{5,4},{6,7},{7,6},{8,9},{9,8},{10,11... | collective-permute-start | bytes 786440 | tf_op jit(solution)/shard_map/ppermute | solution.py:283
  162.7 9.7 %collective-permute-start.16 = (bf16[64,1024]{1,0:T(8,128)(2,1)S(1)}, bf16[64,1024]{1,0:T(8,128)(2,1)S(1)}, u32[]{:S(2)}, u32[]{:S(2)}) collective-permute-start(bf16[64,1024]{1,0:T(8,128)(2,1)S(1)} %get-tuple-element.12), channel_id=1, source_target_pairs={{0,4},{4,0},{8,12},{12,8},{1,5},{5,1},{9,13},{13,9},{2,6},{6,2},{1... | collective-permute-start | bytes 393224 | tf_op jit(solution)/shard_map/ppermute | solution.py:224
  168.8 8.6 %collective-permute-start.49 = (bf16[256,512]{1,0:T(8,128)(2,1)S(1)}, bf16[256,512]{1,0:T(8,128)(2,1)S(1)}, u32[]{:S(2)}, u32[]{:S(2)}) collective-permute-start(bf16[256,512]{1,0:T(8,128)(2,1)S(1)} %add_convert_fusion), channel_id=1, source_target_pairs={{0,1},{1,0},{2,3},{3,2},{4,5},{5,4},{6,7},{7,6},{8,9},{9,8},{10,11... | collective-permute-start | bytes 786440 | tf_op jit(solution)/shard_map/ppermute | solution.py:283
  170.6 4.3 %collective-permute-start.28 = (bf16[64,512]{1,0:T(8,128)(2,1)S(1)}, bf16[64,512]{1,0:T(8,128)(2,1)S(1)}, u32[]{:S(2)}, u32[]{:S(2)}) collective-permute-start(bf16[64,512]{1,0:T(8,128)(2,1)S(1)} %get-tuple-element.28), channel_id=1, source_target_pairs={{0,12},{4,8},{8,4},{12,0},{1,13},{5,9},{9,5},{13,1},{2,14},{6,10},... | collective-permute-start | bytes 196616 | tf_op jit(solution)/shard_map/ppermute | solution.py:224
  171.5 4.9 %collective-permute-start.27 = (bf16[64,512]{1,0:T(8,128)(2,1)S(1)}, bf16[64,512]{1,0:T(8,128)(2,1)S(1)}, u32[]{:S(2)}, u32[]{:S(2)}) collective-permute-start(bf16[64,512]{1,0:T(8,128)(2,1)S(1)} %get-tuple-element.29), channel_id=1, source_target_pairs={{0,8},{4,12},{8,0},{12,4},{1,9},{5,13},{9,1},{13,5},{2,10},{6,14},... | collective-permute-start | bytes 196616 | tf_op jit(solution)/shard_map/ppermute | solution.py:224
  177.7 5.9 %collective-permute-start.52 = (bf16[64,512]{1,0:T(8,128)(2,1)S(1)}, bf16[64,512]{1,0:T(8,128)(2,1)S(1)}, u32[]{:S(2)}, u32[]{:S(2)}) collective-permute-start(bf16[64,512]{1,0:T(8,128)(2,1)S(1)} %get-tuple-element.13), channel_id=1, source_target_pairs={{0,12},{4,8},{8,4},{12,0},{1,13},{5,9},{9,5},{13,1},{2,14},{6,10},... | collective-permute-start | bytes 196616 | tf_op jit(solution)/shard_map/ppermute | solution.py:224
  179.0 4.5 %collective-permute-start.51 = (bf16[64,512]{1,0:T(8,128)(2,1)S(1)}, bf16[64,512]{1,0:T(8,128)(2,1)S(1)}, u32[]{:S(2)}, u32[]{:S(2)}) collective-permute-start(bf16[64,512]{1,0:T(8,128)(2,1)S(1)} %get-tuple-element.14), channel_id=1, source_target_pairs={{0,8},{4,12},{8,0},{12,4},{1,9},{5,13},{9,1},{13,5},{2,10},{6,14},... | collective-permute-start | bytes 196616 | tf_op jit(solution)/shard_map/ppermute | solution.py:224
  (13 other events, 71.1 us)

commit v2 on v0

--- a/solution.py
+++ b/solution.py
@@ -1,14 +1,447 @@
 import jax
 import jax.numpy as jnp
 from jax import lax
+from jax.experimental import pallas as pl
+from jax.experimental.pallas import tpu as pltpu
 from jax.sharding import PartitionSpec as P
 
 DKV = 1024
 R = 64
 BLOCK = 128
+BF = jnp.bfloat16
+F32 = jnp.float32
+WHOLE = pl.BlockSpec(memory_space=pltpu.VMEM)
+SCALARS = pl.BlockSpec(memory_space=pltpu.SMEM)
+FAR = pl.BlockSpec(memory_space=pltpu.HBM)
+EDGE, UPPER, ODD, PLACE = range(4)
+
+
+def launch(body, args, specs, outs, out_specs, scratch, mib, flops, moved, marks, grid=()):
+    n_in, n_args, n_outs = len(args) + len(marks), len(args), len(outs)
+
+    def kernel(*refs):
+        refs[n_in + n_outs][...] = jnp.zeros((8, 128), F32)
+        body(*refs[:n_args], *refs[n_in : n_in + n_outs], *refs[n_in + n_outs + 1 :])
+
+    return pl.pallas_call(
+        kernel,
+        grid=grid,
+        out_shape=[*outs, jax.ShapeDtypeStruct((8, 128), F32)],
+        in_specs=[*specs, *[pl.BlockSpec(memory_space=pl.ANY)] * len(marks)],
+        out_specs=[*out_specs, WHOLE],
+        scratch_shapes=scratch,
+        compiler_params=pltpu.CompilerParams(vmem_limit_bytes=mib * 1024 * 1024),
+        cost_estimate=pl.CostEstimate(flops=flops, bytes_accessed=moved, transcendentals=0),
+    )(*args, *marks)
+
+
+def back_call(flags, slot_rows, up_stack, out_grad, marks, pieces=4):
+    rows, cols = out_grad.shape
+    wide = up_stack.shape[0]
+    depth = rows // pieces
+
+    def body(flag_ref, slot_ref, up_ref, grad_ref, out_ref, held, sems):
+        copies = []
+        for p in range(pieces):
+            here = pl.ds(p * depth, depth)
+            copies.append(pltpu.make_async_copy(grad_ref.at[here, :], held.at[p], sems.at[p]))
+            copies[-1].start()
+        for p in range(pieces):
+            copies[p].wait()
+            here = slice(p * depth, (p + 1) * depth)
+            every = lax.dot_general(
+                up_ref[...], held[p], (((1,), (1,)), ((), ())), preferred_element_type=F32
+            )
+            rel = jnp.bitwise_xor(slot_ref[:, here], flag_ref[PLACE])
+            total = jnp.zeros((R, depth), F32)
+            for m in range(wide // R):
+                total += jnp.where(rel == m, every[m * R : (m + 1) * R], 0.0)
+            out_ref[:, here] = total
+
+    return launch(
+        body,
+        (flags, slot_rows, up_stack, out_grad),
+        (SCALARS, WHOLE, WHOLE, FAR),
+        (jax.ShapeDtypeStruct((R, rows), F32),),
+        (WHOLE,),
+        [pltpu.VMEM((pieces, depth, cols), BF), pltpu.SemaphoreType.DMA((pieces,))],
+        8,
+        2 * rows * cols * wide,
+        rows * cols * 2,
+        marks,
+    )
+
+
+def outer_call(kind, flags, slot_rows, ranks, wide, count, starts, width, marks, pieces=4):
+    rows = wide.shape[0]
+    depth = rows // pieces
+    n = len(starts)
+    half = rows // 2
+    n_extra = {"sum": 2, "halves": 1, "whole": 0, "late": 0}[kind]
+
+    def body(flag_ref, slot_ref, *refs):
+        rank_refs = refs[: len(ranks)]
+        wide_ref = refs[len(ranks)]
+        outs = refs[len(ranks) + 1 : len(ranks) + 1 + n]
+        extra = refs[len(ranks) + 1 + n : len(ranks) + 1 + n + n_extra]
+        lhs, held, sems = refs[-3:]
+
+        def copy(i, p):
+            return pltpu.make_async_copy(
+                wide_ref.at[pl.ds(p * depth, depth), pl.ds(starts[i], width)],
+                held.at[i, p],
+                sems.at[i, p],
+            )
+
+        for i in range(n):
+            for p in range(pieces):
+                copy(i, p).start()
+        odd = flag_ref[ODD] == 1
+        if kind in ("sum", "late"):
+            rank = rank_refs[0][...] + rank_refs[1][...].astype(F32)
+        elif kind == "halves":
+            mine, theirs = rank_refs[0][...].astype(F32), rank_refs[1][...].astype(F32)
+            first = jnp.where(odd, theirs, mine)
+            second = jnp.where(odd, mine, theirs)
+            rank = jnp.concatenate([first, second], axis=1)
+        else:
+            rank = rank_refs[0][...].astype(F32)
+        if kind in ("sum", "halves"):
+            extra[0][...] = rank.astype(BF)
+        if kind == "sum":
+            extra[1][...] = jnp.where(odd, rank[:, half:], rank[:, :half]).astype(BF)
+        slot = slot_ref[...]
+        for m in range(count):
+            lhs[m * R : (m + 1) * R, :] = jnp.where(slot == m, rank, 0.0).astype(BF)
+        for i in range(n):
+            total = jnp.zeros(outs[i].shape, F32)
+            for p in range(pieces):
+                copy(i, p).wait()
+                total += jnp.dot(
+                    lhs[:, p * depth : (p + 1) * depth], held[i, p], preferred_element_type=F32
+                )
+            outs[i][...] = total.astype(BF)
+
+    outs = [jax.ShapeDtypeStruct((count * R, width), BF)] * n
+    outs += [jax.ShapeDtypeStruct((R, rows), BF), jax.ShapeDtypeStruct((R, half), BF)][:n_extra]
+    return launch(
+        body,
+        (flags, slot_rows, *ranks, wide),
+        (SCALARS, WHOLE, *[WHOLE] * len(ranks), FAR),
+        outs,
+        [WHOLE] * len(outs),
+        [
+            pltpu.VMEM((count * R, rows), BF),
+            pltpu.VMEM((n, pieces, depth, width), BF),
+            pltpu.SemaphoreType.DMA((n, pieces)),
+        ],
+        7 + 2 * n,
+        2 * rows * count * R * width * n,
+        rows * width * 2 * n,
+        marks,
+    )
+
+
+def shrink_call(slot, pool, acts, marks, per=4):
+    rows, width = acts.shape
+
+    def body(slot_ref, pool_ref, acts_ref, out_ref):
+        i = pl.program_id(0)
+        for b in range(per):
+            here = slice(b * BLOCK, (b + 1) * BLOCK)
+            part = jnp.dot(
+                acts_ref[here, :], pool_ref[slot_ref[i * per + b]], preferred_element_type=F32
+            )
+            out_ref[:, here] = part.T
+
+    return launch(
+        body,
+        (slot, pool, acts),
+        (SCALARS, WHOLE, pl.BlockSpec((per * BLOCK, width), lambda i: (i, 0))),
+        (jax.ShapeDtypeStruct((2 * R, rows), F32),),
+        (pl.BlockSpec((2 * R, per * BLOCK), lambda i: (0, i)),),
+        [],
+        12,
+        4 * rows * width * 2 * R,
+        rows * width * 2,
+        marks,
+        (rows // (BLOCK * per),),
+    )
+
+
+def mix_call(flags, part, peer, marks):
+    rows = part.shape[1]
+
+    def body(flag_ref, part_ref, peer_ref, keep_ref, send_ref):
+        upper = flag_ref[UPPER] == 1
+        key = part_ref[:R] + peer_ref[:R]
+        value = part_ref[R:] + peer_ref[R:]
+        keep_ref[...] = jnp.where(upper, value, key)
+        send_ref[...] = jnp.where(upper, key, value).astype(BF)
+
+    return launch(
+        body,
+        (flags, part, peer),
+        (SCALARS, WHOLE, WHOLE),
+        (jax.ShapeDtypeStruct((R, rows), F32), jax.ShapeDtypeStruct((R, rows), BF)),
+        (WHOLE, WHOLE),
+        [],
+        6,
+        1,
+        rows * R * 16,
+        marks,
+    )
+
+
+def expand_call(flags, slot, pool, own, other, width, marks, per=4):
+    rows = own.shape[1]
+
+    def body(flag_ref, slot_ref, pool_ref, own_ref, other_ref, out_ref):
+        i = pl.program_id(0)
+        upper = flag_ref[UPPER] == 1
+        for b in range(per):
+            here = slice(b * BLOCK, (b + 1) * BLOCK)
+            mine, theirs = own_ref[:, here].astype(F32), other_ref[:, here].astype(F32)
+            rank = jnp.concatenate(
+                [jnp.where(upper, theirs, mine), jnp.where(upper, mine, theirs)], axis=0
+            )
+            out_ref[here, :] = lax.dot_general(
+                rank.T.astype(BF),
+                pool_ref[slot_ref[i * per + b]],
+                (((1,), (1,)), ((), ())),
+                preferred_element_type=F32,
+            ).astype(BF)
+
+    return launch(
+        body,
+        (flags, slot, pool, own, other),
+        (
+            SCALARS,
+            SCALARS,
+            WHOLE,
+            pl.BlockSpec((R, per * BLOCK), lambda i: (0, i)),
+            pl.BlockSpec((R, per * BLOCK), lambda i: (0, i)),
+        ),
+        (pltpu.HBM((rows, width), BF),),
+        (pl.BlockSpec((per * BLOCK, width), lambda i: (i, 0)),),
+        [],
+        12,
+        4 * rows * width * 2 * R,
+        rows * width * 2,
+        marks,
+        (rows // (BLOCK * per),),
+    )
+
+
+def place_call(first, second, start, total_rows, held):
+    count = first.shape[0] // R
+    width = first.shape[1]
+    extra = [] if held is None else [held]
+
+    def kernel(first_ref, second_ref, *refs):
+        out_ref, turned, sems = refs[-3:]
+        copies = []
+        for m in range(count):
+            rows = slice(m * R, (m + 1) * R)
+            a, b = first_ref[rows].astype(F32), second_ref[rows].astype(F32)
+            pair = [a, b] if m < count // 2 else [b, a]
+            turned[m, :, :] = jnp.concatenate(pair, axis=0).T.astype(BF)
+            row = m * (total_rows // count) + start
+            copies.append(
+                pltpu.make_async_copy(
+                    turned.at[m], out_ref.at[pl.ds(row, width), :], sems.at[m]
+                )
+            )
+            copies[-1].start()
+        for copy in copies:
+            copy.wait()
+
+    return pl.pallas_call(
+        kernel,
+        out_shape=jax.ShapeDtypeStruct((total_rows, 2 * R), BF),
+        in_specs=[WHOLE, WHOLE] + [pl.BlockSpec(memory_space=pl.ANY)] * len(extra),
+        out_specs=pl.BlockSpec(memory_space=pl.ANY),
+        scratch_shapes=[
+            pltpu.VMEM((count, width, 2 * R), BF),
+            pltpu.SemaphoreType.DMA((count,)),
+        ],
+        input_output_aliases={} if held is None else {2: 0},
+        compiler_params=pltpu.CompilerParams(vmem_limit_bytes=10 * 1024 * 1024),
+        cost_estimate=pl.CostEstimate(
+            flops=1, bytes_accessed=4 * count * width * 2 * R * 2, transcendentals=0
+        ),
+    )(first, second, *extra)
+
+
+def step_call(flags, arrays, outs, shape, marks):
+    names = list(arrays)
+
+    def body(flag_ref, *refs):
+        got = dict(zip(names, refs[: len(names)]))
+        put = dict(zip(outs, refs[len(names) :]))
+        edge = flag_ref[EDGE] == 1
+
+        def add(a, b):
+            return (got[a][...].astype(F32) + got[b][...].astype(F32)).astype(BF)
+
+        if "inner" in put:
+            put["inner"][...] = add("old_part", "from_line")
+        if "line" in put:
+            if "old_inner" in got and "part" in got:
+
+                @pl.when(edge)
+                def _():
+                    put["line"][...] = got["part"][...]
+
+                @pl.when(jnp.logical_not(edge))
+                def _():
+                    put["line"][...] = add("old_inner", "from_inner")
+
+            elif "old_inner" in got:
+                put["line"][...] = add("old_inner", "from_inner")
+            else:
+                put["line"][...] = got["part"][...]
+        if "final" in put:
+
+            @pl.when(edge)
+            def _():
+                put["final"][...] = got["from_line"][...]
+
+            @pl.when(jnp.logical_not(edge))
+            def _():
+                put["final"][...] = got["old_line"][...]
+
+    made = launch(
+        body,
+        (flags, *arrays.values()),
+        (SCALARS, *[WHOLE] * len(names)),
+        [jax.ShapeDtypeStruct(shape, BF)] * len(outs),
+        [WHOLE] * len(outs),
+        [],
+        6,
+        1,
+        12 * shape[0] * shape[1],
+        marks,
+    )
+    return dict(zip([*outs, "mark"], made))
 
 
 def local(acts, out_grad, tenant_ids, slot_map, down_pool, up_pool):
+    acts = pltpu.with_memory_space_constraint(acts, pltpu.HBM)
+    out_grad = pltpu.with_memory_space_constraint(out_grad, pltpu.HBM)
+    count = lax.axis_size("adapter")
+    j = lax.axis_index("adapter")
+    z = lax.axis_index("dp")
+    rows, width = acts.shape
+    cols = out_grad.shape[1]
+    total_rows = down_pool.shape[1]
+    edge = (z == 0) | (z == 3)
+    flags = jnp.stack([edge.astype(jnp.int32), j // (count // 2), j % 2, j]).astype(jnp.int32)
+
+    def swap(x, m):
+        return lax.ppermute(x, "adapter", [(i, i ^ m) for i in range(count)])
+
+    def to_owner(x):
+        return lax.all_to_all(x, "adapter", split_axis=0, concat_axis=0, tiled=True)
+
+    slot = slot_map[tenant_ids[:, 0]].astype(jnp.int32)
+    slot_rows = jnp.repeat(slot, BLOCK)[None, :]
+
+    def up_piece(m):
+        return lax.dynamic_slice(up_pool[0], (0, (j ^ m) * cols), (R, cols))
+
+    ups = [up_piece(0)] + [swap(up_piece(m), m) for m in range(1, count)]
+    back_part, mark = back_call(flags, slot_rows, jnp.concatenate(ups, axis=0), out_grad, [])
+    back_peer = swap(back_part, 1)
+
+    chunk = 512
+    names = ["own0", "own1", "own2", "own3", "other0", "other1", "other2", "other3", "up"]
+    n = len(names)
+    parts, line, inner, from_line, from_inner, final = {}, {}, {}, {}, {}, {}
+
+    def joined(*which):
+        return jnp.concatenate([final[w] for w in which], axis=1)
+
+    for t in range(n + 6):
+        if t == 0:
+            parts["own0"], d_own, d_half, mark = outer_call(
+                "sum", flags, slot_rows, [back_part, back_peer], acts, count, [0], chunk, []
+            )
+            came_half = swap(d_half, 2)
+            came_other = swap(came_half, 1)
+            pool_in, _ = lax.optimization_barrier((down_pool[0], came_half))
+            pool = to_owner(pool_in).reshape(count, width, 2 * R)
+            pool = pltpu.with_memory_space_constraint(pool, pltpu.HBM)
+        if t == 1:
+            starts = [chunk, 2 * chunk, 3 * chunk]
+            parts["own1"], parts["own2"], parts["own3"], mark = outer_call(
+                "whole", flags, slot_rows, [d_own], acts, count, starts, chunk, [mark]
+            )
+        if t == 4:
+            starts = [0, chunk, 2 * chunk, 3 * chunk]
+            made = outer_call(
+                "halves", flags, slot_rows, [came_half, came_other], acts, count, starts, chunk,
+                [mark],
+            )
+            parts.update({"other%d" % c: made[c] for c in range(4)})
+            d_other, mark = made[4:]
+        if t == 7:
+            shrunk_part, mark = shrink_call(slot, pool, acts, [mark])
+            shrunk_peer = swap(shrunk_part, 1)
+        if t == 8:
+            keep, send, mark = mix_call(flags, shrunk_part, shrunk_peer, [mark])
+            parts["up"], mark = outer_call(
+                "late", flags, slot_rows, [keep, swap(send, 2)], out_grad, count, [0], cols, [mark]
+            )
+        if t == 13:
+            acts_grad, mark = expand_call(
+                flags, slot, pool, d_own, d_other, width, [mark]
+            )
+        if t < 2:
+            line[t] = parts[names[t]]
+        else:
+            arrays, outs = {}, []
+            if t < n:
+                arrays["part"] = parts[names[t]]
+            if t - 2 < n or t >= 6:
+                arrays["from_line"] = from_line[t - 2]
+            if t - 2 < n:
+                arrays["old_part"] = parts[names[t - 2]]
+                outs.append("inner")
+            if 0 <= t - 4 < n:
+                arrays["old_inner"] = inner[t - 2]
+                arrays["from_inner"] = from_inner[t - 2]
+            if t < n or 0 <= t - 4 < n:
+                outs.append("line")
+            if 0 <= t - 6 < n:
+                arrays["old_line"] = line[t - 2]
+                outs.append("final")
+            marks = [mark, came_half] if t == 2 else [mark]
+            made = step_call(flags, arrays, outs, (count * R, chunk), marks)
+            mark = made["mark"]
+            if "inner" in made:
+                inner[t] = made["inner"]
+            if "line" in made:
+                line[t] = made["line"]
+            if "final" in made:
+                final[names[t - 6]] = made["final"]
+        if t in line:
+            from_line[t] = lax.ppermute(line[t], "dp", [(0, 1), (1, 0), (2, 3), (3, 2)])
+        if t in inner:
+            from_inner[t] = lax.ppermute(inner[t], "dp", [(1, 2), (2, 1)])
+
+    split = 3 * chunk
+    own = to_owner(joined("own0", "own1", "own2", "own3"))
+    three = to_owner(joined("other0", "other1", "other2"))
+    last = to_owner(joined("other3", "up"))
+    down_grad = place_call(own[:, :split], three, 0, total_rows, None)
+    down_grad = place_call(own[:, split:], last[:, :chunk], split, total_rows, down_grad)
+    up_got = last[:, chunk:].reshape(count, R, cols)
+    up_grad = jnp.concatenate([up_got[m] for m in range(count)], axis=1)
+    return acts_grad, down_grad[None], up_grad[None]
+
+
+def local_any(acts, out_grad, tenant_ids, slot_map, down_pool, up_pool):
     position = lax.axis_index("adapter")
     row_count, local_width = acts.shape
     col_count = out_grad.shape[1]
@@ -62,8 +495,9 @@
 
 
 def solution(mesh):
+    line_of_four = mesh.shape["adapter"] == 4 and mesh.shape["dp"] == 4
     return jax.shard_map(
-        local,
+        local if line_of_four else local_any,
         mesh=mesh,
         in_specs=(
             P(("groups", "dp"), "adapter"),

time: 445 us -> 162 us (0.36)
  blocking collectives: 208 us -> 0 us
  other arithmetic: 59.9 us -> 4.38 us
  local copies, waits for them, and re-layouts: 56.4 us -> 3.89 us
  starting transfers between devices: 17.4 us -> 60.6 us
  matrix products: 43.1 us -> 0 us
  Pallas kernels: 0 us -> 42.8 us
  waiting for transfers between devices: 58.6 us -> 48.5 us
    psum x2 -> x0, blocking collectives: 208 us -> none  [the longest x1 167 us: local(): total_down, total_up = lax.psum((owned_down, owned_up), 'dp')]
    unnamed x2 -> x0, other arithmetic: 58.8 us -> none
    all_to_all x4, waiting for transfers between devices: 58.6 us -> 5.31 us  [to_owner(): return lax.all_to_all(x, 'adapter', split_axis=0, concat_axis=0, tiled=True)]
    ppermute x0 -> x30, starting transfers between devices: none -> 45 us  [the longest x13 32.3 us: local(): from_line[t] = lax.ppermute(line[t], 'dp', [(0, 1), (1, 0), (2, 3), (3, 2)])]
    ppermute x0 -> x30, waiting for transfers between devices: none -> 43.2 us  [the longest x13 34.8 us: local(): from_line[t] = lax.ppermute(line[t], 'dp', [(0, 1), (1, 0), (2, 3), (3, 2)])]
    dot_general x7 -> x0, matrix products: 43.1 us -> none  [the longest x1 11.4 us: local(): jnp.einsum('bnd,bnr->bdr', acts_blocks, d_shrunk, preferred_element_type=...]
    pallas_call x0 -> x23, Pallas kernels: none -> 42.8 us  [the longest x21 40.5 us: launch(): pl.pallas_call(kernel, grid=grid, out_shape=[*outs, jax.ShapeDtypeStruct(...]
    unnamed x19 -> x2, local copies, waits for them, and re-layouts: 26.7 us -> 0.01 us
  transfers between devices with their start and end apart: 4 -> 34, of which waited for: 2 -> 16; matrix products, arithmetic and copies ran while one was open for 26% -> 3% of each run, Pallas kernels for 0% -> 17%
where the time goes in v2:
time: 162 us; the launch traced here: 161 us
  starting transfers between devices  60.6 us (37%)
  waiting for transfers between devices  48.5 us (30%)
  Pallas kernels  42.8 us (26%)
  other arithmetic  4.38 us (3%)
  local copies, waits for them, and re-layouts  3.89 us (2%)
    pallas_call x21, Pallas kernels, launch(): pl.pallas_call(kernel, grid=grid, out_shape=[*outs, jax.ShapeDtypeStruct(...  40.5 us
    ppermute x13, waiting for transfers between devices, local(): from_line[t] = lax.ppermute(line[t], 'dp', [(0, 1), (1, 0), (2, 3), (3, 2)])  34.8 us
    ppermute x13, starting transfers between devices, local(): from_line[t] = lax.ppermute(line[t], 'dp', [(0, 1), (1, 0), (2, 3), (3, 2)])  32.3 us
    all_to_all x4, starting transfers between devices, to_owner(): return lax.all_to_all(x, 'adapter', split_axis=0, concat_axis=0, tiled=True)  15.7 us
    ppermute x8, waiting for transfers between devices, swap(): return lax.ppermute(x, 'adapter', [(i, i ^ m) for i in range(count)])  8.35 us
    ppermute x8, starting transfers between devices, swap(): return lax.ppermute(x, 'adapter', [(i, i ^ m) for i in range(count)])  6.62 us
    ppermute x9, starting transfers between devices, local(): from_inner[t] = lax.ppermute(inner[t], 'dp', [(1, 2), (2, 1)])  5.99 us
    all_to_all x4, waiting for transfers between devices, to_owner(): return lax.all_to_all(x, 'adapter', split_axis=0, concat_axis=0, tiled=True)  5.31 us
  transfers between devices with their start and end apart: 34, of which 16 were waited for; matrix products, arithmetic and copies ran while one was open for 3% of the time, Pallas kernels for 17%

profile of v2, /device:TPU:0, one launch (start us, length us, event | category | flops | bytes accessed | tf_op | source)
XLA Modules:
  0.0 161.2 jit_solution(11695848009302301907)
XLA Ops:
  0.7 1.0 dynamic-slice_bitcast_fusion.3
  1.6 2.5 %collective-permute-start.2 = (bf16[64,512]{1,0:T(8,128)(2,1)S(1)}, bf16[64,512]{1,0:T(8,128)(2,1)S(1)}, u32[]{:S(2)}, u32[]{:S(2)}) collective-permute-start(bf16[64,512]{1,0:T(8,128)(2,1)S(1)} %get-tuple-element.141), channel_id=1, source_target_pairs={{0,12},{4,8},{8,4},{12,0},{1,13},{5,9},{9,5},{13,1},{2,14},{6,10},... | collective-permute-start | bytes 196616 | tf_op jit(solution)/shard_map/ppermute | solution.py:342
  6.6 2.2 %collective-permute-done.1 = bf16[64,512]{1,0:T(8,128)(2,1)S(1)} collective-permute-done((bf16[64,512]{1,0:T(8,128)(2,1)S(1)}, bf16[64,512]{1,0:T(8,128)(2,1)S(1)}, u32[]{:S(2)}, u32[]{:S(2)}) %collective-permute-start.1) | collective-permute-done | bytes 65568 | tf_op jit(solution)/shard_map/ppermute | solution.py:342
  8.9 3.2 %shard_map.85 = (f32[64,2048]{1,0:T(8,128)S(1)}, f32[8,128]{1,0:T(8,128)}) custom-call(s32[4]{0:T(128)S(1)} %pad_add_fusion.refs_0_, s32[1,2048]{1,0:T(1,128)S(1)} %bitcast.27, bf16[256,512]{1,0:T(8,128)(2,1)S(1)} %pad_maximum_fusion.3.refs_2_, bf16[2048,512]{1,0:T(8,128)(2,1)} %refs_4_.5), custom_call_target="tpu_custom_call" | custom-call | flops 536870912 | bytes 2097152 | tf_op jit(solution)/shard_map/pallas_call | solution.py:26
  12.2 1.9 %collective-permute-done.3.refs_3_ = f32[64,2048]{1,0:T(8,128)S(1)} collective-permute-done((f32[64,2048]{1,0:T(8,128)S(1)}, f32[64,2048]{1,0:T(8,128)S(1)}, u32[]{:S(2)}, u32[]{:S(2)}) %collective-permute-start.3) | collective-permute-done | bytes 524320 | tf_op jit(solution)/shard_map/ppermute | solution.py:342
  14.1 2.6 %shard_map.86 = (bf16[256,512]{1,0:T(8,128)(2,1)S(1)}, bf16[64,2048]{1,0:T(8,128)(2,1)S(1)}, bf16[64,1024]{1,0:T(8,128)(2,1)S(1)}, f32[8,128]{1,0:T(8,128)S(1)}) custom-call(s32[4]{0:T(128)S(1)} %pad_add_fusion.refs_0_, s32[1,2048]{1,0:T(1,128)S(1)} %bitcast.28, f32[64,2048]{1,0:T(8,128)S(1)} %get-tuple-element.69.refs_2_, ...), custom_call_target="tpu_custom_call" | custom-call | flops 536870912 | bytes 2097152 | tf_op jit(solution)/shard_map/pallas_call | solution.py:26
  16.7 1.8 %collective-permute-start.4 = (bf16[64,1024]{1,0:T(8,128)(2,1)S(1)}, bf16[64,1024]{1,0:T(8,128)(2,1)S(1)}, u32[]{:S(2)}, u32[]{:S(2)}) collective-permute-start(bf16[64,1024]{1,0:T(8,128)(2,1)S(1)} %get-tuple-element.70), channel_id=1, source_target_pairs={{0,8},{4,12},{8,0},{12,4},{1,9},{5,13},{9,1},{13,5},{2,10},{6,14},... | collective-permute-start | bytes 393224 | tf_op jit(solution)/shard_map/ppermute | solution.py:342
  18.4 3.9 %collective-permute-done.4.refs_5_.refs_2_ = bf16[64,1024]{1,0:T(8,128)(2,1)S(1)} collective-permute-done((bf16[64,1024]{1,0:T(8,128)(2,1)S(1)}, bf16[64,1024]{1,0:T(8,128)(2,1)S(1)}, u32[]{:S(2)}, u32[]{:S(2)}) %collective-permute-start.4) | collective-permute-done | bytes 131104 | tf_op jit(solution)/shard_map/ppermute | solution.py:342
  22.3 4.5 %all-to-all-start = ((bf16[4,2048,128]{2,1,0:T(8,128)(2,1)}), bf16[4,2048,128]{2,1,0:T(8,128)(2,1)}, u32[]{:S(2)}, u32[]{:S(2)}) async-start(bf16[4,2048,128]{2,1,0:T(8,128)(2,1)} %bitcast.11), calls=%async_computation | async-start | bytes 4194304 | tf_op jit(solution)/shard_map/all_to_all | solution.py:345
  26.8 1.8 %collective-permute-start.7 = (bf16[256,512]{1,0:T(8,128)(2,1)S(1)}, bf16[256,512]{1,0:T(8,128)(2,1)S(1)}, u32[]{:S(2)}, u32[]{:S(2)}) collective-permute-start(bf16[256,512]{1,0:T(8,128)(2,1)S(1)} %get-tuple-element.77.refs_3_), channel_id=1, source_target_pairs={{0,1},{1,0},{2,3},{3,2},{4,5},{5,4},{6,7},{7,6},{8,9},{9,8},{10,11... | collective-permute-start | bytes 786440 | tf_op jit(solution)/shard_map/ppermute | solution.py:429
  28.6 4.4 %shard_map.87 = (bf16[256,512]{1,0:T(8,128)(2,1)S(1)}, bf16[256,512]{1,0:T(8,128)(2,1)S(1)}, bf16[256,512]{1,0:T(8,128)(2,1)S(1)}, f32[8,128]{1,0:T(8,128)S(1)}) custom-call(s32[4]{0:T(128)S(1)} %pad_add_fusion.refs_0_, s32[1,2048]{1,0:T(1,128)S(1)} %bitcast.29, bf16[64,2048]{1,0:T(8,128)(2,1)S(1)} %get-tuple-element.72.refs_2_.refs_3_, ...), custom_call_target="tpu_custom_call" | custom-call | flops 1610612736 | bytes 6291456 | tf_op jit(solution)/shard_map/pallas_call | solution.py:26
  33.3 2.1 %collective-permute-done.7.refs_2_ = bf16[256,512]{1,0:T(8,128)(2,1)S(1)} collective-permute-done((bf16[256,512]{1,0:T(8,128)(2,1)S(1)}, bf16[256,512]{1,0:T(8,128)(2,1)S(1)}, u32[]{:S(2)}, u32[]{:S(2)}) %collective-permute-start.7) | collective-permute-done | bytes 262176 | tf_op jit(solution)/shard_map/ppermute | solution.py:429
  36.1 2.4 %collective-permute-start.8 = (bf16[256,512]{1,0:T(8,128)(2,1)S(1)}, bf16[256,512]{1,0:T(8,128)(2,1)S(1)}, u32[]{:S(2)}, u32[]{:S(2)}) collective-permute-start(bf16[256,512]{1,0:T(8,128)(2,1)S(1)} %get-tuple-element.84), channel_id=1, source_target_pairs={{0,1},{1,0},{2,3},{3,2},{4,5},{5,4},{6,7},{7,6},{8,9},{9,8},{10,11... | collective-permute-start | bytes 786440 | tf_op jit(solution)/shard_map/ppermute | solution.py:429
  39.1 3.1 %collective-permute-done.6.refs_2_ = bf16[256,512]{1,0:T(8,128)(2,1)S(1)} collective-permute-done((bf16[256,512]{1,0:T(8,128)(2,1)S(1)}, bf16[256,512]{1,0:T(8,128)(2,1)S(1)}, u32[]{:S(2)}, u32[]{:S(2)}) %collective-permute-start.6) | collective-permute-done | bytes 262176 | tf_op jit(solution)/shard_map/ppermute | solution.py:429
  42.8 1.3 collective-permute-start.12
  44.9 5.3 %shard_map.90 = (bf16[256,512]{1,0:T(8,128)(2,1)S(1)}, bf16[256,512]{1,0:T(8,128)(2,1)S(1)}, bf16[256,512]{1,0:T(8,128)(2,1)S(1)}, bf16[256,512]{1,0:T(8,128)(2,...) custom-call(s32[4]{0:T(128)S(1)} %pad_add_fusion.refs_0_, s32[1,2048]{1,0:T(1,128)S(1)} %bitcast.30, ...), custom_call_target="tpu_custom_call" | custom-call | flops 2147483648 | bytes 8388608 | tf_op jit(solution)/shard_map/pallas_call | solution.py:26
  50.8 4.4 %collective-permute-start.10 = (bf16[256,512]{1,0:T(8,128)(2,1)S(1)}, bf16[256,512]{1,0:T(8,128)(2,1)S(1)}, u32[]{:S(2)}, u32[]{:S(2)}) collective-permute-start(bf16[256,512]{1,0:T(8,128)(2,1)S(1)} %get-tuple-element.87.refs_6_), channel_id=1, source_target_pairs={{0,1},{1,0},{2,3},{3,2},{4,5},{5,4},{6,7},{7,6},{8,9},{9,8},{10,11... | collective-permute-start | bytes 786440 | tf_op jit(solution)/shard_map/ppermute | solution.py:429
  56.5 3.7 %collective-permute-done.10.refs_2_ = bf16[256,512]{1,0:T(8,128)(2,1)S(1)} collective-permute-done((bf16[256,512]{1,0:T(8,128)(2,1)S(1)}, bf16[256,512]{1,0:T(8,128)(2,1)S(1)}, u32[]{:S(2)}, u32[]{:S(2)}) %collective-permute-start.10) | collective-permute-done | bytes 262176 | tf_op jit(solution)/shard_map/ppermute | solution.py:429
  60.8 6.5 %shard_map.94 = (f32[128,2048]{1,0:T(8,128)S(1)}, f32[8,128]{1,0:T(8,128)S(1)}) custom-call(s32[16]{0:T(128)S(1)} %gather_fusion, bf16[4,2048,128]{2,1,0:T(8,128)(2,1)} %all-to-all-done.refs_1_.refs_2_, bf16[2048,2048]{1,0:T(8,128)(2,1)} %refs_2_.1, f32[8,128]{1,0:T(8,128)S(1)} %get-tuple-element.94.refs_3_), custom_call_target="tpu_custom_call" | custom-call | flops 2147483648 | bytes 8388608 | tf_op jit(solution)/shard_map/pallas_call | solution.py:26
  67.4 3.8 %collective-permute-start.15 = (bf16[256,512]{1,0:T(8,128)(2,1)S(1)}, bf16[256,512]{1,0:T(8,128)(2,1)S(1)}, u32[]{:S(2)}, u32[]{:S(2)}) collective-permute-start(bf16[256,512]{1,0:T(8,128)(2,1)S(1)} %get-tuple-element.97.refs_6_), channel_id=1, source_target_pairs={{0,1},{1,0},{2,3},{3,2},{4,5},{5,4},{6,7},{7,6},{8,9},{9,8},{10,11... | collective-permute-start | bytes 786440 | tf_op jit(solution)/shard_map/ppermute | solution.py:429
  71.8 6.2 %collective-permute-done.15.refs_2_ = bf16[256,512]{1,0:T(8,128)(2,1)S(1)} collective-permute-done((bf16[256,512]{1,0:T(8,128)(2,1)S(1)}, bf16[256,512]{1,0:T(8,128)(2,1)S(1)}, u32[]{:S(2)}, u32[]{:S(2)}) %collective-permute-start.15) | collective-permute-done | bytes 262176 | tf_op jit(solution)/shard_map/ppermute | solution.py:429
  79.4 1.6 collective-permute-start.17
  81.0 3.7 %collective-permute-start.18 = (bf16[256,512]{1,0:T(8,128)(2,1)S(1)}, bf16[256,512]{1,0:T(8,128)(2,1)S(1)}, u32[]{:S(2)}, u32[]{:S(2)}) collective-permute-start(bf16[256,512]{1,0:T(8,128)(2,1)S(1)} %get-tuple-element.105.refs_6_), channel_id=1, source_target_pairs={{0,1},{1,0},{2,3},{3,2},{4,5},{5,4},{6,7},{7,6},{8,9},{9,8},{10,11... | collective-permute-start | bytes 786440 | tf_op jit(solution)/shard_map/ppermute | solution.py:429
  85.3 1.6 collective-permute-start.22
  87.6 2.6 %shard_map.97 = (bf16[256,512]{1,0:T(8,128)(2,1)S(1)}, f32[8,128]{1,0:T(8,128)S(1)}) custom-call(s32[4]{0:T(128)S(1)} %pad_add_fusion.refs_0_, s32[1,2048]{1,0:T(1,128)S(1)} %bitcast.31, f32[64,2048]{1,0:T(8,128)S(1)} %get-tuple-element.101.refs_2_, bf16[64,2048]{1,0:T(8,128)(2,1)S(1)} %collective-permute-done.17.refs_3_, bf16[2048,512]{1,0:T(8,128)(2,1)} %refs_4_.5, ...), custom_call_target="tpu_custom_call" | custom-call | flops 536870912 | bytes 2097152 | tf_op jit(solution)/shard_map/pallas_call | solution.py:26
  90.2 1.7 %collective-permute-done.18.refs_2_ = bf16[256,512]{1,0:T(8,128)(2,1)S(1)} collective-permute-done((bf16[256,512]{1,0:T(8,128)(2,1)S(1)}, bf16[256,512]{1,0:T(8,128)(2,1)S(1)}, u32[]{:S(2)}, u32[]{:S(2)}) %collective-permute-start.18) | collective-permute-done | bytes 262176 | tf_op jit(solution)/shard_map/ppermute | solution.py:429
  92.5 3.6 %collective-permute-done.22.refs_1_ = bf16[256,512]{1,0:T(8,128)(2,1)S(1)} collective-permute-done((bf16[256,512]{1,0:T(8,128)(2,1)S(1)}, bf16[256,512]{1,0:T(8,128)(2,1)S(1)}, u32[]{:S(2)}, u32[]{:S(2)}) %collective-permute-start.22) | collective-permute-done | bytes 262176 | tf_op jit(solution)/shard_map/ppermute | solution.py:429
  96.8 1.1 pad_maximum_fusion
  97.9 4.3 %all-to-all-start.1 = ((bf16[4,64,2048]{2,1,0:T(8,128)(2,1)}), bf16[4,64,2048]{2,1,0:T(8,128)(2,1)}, u32[]{:S(2)}, u32[]{:S(2)}) async-start(bf16[4,64,2048]{2,1,0:T(8,128)(2,1)} %bitcast.33), calls=%async_computation.1 | async-start | bytes 2097152 | tf_op jit(solution)/shard_map/all_to_all | solution.py:345
  102.2 3.7 %collective-permute-start.20 = (bf16[256,512]{1,0:T(8,128)(2,1)S(1)}, bf16[256,512]{1,0:T(8,128)(2,1)S(1)}, u32[]{:S(2)}, u32[]{:S(2)}) collective-permute-start(bf16[256,512]{1,0:T(8,128)(2,1)S(1)} %get-tuple-element.108.refs_5_), channel_id=1, source_target_pairs={{0,1},{1,0},{2,3},{3,2},{4,5},{5,4},{6,7},{7,6},{8,9},{9,8},{10,11... | collective-permute-start | bytes 786440 | tf_op jit(solution)/shard_map/ppermute | solution.py:429
  106.6 1.7 %collective-permute-start.26 = (bf16[256,512]{1,0:T(8,128)(2,1)S(1)}, bf16[256,512]{1,0:T(8,128)(2,1)S(1)}, u32[]{:S(2)}, u32[]{:S(2)}) collective-permute-start(bf16[256,512]{1,0:T(8,128)(2,1)S(1)} %get-tuple-element.116.refs_4_), channel_id=1, source_target_pairs={{0,1},{1,0},{2,3},{3,2},{4,5},{5,4},{6,7},{7,6},{8,9},{9,8},{10,11... | collective-permute-start | bytes 786440 | tf_op jit(solution)/shard_map/ppermute | solution.py:429
  108.9 4.1 %collective-permute-done.20.refs_1_ = bf16[256,512]{1,0:T(8,128)(2,1)S(1)} collective-permute-done((bf16[256,512]{1,0:T(8,128)(2,1)S(1)}, bf16[256,512]{1,0:T(8,128)(2,1)S(1)}, u32[]{:S(2)}, u32[]{:S(2)}) %collective-permute-start.20) | collective-permute-done | bytes 262176 | tf_op jit(solution)/shard_map/ppermute | solution.py:429
  113.7 3.9 %collective-permute-start.24 = (bf16[256,512]{1,0:T(8,128)(2,1)S(1)}, bf16[256,512]{1,0:T(8,128)(2,1)S(1)}, u32[]{:S(2)}, u32[]{:S(2)}) collective-permute-start(bf16[256,512]{1,0:T(8,128)(2,1)S(1)} %get-tuple-element.114.refs_4_), channel_id=1, source_target_pairs={{0,1},{1,0},{2,3},{3,2},{4,5},{5,4},{6,7},{7,6},{8,9},{9,8},{10,11... | collective-permute-start | bytes 786440 | tf_op jit(solution)/shard_map/ppermute | solution.py:429
  119.3 4.7 %collective-permute-done.24.refs_1_ = bf16[256,512]{1,0:T(8,128)(2,1)S(1)} collective-permute-done((bf16[256,512]{1,0:T(8,128)(2,1)S(1)}, bf16[256,512]{1,0:T(8,128)(2,1)S(1)}, u32[]{:S(2)}, u32[]{:S(2)}) %collective-permute-start.24) | collective-permute-done | bytes 262176 | tf_op jit(solution)/shard_map/ppermute | solution.py:429
  124.6 0.9 pad_maximum_fusion.1
  125.5 3.5 %all-to-all-start.3 = ((bf16[4,64,1536]{2,1,0:T(8,128)(2,1)}), bf16[4,64,1536]{2,1,0:T(8,128)(2,1)S(1)}, u32[]{:S(2)}, u32[]{:S(2)}) async-start(bf16[4,64,1536]{2,1,0:T(8,128)(2,1)} %bitcast.16), calls=%async_computation.3 | async-start | bytes 1572864 | tf_op jit(solution)/shard_map/all_to_all | solution.py:345
  129.0 3.7 %collective-permute-start.28 = (bf16[256,512]{1,0:T(8,128)(2,1)S(1)}, bf16[256,512]{1,0:T(8,128)(2,1)S(1)}, u32[]{:S(2)}, u32[]{:S(2)}) collective-permute-start(bf16[256,512]{1,0:T(8,128)(2,1)S(1)} %get-tuple-element.126.refs_2_), channel_id=1, source_target_pairs={{0,1},{1,0},{2,3},{3,2},{4,5},{5,4},{6,7},{7,6},{8,9},{9,8},{10,11... | collective-permute-start | bytes 786440 | tf_op jit(solution)/shard_map/ppermute | solution.py:429
  132.8 6.6 %shard_map.103 = (bf16[2048,2048]{1,0:T(8,128)(2,1)}, f32[8,128]{1,0:T(8,128)S(1)}) custom-call(s32[4]{0:T(128)S(1)} %pad_add_fusion.refs_0_, s32[16]{0:T(128)S(1)} %gather_fusion, bf16[4,2048,128]{2,1,0:T(8,128)(2,1)} %all-to-all-done.refs_1_.refs_2_, bf16[64,2048]{1,0:T(8,128)(2,1)S(1)} %get-tuple-element.72.refs_2_.refs_3_, ...), custom_call_target="tpu_custom_call" | custom-call | flops 2147483648 | bytes 8388608 | tf_op jit(solution)/shard_map/pallas_call | solution.py:26
  140.4 4.8 %collective-permute-done.29.refs_1_ = bf16[256,512]{1,0:T(8,128)(2,1)S(1)} collective-permute-done((bf16[256,512]{1,0:T(8,128)(2,1)S(1)}, bf16[256,512]{1,0:T(8,128)(2,1)S(1)}, u32[]{:S(2)}, u32[]{:S(2)}) %collective-permute-start.29) | collective-permute-done | bytes 262176 | tf_op jit(solution)/shard_map/ppermute | solution.py:429
  145.2 1.2 shard_map.105
  146.4 0.9 pad_maximum_fusion.2
  147.2 3.5 %all-to-all-start.2 = ((bf16[4,64,1024]{2,1,0:T(8,128)(2,1)}), bf16[4,64,1024]{2,1,0:T(8,128)(2,1)S(1)}, u32[]{:S(2)}, u32[]{:S(2)}) async-start(bf16[4,64,1024]{2,1,0:T(8,128)(2,1)} %bitcast.14), calls=%async_computation.2 | async-start | bytes 1048576 | tf_op jit(solution)/shard_map/all_to_all | solution.py:345
  150.7 1.0 slice.39.first_ref
  151.7 1.2 slice.41.first_ref
  152.9 1.3 shard_map.106.refs_0_
  154.2 5.3 %all-to-all-done.2 = bf16[4,64,1024]{2,1,0:T(8,128)(2,1)S(1)} async-done(((bf16[4,64,1024]{2,1,0:T(8,128)(2,1)}), bf16[4,64,1024]{2,1,0:T(8,128)(2,1)S(1)}, u32[]{:S(2)}, u32[]{:S(2)}) %all-to-all-start.2) | async-done | bytes 524320 | tf_op jit(solution)/shard_map/all_to_all | solution.py:345
  159.6 0.9 shard_map.107
  160.5 0.7 maximum_bitcast_fusion
  (60 shorter events, 18.3 us)
Async XLA Ops:
  0.6 4.8 %copy-start = (s32[4]{0:T(128)S(1)}, s32[4]{0:T(128)}, u32[]{:S(2)}) copy-start(s32[4]{0:T(128)} %param.9) | copy-start | bytes 52
  1.6 5.0 %collective-permute-start.2 = (bf16[64,512]{1,0:T(8,128)(2,1)S(1)}, bf16[64,512]{1,0:T(8,128)(2,1)S(1)}, u32[]{:S(2)}, u32[]{:S(2)}) collective-permute-start(bf16[64,512]{1,0:T(8,128)(2,1)S(1)} %get-tuple-element.141), channel_id=1, source_target_pairs={{0,12},{4,8},{8,4},{12,0},{1,13},{5,9},{9,5},{13,1},{2,14},{6,10},... | collective-permute-start | bytes 196616 | tf_op jit(solution)/shard_map/ppermute | solution.py:342
  4.1 4.7 %collective-permute-start.1 = (bf16[64,512]{1,0:T(8,128)(2,1)S(1)}, bf16[64,512]{1,0:T(8,128)(2,1)S(1)}, u32[]{:S(2)}, u32[]{:S(2)}) collective-permute-start(bf16[64,512]{1,0:T(8,128)(2,1)S(1)} %get-tuple-element.142), channel_id=1, source_target_pairs={{0,8},{4,12},{8,0},{12,4},{1,9},{5,13},{9,1},{13,5},{2,10},{6,14},... | collective-permute-start | bytes 196616 | tf_op jit(solution)/shard_map/ppermute | solution.py:342
  4.8 4.0 %collective-permute-start = (bf16[64,512]{1,0:T(8,128)(2,1)S(1)}, bf16[64,512]{1,0:T(8,128)(2,1)S(1)}, u32[]{:S(2)}, u32[]{:S(2)}) collective-permute-start(bf16[64,512]{1,0:T(8,128)(2,1)S(1)} %get-tuple-element.140), channel_id=1, source_target_pairs={{0,4},{4,0},{8,12},{12,8},{1,5},{5,1},{9,13},{13,9},{2,6},{6,2},{1... | collective-permute-start | bytes 196616 | tf_op jit(solution)/shard_map/ppermute | solution.py:342
  12.1 2.0 %collective-permute-start.3 = (f32[64,2048]{1,0:T(8,128)S(1)}, f32[64,2048]{1,0:T(8,128)S(1)}, u32[]{:S(2)}, u32[]{:S(2)}) collective-permute-start(f32[64,2048]{1,0:T(8,128)S(1)} %get-tuple-element.69.refs_2_), channel_id=1, source_target_pairs={{0,4},{4,0},{8,12},{12,8},{1,5},{5,1},{9,13},{13,9},{2,6},{6,2},{1... | collective-permute-start | bytes 1572872 | tf_op jit(solution)/shard_map/ppermute | solution.py:342
  16.7 5.6 %collective-permute-start.4 = (bf16[64,1024]{1,0:T(8,128)(2,1)S(1)}, bf16[64,1024]{1,0:T(8,128)(2,1)S(1)}, u32[]{:S(2)}, u32[]{:S(2)}) collective-permute-start(bf16[64,1024]{1,0:T(8,128)(2,1)S(1)} %get-tuple-element.70), channel_id=1, source_target_pairs={{0,8},{4,12},{8,0},{12,4},{1,9},{5,13},{9,1},{13,5},{2,10},{6,14},... | collective-permute-start | bytes 393224 | tf_op jit(solution)/shard_map/ppermute | solution.py:342
  22.3 38.5 %all-to-all-start = ((bf16[4,2048,128]{2,1,0:T(8,128)(2,1)}), bf16[4,2048,128]{2,1,0:T(8,128)(2,1)}, u32[]{:S(2)}, u32[]{:S(2)}) async-start(bf16[4,2048,128]{2,1,0:T(8,128)(2,1)} %bitcast.11), calls=%async_computation | async-start | bytes 4194304 | tf_op jit(solution)/shard_map/all_to_all | solution.py:345
  26.8 8.7 %collective-permute-start.7 = (bf16[256,512]{1,0:T(8,128)(2,1)S(1)}, bf16[256,512]{1,0:T(8,128)(2,1)S(1)}, u32[]{:S(2)}, u32[]{:S(2)}) collective-permute-start(bf16[256,512]{1,0:T(8,128)(2,1)S(1)} %get-tuple-element.77.refs_3_), channel_id=1, source_target_pairs={{0,1},{1,0},{2,3},{3,2},{4,5},{5,4},{6,7},{7,6},{8,9},{9,8},{10,11... | collective-permute-start | bytes 786440 | tf_op jit(solution)/shard_map/ppermute | solution.py:429
  33.0 9.2 %collective-permute-start.6 = (bf16[256,512]{1,0:T(8,128)(2,1)S(1)}, bf16[256,512]{1,0:T(8,128)(2,1)S(1)}, u32[]{:S(2)}, u32[]{:S(2)}) collective-permute-start(bf16[256,512]{1,0:T(8,128)(2,1)S(1)} %get-tuple-element.75.refs_3_), channel_id=1, source_target_pairs={{0,1},{1,0},{2,3},{3,2},{4,5},{5,4},{6,7},{7,6},{8,9},{9,8},{10,11... | collective-permute-start | bytes 786440 | tf_op jit(solution)/shard_map/ppermute | solution.py:429
  33.3 11.5 %collective-permute-start.5 = (bf16[64,1024]{1,0:T(8,128)(2,1)S(1)}, bf16[64,1024]{1,0:T(8,128)(2,1)S(1)}, u32[]{:S(2)}, u32[]{:S(2)}) collective-permute-start(bf16[64,1024]{1,0:T(8,128)(2,1)S(1)} %collective-permute-done.4.refs_5_.refs_2_), channel_id=1, source_target_pairs={{0,4},{4,0},{8,12},{12,8},{1,5},{5,1},{9,13},{13,9},{2,6},{6,2},{1... | collective-permute-start | bytes 393224 | tf_op jit(solution)/shard_map/ppermute | solution.py:342
  36.1 14.1 %collective-permute-start.8 = (bf16[256,512]{1,0:T(8,128)(2,1)S(1)}, bf16[256,512]{1,0:T(8,128)(2,1)S(1)}, u32[]{:S(2)}, u32[]{:S(2)}) collective-permute-start(bf16[256,512]{1,0:T(8,128)(2,1)S(1)} %get-tuple-element.84), channel_id=1, source_target_pairs={{0,1},{1,0},{2,3},{3,2},{4,5},{5,4},{6,7},{7,6},{8,9},{9,8},{10,11... | collective-permute-start | bytes 786440 | tf_op jit(solution)/shard_map/ppermute | solution.py:429
  38.4 11.7 %collective-permute-start.9 = (bf16[256,512]{1,0:T(8,128)(2,1)S(1)}, bf16[256,512]{1,0:T(8,128)(2,1)S(1)}, u32[]{:S(2)}, u32[]{:S(2)}) collective-permute-start(bf16[256,512]{1,0:T(8,128)(2,1)S(1)} %get-tuple-element.85.refs_4_), channel_id=1, source_target_pairs={{1,2},{2,1},{5,6},{6,5},{9,10},{10,9},{13,14},{14,13},{17,18},{18,... | collective-permute-start | bytes 786440 | tf_op jit(solution)/shard_map/ppermute | solution.py:431
  42.8 13.0 %collective-permute-start.12 = (bf16[256,512]{1,0:T(8,128)(2,1)S(1)}, bf16[256,512]{1,0:T(8,128)(2,1)S(1)}, u32[]{:S(2)}, u32[]{:S(2)}) collective-permute-start(bf16[256,512]{1,0:T(8,128)(2,1)S(1)} %get-tuple-element.90), channel_id=1, source_target_pairs={{0,1},{1,0},{2,3},{3,2},{4,5},{5,4},{6,7},{7,6},{8,9},{9,8},{10,11... | collective-permute-start | bytes 786440 | tf_op jit(solution)/shard_map/ppermute | solution.py:429
  44.2 11.6 %collective-permute-start.13 = (bf16[256,512]{1,0:T(8,128)(2,1)S(1)}, bf16[256,512]{1,0:T(8,128)(2,1)S(1)}, u32[]{:S(2)}, u32[]{:S(2)}) collective-permute-start(bf16[256,512]{1,0:T(8,128)(2,1)S(1)} %get-tuple-element.91.refs_4_), channel_id=1, source_target_pairs={{1,2},{2,1},{5,6},{6,5},{9,10},{10,9},{13,14},{14,13},{17,18},{18,... | collective-permute-start | bytes 786440 | tf_op jit(solution)/shard_map/ppermute | solution.py:431
  50.8 9.4 %collective-permute-start.10 = (bf16[256,512]{1,0:T(8,128)(2,1)S(1)}, bf16[256,512]{1,0:T(8,128)(2,1)S(1)}, u32[]{:S(2)}, u32[]{:S(2)}) collective-permute-start(bf16[256,512]{1,0:T(8,128)(2,1)S(1)} %get-tuple-element.87.refs_6_), channel_id=1, source_target_pairs={{0,1},{1,0},{2,3},{3,2},{4,5},{5,4},{6,7},{7,6},{8,9},{9,8},{10,11... | collective-permute-start | bytes 786440 | tf_op jit(solution)/shard_map/ppermute | solution.py:429
  55.1 5.0 %collective-permute-start.11 = (bf16[256,512]{1,0:T(8,128)(2,1)S(1)}, bf16[256,512]{1,0:T(8,128)(2,1)S(1)}, u32[]{:S(2)}, u32[]{:S(2)}) collective-permute-start(bf16[256,512]{1,0:T(8,128)(2,1)S(1)} %get-tuple-element.88.refs_4_), channel_id=1, source_target_pairs={{1,2},{2,1},{5,6},{6,5},{9,10},{10,9},{13,14},{14,13},{17,18},{18,... | collective-permute-start | bytes 786440 | tf_op jit(solution)/shard_map/ppermute | solution.py:431
  67.3 11.4 %collective-permute-start.14 = (f32[128,2048]{1,0:T(8,128)S(1)}, f32[128,2048]{1,0:T(8,128)S(1)}, u32[]{:S(2)}, u32[]{:S(2)}) collective-permute-start(f32[128,2048]{1,0:T(8,128)S(1)} %get-tuple-element.95.refs_1_), channel_id=1, source_target_pairs={{0,4},{4,0},{8,12},{12,8},{1,5},{5,1},{9,13},{13,9},{2,6},{6,2},{1... | collective-permute-start | bytes 3145736 | tf_op jit(solution)/shard_map/ppermute | solution.py:342
  67.4 10.7 %collective-permute-start.15 = (bf16[256,512]{1,0:T(8,128)(2,1)S(1)}, bf16[256,512]{1,0:T(8,128)(2,1)S(1)}, u32[]{:S(2)}, u32[]{:S(2)}) collective-permute-start(bf16[256,512]{1,0:T(8,128)(2,1)S(1)} %get-tuple-element.97.refs_6_), channel_id=1, source_target_pairs={{0,1},{1,0},{2,3},{3,2},{4,5},{5,4},{6,7},{7,6},{8,9},{9,8},{10,11... | collective-permute-start | bytes 786440 | tf_op jit(solution)/shard_map/ppermute | solution.py:429
  71.1 6.9 %collective-permute-start.16 = (bf16[256,512]{1,0:T(8,128)(2,1)S(1)}, bf16[256,512]{1,0:T(8,128)(2,1)S(1)}, u32[]{:S(2)}, u32[]{:S(2)}) collective-permute-start(bf16[256,512]{1,0:T(8,128)(2,1)S(1)} %get-tuple-element.98.refs_4_), channel_id=1, source_target_pairs={{1,2},{2,1},{5,6},{6,5},{9,10},{10,9},{13,14},{14,13},{17,18},{18,... | collective-permute-start | bytes 786440 | tf_op jit(solution)/shard_map/ppermute | solution.py:431
  79.4 8.2 %collective-permute-start.17 = (bf16[64,2048]{1,0:T(8,128)(2,1)S(1)}, bf16[64,2048]{1,0:T(8,128)(2,1)S(1)}, u32[]{:S(2)}, u32[]{:S(2)}) collective-permute-start(bf16[64,2048]{1,0:T(8,128)(2,1)S(1)} %get-tuple-element.102), channel_id=1, source_target_pairs={{0,8},{4,12},{8,0},{12,4},{1,9},{5,13},{9,1},{13,5},{2,10},{6,14},... | collective-permute-start | bytes 786440 | tf_op jit(solution)/shard_map/ppermute | solution.py:342
  81.0 10.9 %collective-permute-start.18 = (bf16[256,512]{1,0:T(8,128)(2,1)S(1)}, bf16[256,512]{1,0:T(8,128)(2,1)S(1)}, u32[]{:S(2)}, u32[]{:S(2)}) collective-permute-start(bf16[256,512]{1,0:T(8,128)(2,1)S(1)} %get-tuple-element.105.refs_6_), channel_id=1, source_target_pairs={{0,1},{1,0},{2,3},{3,2},{4,5},{5,4},{6,7},{7,6},{8,9},{9,8},{10,11... | collective-permute-start | bytes 786440 | tf_op jit(solution)/shard_map/ppermute | solution.py:429
  84.7 7.2 %collective-permute-start.19 = (bf16[256,512]{1,0:T(8,128)(2,1)S(1)}, bf16[256,512]{1,0:T(8,128)(2,1)S(1)}, u32[]{:S(2)}, u32[]{:S(2)}) collective-permute-start(bf16[256,512]{1,0:T(8,128)(2,1)S(1)} %get-tuple-element.106.refs_4_), channel_id=1, source_target_pairs={{1,2},{2,1},{5,6},{6,5},{9,10},{10,9},{13,14},{14,13},{17,18},{18,... | collective-permute-start | bytes 786440 | tf_op jit(solution)/shard_map/ppermute | solution.py:431
  85.3 10.8 %collective-permute-start.22 = (bf16[256,512]{1,0:T(8,128)(2,1)S(1)}, bf16[256,512]{1,0:T(8,128)(2,1)S(1)}, u32[]{:S(2)}, u32[]{:S(2)}) collective-permute-start(bf16[256,512]{1,0:T(8,128)(2,1)S(1)} %get-tuple-element.110.refs_5_), channel_id=1, source_target_pairs={{0,1},{1,0},{2,3},{3,2},{4,5},{5,4},{6,7},{7,6},{8,9},{9,8},{10,11... | collective-permute-start | bytes 786440 | tf_op jit(solution)/shard_map/ppermute | solution.py:429
  86.9 9.2 %collective-permute-start.23 = (bf16[256,512]{1,0:T(8,128)(2,1)S(1)}, bf16[256,512]{1,0:T(8,128)(2,1)S(1)}, u32[]{:S(2)}, u32[]{:S(2)}) collective-permute-start(bf16[256,512]{1,0:T(8,128)(2,1)S(1)} %get-tuple-element.111.refs_3_), channel_id=1, source_target_pairs={{1,2},{2,1},{5,6},{6,5},{9,10},{10,9},{13,14},{14,13},{17,18},{18,... | collective-permute-start | bytes 786440 | tf_op jit(solution)/shard_map/ppermute | solution.py:431
  97.9 27.6 %all-to-all-start.1 = ((bf16[4,64,2048]{2,1,0:T(8,128)(2,1)}), bf16[4,64,2048]{2,1,0:T(8,128)(2,1)}, u32[]{:S(2)}, u32[]{:S(2)}) async-start(bf16[4,64,2048]{2,1,0:T(8,128)(2,1)} %bitcast.33), calls=%async_computation.1 | async-start | bytes 2097152 | tf_op jit(solution)/shard_map/all_to_all | solution.py:345
  102.2 10.8 %collective-permute-start.20 = (bf16[256,512]{1,0:T(8,128)(2,1)S(1)}, bf16[256,512]{1,0:T(8,128)(2,1)S(1)}, u32[]{:S(2)}, u32[]{:S(2)}) collective-permute-start(bf16[256,512]{1,0:T(8,128)(2,1)S(1)} %get-tuple-element.108.refs_5_), channel_id=1, source_target_pairs={{0,1},{1,0},{2,3},{3,2},{4,5},{5,4},{6,7},{7,6},{8,9},{9,8},{10,11... | collective-permute-start | bytes 786440 | tf_op jit(solution)/shard_map/ppermute | solution.py:429
  105.9 7.1 %collective-permute-start.21 = (bf16[256,512]{1,0:T(8,128)(2,1)S(1)}, bf16[256,512]{1,0:T(8,128)(2,1)S(1)}, u32[]{:S(2)}, u32[]{:S(2)}) collective-permute-start(bf16[256,512]{1,0:T(8,128)(2,1)S(1)} %get-tuple-element.109.refs_3_), channel_id=1, source_target_pairs={{1,2},{2,1},{5,6},{6,5},{9,10},{10,9},{13,14},{14,13},{17,18},{18,... | collective-permute-start | bytes 786440 | tf_op jit(solution)/shard_map/ppermute | solution.py:431
  106.6 12.1 %collective-permute-start.26 = (bf16[256,512]{1,0:T(8,128)(2,1)S(1)}, bf16[256,512]{1,0:T(8,128)(2,1)S(1)}, u32[]{:S(2)}, u32[]{:S(2)}) collective-permute-start(bf16[256,512]{1,0:T(8,128)(2,1)S(1)} %get-tuple-element.116.refs_4_), channel_id=1, source_target_pairs={{0,1},{1,0},{2,3},{3,2},{4,5},{5,4},{6,7},{7,6},{8,9},{9,8},{10,11... | collective-permute-start | bytes 786440 | tf_op jit(solution)/shard_map/ppermute | solution.py:429
  108.2 10.4 %collective-permute-start.27 = (bf16[256,512]{1,0:T(8,128)(2,1)S(1)}, bf16[256,512]{1,0:T(8,128)(2,1)S(1)}, u32[]{:S(2)}, u32[]{:S(2)}) collective-permute-start(bf16[256,512]{1,0:T(8,128)(2,1)S(1)} %get-tuple-element.117.refs_2_), channel_id=1, source_target_pairs={{1,2},{2,1},{5,6},{6,5},{9,10},{10,9},{13,14},{14,13},{17,18},{18,... | collective-permute-start | bytes 786440 | tf_op jit(solution)/shard_map/ppermute | solution.py:431
  113.7 10.2 %collective-permute-start.24 = (bf16[256,512]{1,0:T(8,128)(2,1)S(1)}, bf16[256,512]{1,0:T(8,128)(2,1)S(1)}, u32[]{:S(2)}, u32[]{:S(2)}) collective-permute-start(bf16[256,512]{1,0:T(8,128)(2,1)S(1)} %get-tuple-element.114.refs_4_), channel_id=1, source_target_pairs={{0,1},{1,0},{2,3},{3,2},{4,5},{5,4},{6,7},{7,6},{8,9},{9,8},{10,11... | collective-permute-start | bytes 786440 | tf_op jit(solution)/shard_map/ppermute | solution.py:429
  117.7 6.3 %collective-permute-start.25 = (bf16[256,512]{1,0:T(8,128)(2,1)S(1)}, bf16[256,512]{1,0:T(8,128)(2,1)S(1)}, u32[]{:S(2)}, u32[]{:S(2)}) collective-permute-start(bf16[256,512]{1,0:T(8,128)(2,1)S(1)} %get-tuple-element.115.refs_2_), channel_id=1, source_target_pairs={{1,2},{2,1},{5,6},{6,5},{9,10},{10,9},{13,14},{14,13},{17,18},{18,... | collective-permute-start | bytes 786440 | tf_op jit(solution)/shard_map/ppermute | solution.py:431
  125.5 21.7 %all-to-all-start.3 = ((bf16[4,64,1536]{2,1,0:T(8,128)(2,1)}), bf16[4,64,1536]{2,1,0:T(8,128)(2,1)S(1)}, u32[]{:S(2)}, u32[]{:S(2)}) async-start(bf16[4,64,1536]{2,1,0:T(8,128)(2,1)} %bitcast.16), calls=%async_computation.3 | async-start | bytes 1572864 | tf_op jit(solution)/shard_map/all_to_all | solution.py:345
  129.0 10.8 %collective-permute-start.28 = (bf16[256,512]{1,0:T(8,128)(2,1)S(1)}, bf16[256,512]{1,0:T(8,128)(2,1)S(1)}, u32[]{:S(2)}, u32[]{:S(2)}) collective-permute-start(bf16[256,512]{1,0:T(8,128)(2,1)S(1)} %get-tuple-element.126.refs_2_), channel_id=1, source_target_pairs={{0,1},{1,0},{2,3},{3,2},{4,5},{5,4},{6,7},{7,6},{8,9},{9,8},{10,11... | collective-permute-start | bytes 786440 | tf_op jit(solution)/shard_map/ppermute | solution.py:429
  132.7 12.5 %collective-permute-start.29 = (bf16[256,512]{1,0:T(8,128)(2,1)S(1)}, bf16[256,512]{1,0:T(8,128)(2,1)S(1)}, u32[]{:S(2)}, u32[]{:S(2)}) collective-permute-start(bf16[256,512]{1,0:T(8,128)(2,1)S(1)} %get-tuple-element.129.refs_2_), channel_id=1, source_target_pairs={{0,1},{1,0},{2,3},{3,2},{4,5},{5,4},{6,7},{7,6},{8,9},{9,8},{10,11... | collective-permute-start | bytes 786440 | tf_op jit(solution)/shard_map/ppermute | solution.py:429
  147.2 12.3 %all-to-all-start.2 = ((bf16[4,64,1024]{2,1,0:T(8,128)(2,1)}), bf16[4,64,1024]{2,1,0:T(8,128)(2,1)S(1)}, u32[]{:S(2)}, u32[]{:S(2)}) async-start(bf16[4,64,1024]{2,1,0:T(8,128)(2,1)} %bitcast.14), calls=%async_computation.2 | async-start | bytes 1048576 | tf_op jit(solution)/shard_map/all_to_all | solution.py:345

commit v3 on v0

--- a/solution.py
+++ b/solution.py
@@ -1,14 +1,620 @@
 import jax
 import jax.numpy as jnp
 from jax import lax
+from jax.experimental import pallas as pl
+from jax.experimental.pallas import tpu as pltpu
 from jax.sharding import PartitionSpec as P
 
 DKV = 1024
 R = 64
 BLOCK = 128
+BF = jnp.bfloat16
+F32 = jnp.float32
+WHOLE = pl.BlockSpec(memory_space=pltpu.VMEM)
+SCALARS = pl.BlockSpec(memory_space=pltpu.SMEM)
+FAR = pl.BlockSpec(memory_space=pltpu.HBM)
+EDGE, UPPER, ODD, PLACE, DP_PLACE = range(5)
+(
+    PART, FROM_LINE, OLD_PART, INNER, OLD_INNER, FROM_INNER, LINE, OLD_LINE, FINAL, FINALS,
+    OLD_FINAL, WIDE, KEEP, SEND, SHRUNK_MINE, SHRUNK_THEIRS, KEPT, CAME, SLOT_ROWS,
+    HALF_MINE, HALF_THEIRS, D_OTHER, RANK, MARK,
+) = range(24)
+
+
+def launch(body, args, specs, outs, out_specs, scratch, mib, flops, moved, marks, grid=()):
+    n_in, n_args, n_outs = len(args) + len(marks), len(args), len(outs)
+
+    def kernel(*refs):
+        refs[n_in + n_outs][...] = jnp.zeros((8, 128), F32)
+        body(*refs[:n_args], *refs[n_in : n_in + n_outs], *refs[n_in + n_outs + 1 :])
+
+    return pl.pallas_call(
+        kernel,
+        grid=grid,
+        out_shape=[*outs, jax.ShapeDtypeStruct((8, 128), F32)],
+        in_specs=[*specs, *[pl.BlockSpec(memory_space=pl.ANY)] * len(marks)],
+        out_specs=[*out_specs, WHOLE],
+        scratch_shapes=scratch,
+        compiler_params=pltpu.CompilerParams(vmem_limit_bytes=mib * 1024 * 1024),
+        cost_estimate=pl.CostEstimate(flops=flops, bytes_accessed=moved, transcendentals=0),
+    )(*args, *marks)
+
+
+def back_call(flags, slot_rows, up_stack, out_grad, marks, pieces=4):
+    rows, cols = out_grad.shape
+    wide = up_stack.shape[0]
+    depth = rows // pieces
+
+    def body(flag_ref, slot_ref, up_ref, grad_ref, out_ref, held, sems):
+        copies = []
+        for p in range(pieces):
+            here = pl.ds(p * depth, depth)
+            copies.append(pltpu.make_async_copy(grad_ref.at[here, :], held.at[p], sems.at[p]))
+            copies[-1].start()
+        for p in range(pieces):
+            copies[p].wait()
+            here = slice(p * depth, (p + 1) * depth)
+            every = lax.dot_general(
+                up_ref[...], held[p], (((1,), (1,)), ((), ())), preferred_element_type=F32
+            )
+            rel = jnp.bitwise_xor(slot_ref[:, here], flag_ref[PLACE])
+            total = jnp.zeros((R, depth), F32)
+            for m in range(wide // R):
+                total += jnp.where(rel == m, every[m * R : (m + 1) * R], 0.0)
+            out_ref[:, here] = total
+
+    return launch(
+        body,
+        (flags, slot_rows, up_stack, out_grad),
+        (SCALARS, WHOLE, WHOLE, FAR),
+        (jax.ShapeDtypeStruct((R, rows), F32),),
+        (WHOLE,),
+        [pltpu.VMEM((pieces, depth, cols), BF), pltpu.SemaphoreType.DMA((pieces,))],
+        8,
+        2 * rows * cols * wide,
+        rows * cols * 2,
+        marks,
+    )
+
+
+def masked(slot, rank, count, lhs_ref):
+    for m in range(count):
+        lhs_ref[m * R : (m + 1) * R, :] = jnp.where(slot == m, rank, 0.0).astype(BF)
+
+
+def tile_copies(wide_ref, held, sems, start):
+    pieces, depth, width = held.shape
+    copies = [
+        pltpu.make_async_copy(
+            wide_ref.at[pl.ds(p * depth, depth), pl.ds(start, width)], held.at[p], sems.at[p]
+        )
+        for p in range(pieces)
+    ]
+    for copy in copies:
+        copy.start()
+    return copies
+
+
+def tile_dot(lhs_ref, held, copies):
+    pieces, depth, width = held.shape
+    total = jnp.zeros((lhs_ref.shape[0], width), F32)
+    for p in range(pieces):
+        copies[p].wait()
+        total += jnp.dot(
+            lhs_ref[:, p * depth : (p + 1) * depth], held[p], preferred_element_type=F32
+        )
+    return total.astype(BF)
+
+
+def tile_scratch(rows, width, pieces=4):
+    return [pltpu.VMEM((pieces, rows // pieces, width), BF), pltpu.SemaphoreType.DMA((pieces,))]
+
+
+def first_call(flags, slot_rows, mine, theirs, acts, count, width, marks):
+    rows = acts.shape[0]
+    half = rows // 2
+
+    def body(flag_ref, slot_ref, mine_ref, theirs_ref, acts_ref, out, lhs, d_own, d_half, held, sems):
+        copies = tile_copies(acts_ref, held, sems, 0)
+        rank = mine_ref[...] + theirs_ref[...]
+        d_own[...] = rank.astype(BF)
+        odd = flag_ref[ODD] == 1
+        d_half[...] = jnp.where(odd, rank[:, half:], rank[:, :half]).astype(BF)
+        masked(slot_ref[...], rank, count, lhs)
+        out[...] = tile_dot(lhs, held, copies)
+
+    return launch(
+        body,
+        (flags, slot_rows, mine, theirs, acts),
+        (SCALARS, WHOLE, WHOLE, WHOLE, FAR),
+        [
+            jax.ShapeDtypeStruct((count * R, width), BF),
+            jax.ShapeDtypeStruct((count * R, rows), BF),
+            jax.ShapeDtypeStruct((R, rows), BF),
+            jax.ShapeDtypeStruct((R, half), BF),
+        ],
+        [WHOLE] * 4,
+        tile_scratch(rows, width),
+        10,
+        2 * rows * count * R * width,
+        rows * width * 2,
+        marks,
+    )
+
+
+def tiles_call(lhs, acts, tiles, marks):
+    rows = acts.shape[0]
+    n = len(tiles)
+    total = sum(width for _, width in tiles)
+
+    def body(lhs_ref, acts_ref, *refs):
+        held, sems = refs[n::2], refs[n + 1 :: 2]
+        copies = [
+            tile_copies(acts_ref, held[i], sems[i], start) for i, (start, _) in enumerate(tiles)
+        ]
+        for i in range(n):
+            refs[i][...] = tile_dot(lhs_ref, held[i], copies[i])
+
+    return launch(
+        body,
+        (lhs, acts),
+        (WHOLE, FAR),
+        [jax.ShapeDtypeStruct((lhs.shape[0], width), BF) for _, width in tiles],
+        [WHOLE] * n,
+        [x for _, width in tiles for x in tile_scratch(rows, width)],
+        12,
+        2 * rows * lhs.shape[0] * total,
+        rows * total * 2,
+        marks,
+    )
+
+
+def place_call(position, firsts, seconds, start, total_rows, held):
+    width = sum(part[2] for part in firsts)
+    count = len(seconds[0][0])
+    flat, reads = [], []
+    for parts in (firsts, seconds):
+        reads.append([])
+        for arrays, offset, wide in parts:
+            listed = isinstance(arrays, list)
+            reads[-1].append((len(flat), listed, offset, wide))
+            flat += arrays if listed else [arrays]
+    extra = [] if held is None else [held]
+
+    def kernel(flag_ref, *refs):
+        out_ref, turned, sems = refs[-3:]
+
+        def read(parts, m, here):
+            got = []
+            for k, listed, offset, wide in parts:
+                cols = slice(offset, offset + wide)
+                got.append(refs[k + m][:, cols] if listed else refs[k][here, cols])
+            return jnp.concatenate(got, axis=1).astype(F32)
+
+        copies = []
+        for m in range(count):
+            sender = jnp.bitwise_xor(flag_ref[PLACE], m)
+            swapped = sender >= count // 2
+            here = pl.ds(pl.multiple_of(sender * R, R), R)
+            a, b = read(reads[0], m, here), read(reads[1], m, here)
+            turned[m, :, :] = jnp.concatenate(
+                [jnp.where(swapped, b, a), jnp.where(swapped, a, b)], axis=0
+            ).T.astype(BF)
+            row = pl.multiple_of(sender * (total_rows // count) + start, 128)
+            copies.append(
+                pltpu.make_async_copy(
+                    turned.at[m], out_ref.at[pl.ds(row, width), :], sems.at[m]
+                )
+            )
+            copies[-1].start()
+        for copy in copies:
+            copy.wait()
+
+    return pl.pallas_call(
+        kernel,
+        out_shape=jax.ShapeDtypeStruct((total_rows, 2 * R), BF),
+        in_specs=[SCALARS]
+        + [WHOLE] * len(flat)
+        + [pl.BlockSpec(memory_space=pl.ANY)] * len(extra),
+        out_specs=pl.BlockSpec(memory_space=pl.ANY),
+        scratch_shapes=[
+            pltpu.VMEM((count, width, 2 * R), BF),
+            pltpu.SemaphoreType.DMA((count,)),
+        ],
+        input_output_aliases={} if held is None else {1 + len(flat): 0},
+        compiler_params=pltpu.CompilerParams(vmem_limit_bytes=12 * 1024 * 1024),
+        cost_estimate=pl.CostEstimate(
+            flops=1, bytes_accessed=4 * count * width * 2 * R * 2, transcendentals=0
+        ),
+    )(position, *flat, *extra)
+
+
+def fold_call(pieces, groups, rows, marks):
+    width = pieces.shape[1]
+    per = pieces.shape[0] // groups // rows
+
+    def body(in_ref, out_ref):
+        for a in range(groups):
+            total = jnp.zeros((rows, width), F32)
+            for z in range(per):
+                start = (a * per + z) * rows
+                total += in_ref[start : start + rows, :].astype(F32)
+            out_ref[:, a * width : (a + 1) * width] = total.astype(BF)
+
+    return launch(
+        body,
+        (pieces,),
+        (WHOLE,),
+        [jax.ShapeDtypeStruct((rows, groups * width), BF)],
+        [WHOLE],
+        [],
+        6,
+        1,
+        pieces.size * 3,
+        marks,
+    )[0]
+
+
+def stack_call(flags, parts):
+    rows, width = parts[0].shape
+
+    def body(flag_ref, *refs):
+        for m in range(len(parts)):
+            place = jnp.bitwise_xor(flag_ref[DP_PLACE], m)
+            refs[-1][pl.ds(pl.multiple_of(place * rows, rows), rows), :] = refs[m][...]
+
+    return launch(
+        body,
+        (flags, *parts),
+        (SCALARS, *[WHOLE] * len(parts)),
+        [jax.ShapeDtypeStruct((rows * len(parts), width), BF)],
+        [WHOLE],
+        [],
+        6,
+        1,
+        rows * width * 16,
+        [],
+    )[0]
+
+
+def step_call(flags, arrays, outs, marks, count, start=None):
+    names = list(arrays)
+    out_names = list(outs)
+    rows = None
+    scratch = []
+    mib = 4
+    if start is not None:
+        wide = arrays[WIDE]
+        rows = wide.shape[0]
+        width = outs[PART][1]
+        scratch += tile_scratch(rows, width)
+        scratch.append(pltpu.VMEM((count * R, rows), BF))
+        mib += 7
+
+    def body(flag_ref, *refs):
+        got = dict(zip(names, refs[: len(names)]))
+        put = dict(zip(out_names, refs[len(names) :]))
+        rest = list(refs[len(names) + len(out_names) :])
+        edge = flag_ref[EDGE] == 1
+        inside = jnp.logical_not(edge)
+
+        def add(a, b):
+            return (got[a][...].astype(F32) + got[b][...].astype(F32)).astype(BF)
+
+        if start is not None:
+            held, sems = rest[:2]
+            rest = rest[2:]
+            copies = tile_copies(got[WIDE], held, sems, start)
+        if INNER in put:
+            put[INNER][...] = add(OLD_PART, FROM_LINE)
+        if FINAL in put or (FINAL, 0) in put or FINALS in put:
+
+            def finish(src):
+                if FINAL in put:
+                    put[FINAL][...] = src[...]
+                elif FINALS in put:
+                    first_width = got[OLD_FINAL].shape[1]
+                    put[FINALS][:, :first_width] = got[OLD_FINAL][...]
+                    put[FINALS][:, first_width:] = src[...]
+                else:
+                    for m in range(count):
+                        place = jnp.bitwise_xor(flag_ref[PLACE], m)
+                        here = pl.ds(pl.multiple_of(place * R, R), R)
+                        first_width = 0
+                        if OLD_FINAL in got:
+                            first_width = got[OLD_FINAL].shape[1]
+                            put[(FINAL, m)][:, :first_width] = got[OLD_FINAL][here, :]
+                        put[(FINAL, m)][:, first_width:] = src[here, :]
+
+            pl.when(edge)(lambda: finish(got[FROM_LINE]))
+            pl.when(inside)(lambda: finish(got[OLD_LINE]))
+        if KEEP in put:
+            upper = flag_ref[UPPER] == 1
+            key = got[SHRUNK_MINE][:R] + got[SHRUNK_THEIRS][:R]
+            value = got[SHRUNK_MINE][R:] + got[SHRUNK_THEIRS][R:]
+            put[KEEP][...] = jnp.where(upper, value, key)
+            put[SEND][...] = jnp.where(upper, key, value).astype(BF)
+        if start is not None:
+            lhs = rest[0]
+            if HALF_MINE in got:
+                odd = flag_ref[ODD] == 1
+                a, b = got[HALF_MINE][...].astype(F32), got[HALF_THEIRS][...].astype(F32)
+                rank = jnp.concatenate([jnp.where(odd, b, a), jnp.where(odd, a, b)], axis=1)
+                put[D_OTHER][...] = rank.astype(BF)
+            elif KEPT in got:
+                rank = got[KEPT][...] + got[CAME][...].astype(F32)
+            else:
+                rank = got[RANK][...].astype(F32)
+            masked(got[SLOT_ROWS][...], rank, count, lhs)
+            put[PART][...] = tile_dot(lhs, held, copies)
+        if LINE in put:
+            if OLD_INNER in got and (PART in got or start is not None):
+                part = got[PART] if PART in got else put[PART]
+
+                @pl.when(edge)
+                def _():
+                    put[LINE][...] = part[...]
+
+                @pl.when(inside)
+                def _():
+                    put[LINE][...] = add(OLD_INNER, FROM_INNER)
+
+            elif OLD_INNER in got:
+                put[LINE][...] = add(OLD_INNER, FROM_INNER)
+            else:
+                put[LINE][...] = got.get(PART, put.get(PART))[...]
+    made = launch(
+        body,
+        (flags, *arrays.values()),
+        (SCALARS, *[FAR if k == WIDE else WHOLE for k in names]),
+        [
+            jax.ShapeDtypeStruct(shape, F32 if k == KEEP else BF)
+            for k, shape in outs.items()
+        ],
+        [WHOLE] * len(outs),
+        scratch,
+        mib,
+        15 * 10**9 if FROM_LINE in names else 1,
+        24 * 10**6,
+        marks,
+    )
+    return dict(zip([*out_names, MARK], made))
+
+
+def shrink_call(slot, pool, acts, marks, per=4):
+    rows, width = acts.shape
+
+    def body(slot_ref, pool_ref, acts_ref, out_ref):
+        i = pl.program_id(0)
+        for b in range(per):
+            here = slice(b * BLOCK, (b + 1) * BLOCK)
+            part = jnp.dot(
+                acts_ref[here, :], pool_ref[slot_ref[i * per + b]], preferred_element_type=F32
+            )
+            out_ref[:, here] = part.T
+
+    return launch(
+        body,
+        (slot, pool, acts),
+        (SCALARS, WHOLE, pl.BlockSpec((per * BLOCK, width), lambda i: (i, 0))),
+        (jax.ShapeDtypeStruct((2 * R, rows), F32),),
+        (pl.BlockSpec((2 * R, per * BLOCK), lambda i: (0, i)),),
+        [],
+        12,
+        4 * rows * width * 2 * R,
+        rows * width * 2,
+        marks,
+        (rows // (BLOCK * per),),
+    )
+
+
+def expand_call(flags, slot, pools, own, other, width, marks, per=4):
+    rows = own.shape[1]
+
+    def body(flag_ref, slot_ref, *refs):
+        pool_refs = refs[: len(pools)]
+        own_ref, other_ref, out_ref = refs[len(pools) :]
+        i = pl.program_id(0)
+        upper = flag_ref[UPPER] == 1
+        for b in range(per):
+            here = slice(b * BLOCK, (b + 1) * BLOCK)
+            mine, theirs = own_ref[:, here].astype(F32), other_ref[:, here].astype(F32)
+            rank = jnp.concatenate(
+                [jnp.where(upper, theirs, mine), jnp.where(upper, mine, theirs)], axis=0
+            )
+            turned = rank.T.astype(BF)
+            first = 0
+            for pool_ref in pool_refs:
+                depth = pool_ref.shape[1]
+                out_ref[here, first : first + depth] = lax.dot_general(
+                    turned,
+                    pool_ref[slot_ref[i * per + b]],
+                    (((1,), (1,)), ((), ())),
+                    preferred_element_type=F32,
+                ).astype(BF)
+                first += depth
+
+    return launch(
+        body,
+        (flags, slot, *pools, own, other),
+        (
+            SCALARS,
+            SCALARS,
+            *[WHOLE] * len(pools),
+            pl.BlockSpec((R, per * BLOCK), lambda i: (0, i)),
+            pl.BlockSpec((R, per * BLOCK), lambda i: (0, i)),
+        ),
+        (pltpu.HBM((rows, width), BF),),
+        (pl.BlockSpec((per * BLOCK, width), lambda i: (i, 0)),),
+        [],
+        12,
+        4 * rows * width * 2 * R,
+        rows * width * 2,
+        marks,
+        (rows // (BLOCK * per),),
+    )
 
 
 def local(acts, out_grad, tenant_ids, slot_map, down_pool, up_pool):
+    acts = pltpu.with_memory_space_constraint(acts, pltpu.HBM)
+    out_grad = pltpu.with_memory_space_constraint(out_grad, pltpu.HBM)
+    count = lax.axis_size("adapter")
+    j = lax.axis_index("adapter")
+    z = lax.axis_index("dp")
+    rows, width = acts.shape
+    cols = out_grad.shape[1]
+    total_rows = down_pool.shape[1]
+    edge = (z == 0) | (z == 3)
+    flags = jnp.stack([edge.astype(jnp.int32), j // (count // 2), j % 2, j, z]).astype(jnp.int32)
+
+    def swap(x, m):
+        return lax.ppermute(x, "adapter", [(i, i ^ m) for i in range(count)])
+
+    def to_owner(x):
+        return lax.all_to_all(x, "adapter", split_axis=0, concat_axis=0, tiled=True)
+
+    slot = slot_map[tenant_ids[:, 0]].astype(jnp.int32)
+    slot_rows = jnp.repeat(slot, BLOCK)[None, :]
+
+    def up_piece(m):
+        return lax.dynamic_slice(up_pool[0], (0, (j ^ m) * cols), (R, cols))
+
+    ups = [up_piece(0)] + [swap(up_piece(m), m) for m in range(1, count)]
+    back_part, mark = back_call(flags, slot_rows, jnp.concatenate(ups, axis=0), out_grad, [])
+    back_peer = swap(back_part, 1)
+
+    unit = width // 16
+    sizes = [5 * unit, 5 * unit, 6 * unit, 6 * unit, 5 * unit, 5 * unit]
+    n = len(sizes)
+    per_kind = n // 2
+    starts = [sum(sizes[:c]) % width for c in range(n)]
+    tenants = count * R
+    parts, line, inner, from_line, from_inner, final = {}, {}, {}, {}, {}, {}
+    parts[0], lhs_own, d_own, d_half, mark = first_call(
+        flags, slot_rows, back_part, back_peer, acts, count, sizes[0], []
+    )
+    came_half = swap(d_half, 2)
+    came_other = swap(came_half, 1)
+    tiles = [(starts[c], sizes[c]) for c in range(1, per_kind)]
+    *more, mark = tiles_call(lhs_own, acts, tiles, [mark])
+    for c in range(1, per_kind):
+        parts[c] = more[c - 1]
+
+    for t in range(n + 6):
+        if t < 2:
+            line[t] = parts[t]
+        else:
+            arrays, outs, start = {}, {}, None
+            if t < n and t in parts:
+                arrays[PART] = parts[t]
+            elif t < n:
+                start = starts[t]
+                arrays[WIDE], arrays[SLOT_ROWS] = acts, slot_rows
+                outs[PART] = (tenants, sizes[t])
+                if t == per_kind:
+                    arrays[HALF_MINE], arrays[HALF_THEIRS] = came_half, came_other
+                    outs[D_OTHER] = (R, rows)
+                else:
+                    arrays[RANK] = d_other
+            arrays[FROM_LINE] = from_line[t - 2]
+            if t - 2 < n:
+                arrays[OLD_PART] = parts[t - 2]
+                outs[INNER] = (tenants, sizes[t - 2])
+            if 0 <= t - 4 < n:
+                arrays[OLD_INNER] = inner[t - 2]
+                arrays[FROM_INNER] = from_inner[t - 2]
+            if t < n or 0 <= t - 4 < n:
+                outs[LINE] = (tenants, sizes[t] if t < n else sizes[t - 4])
+            if t >= 6:
+                arrays[OLD_LINE] = line[t - 2]
+                c = t - 6
+                if c in (0, per_kind - 1):
+                    outs[FINAL] = (tenants, sizes[c])
+                elif c == n - 1:
+                    outs.update({(FINAL, m): (R, sizes[c]) for m in range(count)})
+                else:
+                    arrays[OLD_FINAL] = final[c - 1]
+                    wide_now = final[c - 1].shape[1] + sizes[c]
+                    if c == n - 2:
+                        outs.update({(FINAL, m): (R, wide_now) for m in range(count)})
+                    else:
+                        outs[FINALS] = (tenants, wide_now)
+            if t == 8:
+                arrays[SHRUNK_MINE], arrays[SHRUNK_THEIRS] = shrunk_part, swap(shrunk_part, 1)
+                outs[KEEP] = outs[SEND] = (R, rows)
+            marks = [mark]
+            if t == 10:
+                late = {WIDE: out_grad, KEPT: keep, CAME: came_shrunk, SLOT_ROWS: slot_rows}
+                made = step_call(flags, late, {PART: (tenants, cols)}, [mark], count, 0)
+                up, mark = made[PART], made[MARK]
+                marks = [mark, own]
+                up_pieces = lax.all_to_all(
+                    up, ("adapter", "dp"), split_axis=0, concat_axis=0, tiled=True
+                )
+            if t == 6:
+                shrunk_part, mark = shrink_call(slot, pools[0], acts, [mark])
+                marks = [mark]
+            made = step_call(flags, arrays, outs, marks, count, start)
+            mark = made[MARK]
+            if t == 2:
+                pool_in, _ = lax.optimization_barrier((down_pool[0], mark))
+                pool = to_owner(pool_in).reshape(count, width, 2 * R)
+                pools = [pltpu.with_memory_space_constraint(pool, pltpu.HBM)]
+            if PART in made and t < n:
+                parts[t] = made[PART]
+            if t == per_kind:
+                d_other = made[D_OTHER]
+            if INNER in made:
+                inner[t] = made[INNER]
+            if LINE in made:
+                line[t] = made[LINE]
+            if FINAL in made:
+                final[t - 6] = made[FINAL]
+            if FINALS in made:
+                final[t - 6] = made[FINALS]
+            if t == 7:
+                own = to_owner(made[FINALS])
+            if (FINAL, 0) in made:
+                final[t - 6] = [made[(FINAL, 0)]] + [
+                    swap(made[(FINAL, m)], m) for m in range(1, count)
+                ]
+            if t == 8:
+                keep, came_shrunk = made[KEEP], swap(made[SEND], 2)
+        if t in line and t < n + 4:
+            from_line[t] = lax.ppermute(line[t], "dp", [(0, 1), (1, 0), (2, 3), (3, 2)])
+        if t in inner:
+            from_inner[t] = lax.ppermute(inner[t], "dp", [(1, 2), (2, 1)])
+
+    acts_grad, mark = expand_call(flags, slot, pools, d_own, d_other, width, [mark])
+    dp = lax.axis_size("dp")
+    up_rows = fold_call(up_pieces, count, R // dp, [mark])
+    up_parts = [up_rows] + [
+        lax.ppermute(up_rows, "dp", [(i, i ^ m) for i in range(dp)]) for m in range(1, dp)
+    ]
+    up_grad = stack_call(flags, up_parts)
+    down_grad = None
+    mixed, last = final[n - 2], final[n - 1]
+    joint, rest, split = sizes[0] + sizes[1], sizes[2], width - sizes[n - 1]
+    down_grad = place_call(
+        flags,
+        [(own, 0, joint), (mixed, 0, split - joint)],
+        [(mixed, rest, split)],
+        0,
+        total_rows,
+        None,
+    )
+    down_grad = place_call(
+        flags,
+        [(mixed, split - joint, width - split)],
+        [(last, 0, width - split)],
+        split,
+        total_rows,
+        down_grad,
+    )
+    return acts_grad, down_grad[None], up_grad[None]
+
+
+def local_any(acts, out_grad, tenant_ids, slot_map, down_pool, up_pool):
     position = lax.axis_index("adapter")
     row_count, local_width = acts.shape
     col_count = out_grad.shape[1]
@@ -62,8 +668,9 @@
 
 
 def solution(mesh):
+    line_of_four = mesh.shape["adapter"] == 4 and mesh.shape["dp"] == 4
     return jax.shard_map(
-        local,
+        local if line_of_four else local_any,
         mesh=mesh,
         in_specs=(
             P(("groups", "dp"), "adapter"),

time: 445 us -> 138 us (0.31)
  blocking collectives: 208 us -> 0 us
  other arithmetic: 59.9 us -> 0.68 us
  Pallas kernels: 0 us -> 53.2 us
  local copies, waits for them, and re-layouts: 56.4 us -> 7.42 us
  matrix products: 43.1 us -> 0 us
  waiting for transfers between devices: 58.6 us -> 19.1 us
  starting transfers between devices: 17.4 us -> 55.2 us
    psum x2 -> x0, blocking collectives: 208 us -> none  [the longest x1 167 us: local(): total_down, total_up = lax.psum((owned_down, owned_up), 'dp')]
    unnamed x2 -> x0, other arithmetic: 58.8 us -> none
    all_to_all x4 -> x3, waiting for transfers between devices: 58.6 us -> 0.01 us  [the longest x2 0.01 us: to_owner(): return lax.all_to_all(x, 'adapter', split_axis=0, concat_axis=0, tiled=True)]
    pallas_call x0 -> x20, Pallas kernels: none -> 53.2 us  [the longest x18 49.7 us: launch(): pl.pallas_call(kernel, grid=grid, out_shape=[*outs, jax.ShapeDtypeStruct(...]
    dot_general x7 -> x0, matrix products: 43.1 us -> none  [the longest x1 11.4 us: local(): jnp.einsum('bnd,bnr->bdr', acts_blocks, d_shrunk, preferred_element_type=...]
    ppermute x0 -> x33, starting transfers between devices: none -> 42.1 us  [the longest x10 21 us: local(): from_line[t] = lax.ppermute(line[t], 'dp', [(0, 1), (1, 0), (2, 3), (3, 2)])]
    unnamed x19 -> x30, local copies, waits for them, and re-layouts: 26.7 us -> 5.65 us
    dot_general x3 -> x0, local copies, waits for them, and re-layouts: 20.9 us -> none  [the longest x1 17.7 us: local(): jnp.einsum('bnd,bnr->bdr', acts_blocks, d_shrunk, preferred_element_type=...]
  transfers between devices with their start and end apart: 4 -> 36, of which waited for: 2 -> 11; matrix products, arithmetic and copies ran while one was open for 26% -> 1% of each run, Pallas kernels for 0% -> 33%
where the time goes in v3:
time: 138 us; the launch traced here: 137 us
  starting transfers between devices  55.2 us (40%)
  Pallas kernels  53.2 us (39%)
  waiting for transfers between devices  19.1 us (14%)
  local copies, waits for them, and re-layouts  7.42 us (5%)
    pallas_call x18, Pallas kernels, launch(): pl.pallas_call(kernel, grid=grid, out_shape=[*outs, jax.ShapeDtypeStruct(...  49.7 us
    ppermute x10, starting transfers between devices, local(): from_line[t] = lax.ppermute(line[t], 'dp', [(0, 1), (1, 0), (2, 3), (3, 2)])  21 us
    ppermute x10, waiting for transfers between devices, local(): from_line[t] = lax.ppermute(line[t], 'dp', [(0, 1), (1, 0), (2, 3), (3, 2)])  11.9 us
    ppermute x14, starting transfers between devices, swap(): return lax.ppermute(x, 'adapter', [(i, i ^ m) for i in range(count)])  11 us
    all_to_all x2, starting transfers between devices, to_owner(): return lax.all_to_all(x, 'adapter', split_axis=0, concat_axis=0, tiled=True)  8.2 us
    ppermute x14, waiting for transfers between devices, swap(): return lax.ppermute(x, 'adapter', [(i, i ^ m) for i in range(count)])  6.19 us
    unnamed x30, local copies, waits for them, and re-layouts  5.65 us
    ppermute x6, starting transfers between devices, local(): from_inner[t] = lax.ppermute(inner[t], 'dp', [(1, 2), (2, 1)])  5.52 us
  transfers between devices with their start and end apart: 36, of which 11 were waited for; matrix products, arithmetic and copies ran while one was open for 1% of the time, Pallas kernels for 33%

profile of v3, /device:TPU:0, one launch (start us, length us, event | category | flops | bytes accessed | tf_op | source)
XLA Modules:
  0.0 136.7 jit_solution(17789225905736519133)
XLA Ops:
  0.7 1.0 dynamic-slice_bitcast_fusion.3
  2.2 2.6 %collective-permute-start.2 = (bf16[64,512]{1,0:T(8,128)(2,1)S(1)}, bf16[64,512]{1,0:T(8,128)(2,1)S(1)}, u32[]{:S(2)}, u32[]{:S(2)}) collective-permute-start(bf16[64,512]{1,0:T(8,128)(2,1)S(1)} %get-tuple-element.125), channel_id=1, source_target_pairs={{0,12},{4,8},{8,4},{12,0},{1,13},{5,9},{9,5},{13,1},{2,14},{6,10},... | collective-permute-start | bytes 196616 | tf_op jit(solution)/shard_map/ppermute | solution.py:471
  6.3 1.0 collective-permute-done.2
  7.2 1.8 %collective-permute-done.1 = bf16[64,512]{1,0:T(8,128)(2,1)S(1)} collective-permute-done((bf16[64,512]{1,0:T(8,128)(2,1)S(1)}, bf16[64,512]{1,0:T(8,128)(2,1)S(1)}, u32[]{:S(2)}, u32[]{:S(2)}) %collective-permute-start.1) | collective-permute-done | bytes 65568 | tf_op jit(solution)/shard_map/ppermute | solution.py:471
  9.2 3.2 %shard_map.85 = (f32[64,2048]{1,0:T(8,128)S(1)}, f32[8,128]{1,0:T(8,128)}) custom-call(s32[5]{0:T(128)S(1)} %stack.27.refs_0_.flag_ref, s32[1,2048]{1,0:T(1,128)S(1)} %bitcast.27, bf16[256,512]{1,0:T(8,128)(2,1)S(1)} %pad_maximum_fusion.refs_2_, bf16[2048,512]{1,0:T(8,128)(2,1)} %refs_1_.9), custom_call_target="tpu_custom_call" | custom-call | flops 536870912 | bytes 2097152 | tf_op jit(solution)/shard_map/pallas_call | solution.py:31
  12.5 1.9 %collective-permute-done.3.refs_3_ = f32[64,2048]{1,0:T(8,128)S(1)} collective-permute-done((f32[64,2048]{1,0:T(8,128)S(1)}, f32[64,2048]{1,0:T(8,128)S(1)}, u32[]{:S(2)}, u32[]{:S(2)}) %collective-permute-start.3) | collective-permute-done | bytes 524320 | tf_op jit(solution)/shard_map/ppermute | solution.py:471
  14.4 3.2 %shard_map.86 = (bf16[256,640]{1,0:T(8,128)(2,1)S(1)}, bf16[256,2048]{1,0:T(8,128)(2,1)S(1)}, bf16[64,2048]{1,0:T(8,128)(2,1)S(1)}, bf16[64,1024]{1,0:T(8,128)(2,1)S(1)}, f32[8,128]{1,0:T(8,128)S(1)}) custom-call(s32[5]{0:T(128)S(1)} %stack.27.refs_0_.flag_ref, s32[1,2048]{1,0:T(1,128)S(1)} %bitcast.28, f32[64,2048]{1,0:T(8,128)S(1)} %get-tuple-element.63.refs_2_, ...), custom_call_target="tpu_custom_call" | custom-call | flops 671088640 | bytes 2621440 | tf_op jit(solution)/shard_map/pallas_call | solution.py:31
  18.3 1.6 %collective-permute-start.4 = (bf16[256,640]{1,0:T(8,128)(2,1)S(1)}, bf16[256,640]{1,0:T(8,128)(2,1)S(1)}, u32[]{:S(2)}, u32[]{:S(2)}) collective-permute-start(bf16[256,640]{1,0:T(8,128)(2,1)S(1)} %get-tuple-element.67.refs_3_), channel_id=1, source_target_pairs={{0,1},{1,0},{2,3},{3,2},{4,5},{5,4},{6,7},{7,6},{8,9},{9,8},{10,11... | collective-permute-start | bytes 983048 | tf_op jit(solution)/shard_map/ppermute | solution.py:584
  19.9 1.5 %collective-permute-start.5 = (bf16[64,1024]{1,0:T(8,128)(2,1)S(1)}, bf16[64,1024]{1,0:T(8,128)(2,1)S(1)}, u32[]{:S(2)}, u32[]{:S(2)}) collective-permute-start(bf16[64,1024]{1,0:T(8,128)(2,1)S(1)} %get-tuple-element.72), channel_id=1, source_target_pairs={{0,8},{4,12},{8,0},{12,4},{1,9},{5,13},{9,1},{13,5},{2,10},{6,14},... | collective-permute-start | bytes 393224 | tf_op jit(solution)/shard_map/ppermute | solution.py:471
  21.3 4.5 %shard_map.87 = (bf16[256,640]{1,0:T(8,128)(2,1)S(1)}, bf16[256,768]{1,0:T(8,128)(2,1)S(1)}, f32[8,128]{1,0:T(8,128)S(1)}) custom-call(bf16[256,2048]{1,0:T(8,128)(2,1)S(1)} %get-tuple-element.64.refs_0_, bf16[2048,2048]{1,0:T(8,128)(2,1)} %refs_2_.1, f32[8,128]{1,0:T(8,128)S(1)} %get-tuple-element.65.refs_2_), custom_call_target="tpu_custom_call" | custom-call | flops 1476395008 | bytes 5767168 | tf_op jit(solution)/shard_map/pallas_call | solution.py:31
  26.3 1.7 %collective-permute-done.4.refs_2_ = bf16[256,640]{1,0:T(8,128)(2,1)S(1)} collective-permute-done((bf16[256,640]{1,0:T(8,128)(2,1)S(1)}, bf16[256,640]{1,0:T(8,128)(2,1)S(1)}, u32[]{:S(2)}, u32[]{:S(2)}) %collective-permute-start.4) | collective-permute-done | bytes 327712 | tf_op jit(solution)/shard_map/ppermute | solution.py:584
  28.7 4.5 %all-to-all-start = ((bf16[4,2048,128]{2,1,0:T(8,128)(2,1)}), bf16[4,2048,128]{2,1,0:T(8,128)(2,1)}, u32[]{:S(2)}, u32[]{:S(2)}) async-start(bf16[4,2048,128]{2,1,0:T(8,128)(2,1)} %bitcast.34), calls=%async_computation | async-start | bytes 4194304 | tf_op jit(solution)/shard_map/all_to_all | solution.py:474
  33.8 4.4 %collective-permute-start.10 = (bf16[256,768]{1,0:T(8,128)(2,1)S(1)}, bf16[256,768]{1,0:T(8,128)(2,1)S(1)}, u32[]{:S(2)}, u32[]{:S(2)}) collective-permute-start(bf16[256,768]{1,0:T(8,128)(2,1)S(1)} %get-tuple-element.78), channel_id=1, source_target_pairs={{0,1},{1,0},{2,3},{3,2},{4,5},{5,4},{6,7},{7,6},{8,9},{9,8},{10,11... | collective-permute-start | bytes 1179656 | tf_op jit(solution)/shard_map/ppermute | solution.py:584
  38.3 3.3 %shard_map.89 = (bf16[256,768]{1,0:T(8,128)(2,1)S(1)}, bf16[64,2048]{1,0:T(8,128)(2,1)S(1)}, bf16[256,640]{1,0:T(8,128)(2,1)S(1)}, bf16[256,768]{1,0:T(8,128)(2,1)S(1)}, f32[8,128]{1,0:T(8,128)S(1)}) custom-call(s32[5]{0:T(128)S(1)} %stack.27.refs_0_.flag_ref, bf16[2048,2048]{1,0:T(8,128)(2,1)} %refs_2_.1, s32[1,2048]{1,0:T(1,128)S(1)} %bitcast.29, ...), custom_call_target="tpu_custom_call" | custom-call | flops 15000000512 | bytes 24000000 | tf_op jit(solution)/shard_map/pallas_call | solution.py:31
  42.3 2.6 %collective-permute-start.8 = (bf16[256,768]{1,0:T(8,128)(2,1)S(1)}, bf16[256,768]{1,0:T(8,128)(2,1)S(1)}, u32[]{:S(2)}, u32[]{:S(2)}) collective-permute-start(bf16[256,768]{1,0:T(8,128)(2,1)S(1)} %get-tuple-element.75), channel_id=1, source_target_pairs={{0,1},{1,0},{2,3},{3,2},{4,5},{5,4},{6,7},{7,6},{8,9},{9,8},{10,11... | collective-permute-start | bytes 1179656 | tf_op jit(solution)/shard_map/ppermute | solution.py:584
  44.9 3.3 %collective-permute-done.10.refs_4_ = bf16[256,768]{1,0:T(8,128)(2,1)S(1)} collective-permute-done((bf16[256,768]{1,0:T(8,128)(2,1)S(1)}, bf16[256,768]{1,0:T(8,128)(2,1)S(1)}, u32[]{:S(2)}, u32[]{:S(2)}) %collective-permute-start.10) | collective-permute-done | bytes 393248 | tf_op jit(solution)/shard_map/ppermute | solution.py:584
  48.2 3.9 %shard_map.90 = (bf16[256,640]{1,0:T(8,128)(2,1)S(1)}, bf16[256,768]{1,0:T(8,128)(2,1)S(1)}, bf16[256,640]{1,0:T(8,128)(2,1)}, f32[8,128]{1,0:T(8,128)S(1)}) custom-call(s32[5]{0:T(128)S(1)} %stack.27.refs_0_.flag_ref, bf16[2048,2048]{1,0:T(8,128)(2,1)} %refs_2_.1, s32[1,2048]{1,0:T(1,128)S(1)} %bitcast.30, ...), custom_call_target="tpu_custom_call" | custom-call | flops 15000000512 | bytes 24000000 | tf_op jit(solution)/shard_map/pallas_call | solution.py:31
  52.9 2.1 %collective-permute-start.14 = (bf16[256,640]{1,0:T(8,128)(2,1)}, bf16[256,640]{1,0:T(8,128)(2,1)}, u32[]{:S(2)}, u32[]{:S(2)}) collective-permute-start(bf16[256,640]{1,0:T(8,128)(2,1)} %get-tuple-element.85.refs_5_), channel_id=1, source_target_pairs={{0,1},{1,0},{2,3},{3,2},{4,5},{5,4},{6,7},{7,6},{8,9},{9,8},{10,11... | collective-permute-start | bytes 983048 | tf_op jit(solution)/shard_map/ppermute | solution.py:584
  55.7 0.9 collective-permute-done.8.refs_4_
  56.6 3.9 %shard_map.91 = (bf16[256,640]{1,0:T(8,128)(2,1)S(1)}, bf16[256,768]{1,0:T(8,128)(2,1)S(1)}, bf16[256,640]{1,0:T(8,128)(2,1)}, f32[8,128]{1,0:T(8,128)S(1)}) custom-call(s32[5]{0:T(128)S(1)} %stack.27.refs_0_.flag_ref, bf16[2048,2048]{1,0:T(8,128)(2,1)} %refs_2_.1, s32[1,2048]{1,0:T(1,128)S(1)} %bitcast.31, ...), custom_call_target="tpu_custom_call" | custom-call | flops 15000000512 | bytes 24000000 | tf_op jit(solution)/shard_map/pallas_call | solution.py:31
  61.3 2.1 %collective-permute-start.12 = (bf16[256,640]{1,0:T(8,128)(2,1)}, bf16[256,640]{1,0:T(8,128)(2,1)}, u32[]{:S(2)}, u32[]{:S(2)}) collective-permute-start(bf16[256,640]{1,0:T(8,128)(2,1)} %get-tuple-element.82.refs_5_), channel_id=1, source_target_pairs={{0,1},{1,0},{2,3},{3,2},{4,5},{5,4},{6,7},{7,6},{8,9},{9,8},{10,11... | collective-permute-start | bytes 983048 | tf_op jit(solution)/shard_map/ppermute | solution.py:584
  63.4 1.4 %collective-permute-start.13 = (bf16[256,768]{1,0:T(8,128)(2,1)S(1)}, bf16[256,768]{1,0:T(8,128)(2,1)}, u32[]{:S(2)}, u32[]{:S(2)}) collective-permute-start(bf16[256,768]{1,0:T(8,128)(2,1)S(1)} %get-tuple-element.84.refs_3_), channel_id=1, source_target_pairs={{1,2},{2,1},{5,6},{6,5},{9,10},{10,9},{13,14},{14,13},{17,18},{18,... | collective-permute-start | bytes 1179656 | tf_op jit(solution)/shard_map/ppermute | solution.py:586
  64.8 6.5 %shard_map.92 = (f32[128,2048]{1,0:T(8,128)S(1)}, f32[8,128]{1,0:T(8,128)S(1)}) custom-call(s32[16]{0:T(128)S(1)} %gather_fusion, bf16[4,2048,128]{2,1,0:T(8,128)(2,1)} %all-to-all-done.refs_1_.refs_2_, bf16[2048,2048]{1,0:T(8,128)(2,1)} %refs_2_.1, f32[8,128]{1,0:T(8,128)S(1)} %get-tuple-element.88.refs_3_), custom_call_target="tpu_custom_call" | custom-call | flops 2147483648 | bytes 8388608 | tf_op jit(solution)/shard_map/pallas_call | solution.py:31
  71.4 1.3 shard_map.93
  72.7 1.4 %collective-permute-start.19 = (bf16[256,640]{1,0:T(8,128)(2,1)S(1)}, bf16[256,640]{1,0:T(8,128)(2,1)}, u32[]{:S(2)}, u32[]{:S(2)}) collective-permute-start(bf16[256,640]{1,0:T(8,128)(2,1)S(1)} %get-tuple-element.95.refs_2_), channel_id=1, source_target_pairs={{1,2},{2,1},{5,6},{6,5},{9,10},{10,9},{13,14},{14,13},{17,18},{18,... | collective-permute-start | bytes 983048 | tf_op jit(solution)/shard_map/ppermute | solution.py:586
  74.1 3.1 %collective-permute-start.18 = (bf16[256,768]{1,0:T(8,128)(2,1)S(1)}, bf16[256,768]{1,0:T(8,128)(2,1)}, u32[]{:S(2)}, u32[]{:S(2)}) collective-permute-start(bf16[256,768]{1,0:T(8,128)(2,1)S(1)} %get-tuple-element.94.refs_4_), channel_id=1, source_target_pairs={{0,1},{1,0},{2,3},{3,2},{4,5},{5,4},{6,7},{7,6},{8,9},{9,8},{10,11... | collective-permute-start | bytes 1179656 | tf_op jit(solution)/shard_map/ppermute | solution.py:584
  77.3 2.2 %shard_map.94 = (bf16[256,640]{1,0:T(8,128)(2,1)S(1)}, bf16[256,768]{1,0:T(8,128)(2,1)S(1)}, bf16[256,1280]{1,0:T(8,128)(2,1)}, f32[8,128]{1,0:T(8,128)S(1)}) custom-call(s32[5]{0:T(128)S(1)} %stack.27.refs_0_.flag_ref, bf16[256,640]{1,0:T(8,128)(2,1)} %collective-permute-done.12.refs_1_, bf16[256,640]{1,0:T(8,128)(2,1)S(1)} %copy-done.12, ...), custom_call_target="tpu_custom_call" | custom-call | flops 15000000512 | bytes 24000000 | tf_op jit(solution)/shard_map/pallas_call | solution.py:31
  80.9 3.7 %all-to-all-start.1 = ((bf16[4,64,1280]{2,1,0:T(8,128)(2,1)}), bf16[4,64,1280]{2,1,0:T(8,128)(2,1)S(1)}, u32[]{:S(2)}, u32[]{:S(2)}) async-start(bf16[4,64,1280]{2,1,0:T(8,128)(2,1)} %bitcast.13), calls=%async_computation.1 | async-start | bytes 1310720 | tf_op jit(solution)/shard_map/all_to_all | solution.py:474
  85.3 2.4 %collective-permute-start.16 = (bf16[256,768]{1,0:T(8,128)(2,1)}, bf16[256,768]{1,0:T(8,128)(2,1)S(1)}, u32[]{:S(2)}, u32[]{:S(2)}) collective-permute-start(bf16[256,768]{1,0:T(8,128)(2,1)} %copy-done.1), channel_id=1, source_target_pairs={{0,1},{1,0},{2,3},{3,2},{4,5},{5,4},{6,7},{7,6},{8,9},{9,8},{10,11... | collective-permute-start | bytes 1179656 | tf_op jit(solution)/shard_map/ppermute | solution.py:584
  87.8 2.1 %shard_map.95 = (bf16[256,640]{1,0:T(8,128)(2,1)}, bf16[256,768]{1,0:T(8,128)(2,1)S(1)}, f32[64,2048]{1,0:T(8,128)S(1)}, bf16[64,2048]{1,0:T(8,128)(2,1)S(1)}, f32[8,128]{1,0:T(8,128)S(1)}) custom-call(s32[5]{0:T(128)S(1)} %stack.27.refs_0_.flag_ref, bf16[256,768]{1,0:T(8,128)(2,1)} %collective-permute-done.18.refs_1_, ...), custom_call_target="tpu_custom_call" | custom-call | flops 15000000512 | bytes 24000000 | tf_op jit(solution)/shard_map/pallas_call | solution.py:31
  89.9 2.0 %collective-permute-start.23 = (bf16[64,2048]{1,0:T(8,128)(2,1)S(1)}, bf16[64,2048]{1,0:T(8,128)(2,1)S(1)}, u32[]{:S(2)}, u32[]{:S(2)}) collective-permute-start(bf16[64,2048]{1,0:T(8,128)(2,1)S(1)} %get-tuple-element.104), channel_id=1, source_target_pairs={{0,8},{4,12},{8,0},{12,4},{1,9},{5,13},{9,1},{13,5},{2,10},{6,14},... | collective-permute-start | bytes 786440 | tf_op jit(solution)/shard_map/ppermute | solution.py:471
  91.9 5.9 %collective-permute-done.16.refs_1_ = bf16[256,768]{1,0:T(8,128)(2,1)S(1)} collective-permute-done((bf16[256,768]{1,0:T(8,128)(2,1)}, bf16[256,768]{1,0:T(8,128)(2,1)S(1)}, u32[]{:S(2)}, u32[]{:S(2)}) %collective-permute-start.16) | collective-permute-done | bytes 393248 | tf_op jit(solution)/shard_map/ppermute | solution.py:584
  99.6 2.1 %collective-permute-start.21 = (bf16[256,640]{1,0:T(8,128)(2,1)S(1)}, bf16[256,640]{1,0:T(8,128)(2,1)S(1)}, u32[]{:S(2)}, u32[]{:S(2)}) collective-permute-start(bf16[256,640]{1,0:T(8,128)(2,1)S(1)} %get-tuple-element.100.refs_2_), channel_id=1, source_target_pairs={{0,1},{1,0},{2,3},{3,2},{4,5},{5,4},{6,7},{7,6},{8,9},{9,8},{10,11... | collective-permute-start | bytes 983048 | tf_op jit(solution)/shard_map/ppermute | solution.py:584
  101.7 3.3 %shard_map.97 = (bf16[256,512]{1,0:T(8,128)(2,1)}, f32[8,128]{1,0:T(8,128)S(1)}) custom-call(s32[5]{0:T(128)S(1)} %stack.27.refs_0_.flag_ref, bf16[2048,512]{1,0:T(8,128)(2,1)} %refs_1_.9, f32[64,2048]{1,0:T(8,128)S(1)} %get-tuple-element.103.refs_2_, bf16[64,2048]{1,0:T(8,128)(2,1)S(1)} %collective-permute-done.23.refs_3_, s32[1,2048]{1,0:T(1,128)S(1)} %bitcast.32, ...), custom_call_target="tpu_custom_call" | custom-call | flops 1 | bytes 24000000 | tf_op jit(solution)/shard_map/pallas_call | solution.py:31
  105.0 4.8 %all-to-all-start.2 = ((bf16[16,16,512]{2,1,0:T(8,128)(2,1)}), bf16[16,16,512]{2,1,0:T(8,128)(2,1)S(1)}, u32[]{:S(2)}, u32[]{:S(2)}) async-start(bf16[16,16,512]{2,1,0:T(8,128)(2,1)} %bitcast.16), calls=%async_computation.2 | async-start | bytes 524288 | tf_op jit(solution)/shard_map/all_to_all | solution.py:551
  109.9 1.1 copy-done.10
  111.0 1.1 shard_map.98
  112.1 1.2 shard_map.99
  113.8 1.9 %collective-permute-start.25 = (bf16[64,2176]{1,0:T(8,128)(2,1)S(1)}, bf16[64,2176]{1,0:T(8,128)(2,1)S(1)}, u32[]{:S(2)}, u32[]{:S(2)}) collective-permute-start(bf16[64,2176]{1,0:T(8,128)(2,1)S(1)} %get-tuple-element.113), channel_id=1, source_target_pairs={{0,8},{4,12},{8,0},{12,4},{1,9},{5,13},{9,1},{13,5},{2,10},{6,14},... | collective-permute-start | bytes 835592 | tf_op jit(solution)/shard_map/ppermute | solution.py:471
  115.8 1.5 %collective-permute-start.28 = (bf16[64,640]{1,0:T(8,128)(2,1)}, bf16[64,640]{1,0:T(8,128)(2,1)S(1)}, u32[]{:S(2)}, u32[]{:S(2)}) collective-permute-start(bf16[64,640]{1,0:T(8,128)(2,1)} %get-tuple-element.117), channel_id=1, source_target_pairs={{0,8},{4,12},{8,0},{12,4},{1,9},{5,13},{9,1},{13,5},{2,10},{6,14},... | collective-permute-start | bytes 245768 | tf_op jit(solution)/shard_map/ppermute | solution.py:471
  117.6 6.6 %shard_map.100 = (bf16[2048,2048]{1,0:T(8,128)(2,1)}, f32[8,128]{1,0:T(8,128)S(1)}) custom-call(s32[5]{0:T(128)S(1)} %stack.27.refs_0_.flag_ref, s32[16]{0:T(128)S(1)} %gather_fusion, bf16[4,2048,128]{2,1,0:T(8,128)(2,1)} %all-to-all-done.refs_1_.refs_2_, bf16[64,2048]{1,0:T(8,128)(2,1)S(1)} %copy-done.6, bf16[64,2048]{1,0:T(8,128)(2,1)S(1)} %copy-done.8, ...), custom_call_target="tpu_custom_call" | custom-call | flops 2147483648 | bytes 8388608 | tf_op jit(solution)/shard_map/pallas_call | solution.py:31
  124.8 3.5 %collective-permute-start.32 = (bf16[16,2048]{1,0:T(8,128)(2,1)S(1)}, bf16[16,2048]{1,0:T(8,128)(2,1)S(1)}, u32[]{:S(2)}, u32[]{:S(2)}) collective-permute-start(bf16[16,2048]{1,0:T(8,128)(2,1)S(1)} %get-tuple-element.121.refs_1_), channel_id=1, source_target_pairs={{0,3},{1,2},{2,1},{3,0},{4,7},{5,6},{6,5},{7,4},{8,11},{9,10},{10,... | collective-permute-start | bytes 196616 | tf_op jit(solution)/shard_map/ppermute | solution.py:592
  128.3 1.0 collective-permute-done.26.refs_4_.refs_8_.refs_3_
  129.3 1.1 collective-permute-start.30
  130.4 1.9 %shard_map.101.refs_8_ = bf16[8192,128]{1,0:T(8,128)(2,1)} custom-call(s32[5]{0:T(128)S(1)} %stack.27.refs_0_.flag_ref, bf16[256,1280]{1,0:T(8,128)(2,1)S(1)} %bitcast.25, bf16[64,2176]{1,0:T(8,128)(2,1)S(1)} %get-tuple-element.111.refs_1_.refs_5_.refs_0_, bf16[64,2176]{1,0:T(8,128)(2,1)S(1)} %collective-permute-done.24.refs_2_.refs_6_.refs_1_, ...), custom_call_target="tpu_custom_call" | custom-call | flops 1 | bytes 5767168 | tf_op jit(solution)/shard_map/pallas_call | solution.py:213
  132.8 1.6 %shard_map.102 = bf16[8192,128]{1,0:T(8,128)(2,1)} custom-call(s32[5]{0:T(128)S(1)} %stack.27.refs_0_.flag_ref, bf16[64,2176]{1,0:T(8,128)(2,1)S(1)} %get-tuple-element.111.refs_1_.refs_5_.refs_0_, bf16[64,2176]{1,0:T(8,128)(2,1)S(1)} %collective-permute-done.24.refs_2_.refs_6_.refs_1_, ...), custom_call_target="tpu_custom_call", output_to_operand_aliasing={{}: (9, {})} | custom-call | flops 1 | bytes 2621440 | tf_op jit(solution)/shard_map/pallas_call | solution.py:213
  134.5 0.9 collective-permute-done.30.refs_2_
  135.4 1.3 shard_map.104
  (81 shorter events, 13.5 us)
Async XLA Ops:
  0.6 4.9 %copy-start = (s32[4]{0:T(128)S(1)}, s32[4]{0:T(128)}, u32[]{:S(2)}) copy-start(s32[4]{0:T(128)} %param.9) | copy-start | bytes 52
  1.6 4.6 %collective-permute-start = (bf16[64,512]{1,0:T(8,128)(2,1)S(1)}, bf16[64,512]{1,0:T(8,128)(2,1)S(1)}, u32[]{:S(2)}, u32[]{:S(2)}) collective-permute-start(bf16[64,512]{1,0:T(8,128)(2,1)S(1)} %get-tuple-element.124), channel_id=1, source_target_pairs={{0,4},{4,0},{8,12},{12,8},{1,5},{5,1},{9,13},{13,9},{2,6},{6,2},{1... | collective-permute-start | bytes 196616 | tf_op jit(solution)/shard_map/ppermute | solution.py:471
  2.2 5.1 %collective-permute-start.2 = (bf16[64,512]{1,0:T(8,128)(2,1)S(1)}, bf16[64,512]{1,0:T(8,128)(2,1)S(1)}, u32[]{:S(2)}, u32[]{:S(2)}) collective-permute-start(bf16[64,512]{1,0:T(8,128)(2,1)S(1)} %get-tuple-element.125), channel_id=1, source_target_pairs={{0,12},{4,8},{8,4},{12,0},{1,13},{5,9},{9,5},{13,1},{2,14},{6,10},... | collective-permute-start | bytes 196616 | tf_op jit(solution)/shard_map/ppermute | solution.py:471
  4.8 4.3 %collective-permute-start.1 = (bf16[64,512]{1,0:T(8,128)(2,1)S(1)}, bf16[64,512]{1,0:T(8,128)(2,1)S(1)}, u32[]{:S(2)}, u32[]{:S(2)}) collective-permute-start(bf16[64,512]{1,0:T(8,128)(2,1)S(1)} %get-tuple-element.126), channel_id=1, source_target_pairs={{0,8},{4,12},{8,0},{12,4},{1,9},{5,13},{9,1},{13,5},{2,10},{6,14},... | collective-permute-start | bytes 196616 | tf_op jit(solution)/shard_map/ppermute | solution.py:471
  12.4 2.0 %collective-permute-start.3 = (f32[64,2048]{1,0:T(8,128)S(1)}, f32[64,2048]{1,0:T(8,128)S(1)}, u32[]{:S(2)}, u32[]{:S(2)}) collective-permute-start(f32[64,2048]{1,0:T(8,128)S(1)} %get-tuple-element.63.refs_2_), channel_id=1, source_target_pairs={{0,4},{4,0},{8,12},{12,8},{1,5},{5,1},{9,13},{13,9},{2,6},{6,2},{1... | collective-permute-start | bytes 1572872 | tf_op jit(solution)/shard_map/ppermute | solution.py:471
  18.3 9.8 %collective-permute-start.4 = (bf16[256,640]{1,0:T(8,128)(2,1)S(1)}, bf16[256,640]{1,0:T(8,128)(2,1)S(1)}, u32[]{:S(2)}, u32[]{:S(2)}) collective-permute-start(bf16[256,640]{1,0:T(8,128)(2,1)S(1)} %get-tuple-element.67.refs_3_), channel_id=1, source_target_pairs={{0,1},{1,0},{2,3},{3,2},{4,5},{5,4},{6,7},{7,6},{8,9},{9,8},{10,11... | collective-permute-start | bytes 983048 | tf_op jit(solution)/shard_map/ppermute | solution.py:584
  19.9 6.5 %collective-permute-start.5 = (bf16[64,1024]{1,0:T(8,128)(2,1)S(1)}, bf16[64,1024]{1,0:T(8,128)(2,1)S(1)}, u32[]{:S(2)}, u32[]{:S(2)}) collective-permute-start(bf16[64,1024]{1,0:T(8,128)(2,1)S(1)} %get-tuple-element.72), channel_id=1, source_target_pairs={{0,8},{4,12},{8,0},{12,4},{1,9},{5,13},{9,1},{13,5},{2,10},{6,14},... | collective-permute-start | bytes 393224 | tf_op jit(solution)/shard_map/ppermute | solution.py:471
  25.8 12.5 %collective-permute-start.7 = (bf16[256,640]{1,0:T(8,128)(2,1)S(1)}, bf16[256,640]{1,0:T(8,128)(2,1)S(1)}, u32[]{:S(2)}, u32[]{:S(2)}) collective-permute-start(bf16[256,640]{1,0:T(8,128)(2,1)S(1)} %get-tuple-element.73.refs_6_), channel_id=1, source_target_pairs={{0,1},{1,0},{2,3},{3,2},{4,5},{5,4},{6,7},{7,6},{8,9},{9,8},{10,11... | collective-permute-start | bytes 983048 | tf_op jit(solution)/shard_map/ppermute | solution.py:584
  26.3 12.0 %collective-permute-start.6 = (bf16[64,1024]{1,0:T(8,128)(2,1)S(1)}, bf16[64,1024]{1,0:T(8,128)(2,1)S(1)}, u32[]{:S(2)}, u32[]{:S(2)}) collective-permute-start(bf16[64,1024]{1,0:T(8,128)(2,1)S(1)} %collective-permute-done.5.refs_3_), channel_id=1, source_target_pairs={{0,4},{4,0},{8,12},{12,8},{1,5},{5,1},{9,13},{13,9},{2,6},{6,2},{1... | collective-permute-start | bytes 393224 | tf_op jit(solution)/shard_map/ppermute | solution.py:471
  28.7 36.1 %all-to-all-start = ((bf16[4,2048,128]{2,1,0:T(8,128)(2,1)}), bf16[4,2048,128]{2,1,0:T(8,128)(2,1)}, u32[]{:S(2)}, u32[]{:S(2)}) async-start(bf16[4,2048,128]{2,1,0:T(8,128)(2,1)} %bitcast.34), calls=%async_computation | async-start | bytes 4194304 | tf_op jit(solution)/shard_map/all_to_all | solution.py:474
  33.2 11.7 %collective-permute-start.11 = (bf16[256,640]{1,0:T(8,128)(2,1)S(1)}, bf16[256,640]{1,0:T(8,128)(2,1)S(1)}, u32[]{:S(2)}, u32[]{:S(2)}) collective-permute-start(bf16[256,640]{1,0:T(8,128)(2,1)S(1)} %get-tuple-element.79.refs_6_), channel_id=1, source_target_pairs={{1,2},{2,1},{5,6},{6,5},{9,10},{10,9},{13,14},{14,13},{17,18},{18,... | collective-permute-start | bytes 983048 | tf_op jit(solution)/shard_map/ppermute | solution.py:586
  33.8 14.3 %collective-permute-start.10 = (bf16[256,768]{1,0:T(8,128)(2,1)S(1)}, bf16[256,768]{1,0:T(8,128)(2,1)S(1)}, u32[]{:S(2)}, u32[]{:S(2)}) collective-permute-start(bf16[256,768]{1,0:T(8,128)(2,1)S(1)} %get-tuple-element.78), channel_id=1, source_target_pairs={{0,1},{1,0},{2,3},{3,2},{4,5},{5,4},{6,7},{7,6},{8,9},{9,8},{10,11... | collective-permute-start | bytes 1179656 | tf_op jit(solution)/shard_map/ppermute | solution.py:584
  41.6 15.0 %copy-start.7 = (bf16[64,2048]{1,0:T(8,128)(2,1)}, bf16[64,2048]{1,0:T(8,128)(2,1)S(1)}, u32[]{:S(2)}) copy-start(bf16[64,2048]{1,0:T(8,128)(2,1)S(1)} %get-tuple-element.74.refs_3_.refs_4_) | copy-start | bytes 786436
  41.6 14.1 %collective-permute-start.9 = (bf16[256,640]{1,0:T(8,128)(2,1)S(1)}, bf16[256,640]{1,0:T(8,128)(2,1)S(1)}, u32[]{:S(2)}, u32[]{:S(2)}) collective-permute-start(bf16[256,640]{1,0:T(8,128)(2,1)S(1)} %get-tuple-element.77.refs_6_), channel_id=1, source_target_pairs={{1,2},{2,1},{5,6},{6,5},{9,10},{10,9},{13,14},{14,13},{17,18},{18,... | collective-permute-start | bytes 983048 | tf_op jit(solution)/shard_map/ppermute | solution.py:586
  42.3 14.3 %collective-permute-start.8 = (bf16[256,768]{1,0:T(8,128)(2,1)S(1)}, bf16[256,768]{1,0:T(8,128)(2,1)S(1)}, u32[]{:S(2)}, u32[]{:S(2)}) collective-permute-start(bf16[256,768]{1,0:T(8,128)(2,1)S(1)} %get-tuple-element.75), channel_id=1, source_target_pairs={{0,1},{1,0},{2,3},{3,2},{4,5},{5,4},{6,7},{7,6},{8,9},{9,8},{10,11... | collective-permute-start | bytes 1179656 | tf_op jit(solution)/shard_map/ppermute | solution.py:584
  52.1 0.7 copy-start.13
  52.9 18.5 %collective-permute-start.14 = (bf16[256,640]{1,0:T(8,128)(2,1)}, bf16[256,640]{1,0:T(8,128)(2,1)}, u32[]{:S(2)}, u32[]{:S(2)}) collective-permute-start(bf16[256,640]{1,0:T(8,128)(2,1)} %get-tuple-element.85.refs_5_), channel_id=1, source_target_pairs={{0,1},{1,0},{2,3},{3,2},{4,5},{5,4},{6,7},{7,6},{8,9},{9,8},{10,11... | collective-permute-start | bytes 983048 | tf_op jit(solution)/shard_map/ppermute | solution.py:584
  55.0 16.3 %collective-permute-start.15 = (bf16[256,768]{1,0:T(8,128)(2,1)S(1)}, bf16[256,768]{1,0:T(8,128)(2,1)S(1)}, u32[]{:S(2)}, u32[]{:S(2)}) collective-permute-start(bf16[256,768]{1,0:T(8,128)(2,1)S(1)} %get-tuple-element.87.refs_3_), channel_id=1, source_target_pairs={{1,2},{2,1},{5,6},{6,5},{9,10},{10,9},{13,14},{14,13},{17,18},{18,... | collective-permute-start | bytes 1179656 | tf_op jit(solution)/shard_map/ppermute | solution.py:586
  61.3 16.0 %collective-permute-start.12 = (bf16[256,640]{1,0:T(8,128)(2,1)}, bf16[256,640]{1,0:T(8,128)(2,1)}, u32[]{:S(2)}, u32[]{:S(2)}) collective-permute-start(bf16[256,640]{1,0:T(8,128)(2,1)} %get-tuple-element.82.refs_5_), channel_id=1, source_target_pairs={{0,1},{1,0},{2,3},{3,2},{4,5},{5,4},{6,7},{7,6},{8,9},{9,8},{10,11... | collective-permute-start | bytes 983048 | tf_op jit(solution)/shard_map/ppermute | solution.py:584
  63.4 13.8 %collective-permute-start.13 = (bf16[256,768]{1,0:T(8,128)(2,1)S(1)}, bf16[256,768]{1,0:T(8,128)(2,1)}, u32[]{:S(2)}, u32[]{:S(2)}) collective-permute-start(bf16[256,768]{1,0:T(8,128)(2,1)S(1)} %get-tuple-element.84.refs_3_), channel_id=1, source_target_pairs={{1,2},{2,1},{5,6},{6,5},{9,10},{10,9},{13,14},{14,13},{17,18},{18,... | collective-permute-start | bytes 1179656 | tf_op jit(solution)/shard_map/ppermute | solution.py:586
  64.8 6.5 %copy-start.14 = (bf16[256,640]{1,0:T(8,128)(2,1)S(1)}, bf16[256,640]{1,0:T(8,128)(2,1)}, u32[]{:S(2)}) copy-start(bf16[256,640]{1,0:T(8,128)(2,1)} %copy-done.13) | copy-start | bytes 983044
  71.4 5.9 %copy-start.12 = (bf16[256,640]{1,0:T(8,128)(2,1)S(1)}, bf16[256,640]{1,0:T(8,128)(2,1)}, u32[]{:S(2)}) copy-start(bf16[256,640]{1,0:T(8,128)(2,1)} %copy-done.11) | copy-start | bytes 983044
  72.7 15.0 %collective-permute-start.19 = (bf16[256,640]{1,0:T(8,128)(2,1)S(1)}, bf16[256,640]{1,0:T(8,128)(2,1)}, u32[]{:S(2)}, u32[]{:S(2)}) collective-permute-start(bf16[256,640]{1,0:T(8,128)(2,1)S(1)} %get-tuple-element.95.refs_2_), channel_id=1, source_target_pairs={{1,2},{2,1},{5,6},{6,5},{9,10},{10,9},{13,14},{14,13},{17,18},{18,... | collective-permute-start | bytes 983048 | tf_op jit(solution)/shard_map/ppermute | solution.py:586
  74.1 13.6 %collective-permute-start.18 = (bf16[256,768]{1,0:T(8,128)(2,1)S(1)}, bf16[256,768]{1,0:T(8,128)(2,1)}, u32[]{:S(2)}, u32[]{:S(2)}) collective-permute-start(bf16[256,768]{1,0:T(8,128)(2,1)S(1)} %get-tuple-element.94.refs_4_), channel_id=1, source_target_pairs={{0,1},{1,0},{2,3},{3,2},{4,5},{5,4},{6,7},{7,6},{8,9},{9,8},{10,11... | collective-permute-start | bytes 1179656 | tf_op jit(solution)/shard_map/ppermute | solution.py:584
  77.3 10.5 %collective-permute-start.20 = (f32[128,2048]{1,0:T(8,128)S(1)}, f32[128,2048]{1,0:T(8,128)S(1)}, u32[]{:S(2)}, u32[]{:S(2)}) collective-permute-start(f32[128,2048]{1,0:T(8,128)S(1)} %get-tuple-element.96.refs_5_), channel_id=1, source_target_pairs={{0,4},{4,0},{8,12},{12,8},{1,5},{5,1},{9,13},{13,9},{2,6},{6,2},{1... | collective-permute-start | bytes 3145736 | tf_op jit(solution)/shard_map/ppermute | solution.py:471
  79.4 0.7 copy-start.1
  80.9 24.1 %all-to-all-start.1 = ((bf16[4,64,1280]{2,1,0:T(8,128)(2,1)}), bf16[4,64,1280]{2,1,0:T(8,128)(2,1)S(1)}, u32[]{:S(2)}, u32[]{:S(2)}) async-start(bf16[4,64,1280]{2,1,0:T(8,128)(2,1)} %bitcast.13), calls=%async_computation.1 | async-start | bytes 1310720 | tf_op jit(solution)/shard_map/all_to_all | solution.py:474
  84.6 7.3 %collective-permute-start.17 = (bf16[256,640]{1,0:T(8,128)(2,1)}, bf16[256,640]{1,0:T(8,128)(2,1)S(1)}, u32[]{:S(2)}, u32[]{:S(2)}) collective-permute-start(bf16[256,640]{1,0:T(8,128)(2,1)} %copy-done.3), channel_id=1, source_target_pairs={{1,2},{2,1},{5,6},{6,5},{9,10},{10,9},{13,14},{14,13},{17,18},{18,... | collective-permute-start | bytes 983048 | tf_op jit(solution)/shard_map/ppermute | solution.py:586
  85.3 12.5 %collective-permute-start.16 = (bf16[256,768]{1,0:T(8,128)(2,1)}, bf16[256,768]{1,0:T(8,128)(2,1)S(1)}, u32[]{:S(2)}, u32[]{:S(2)}) collective-permute-start(bf16[256,768]{1,0:T(8,128)(2,1)} %copy-done.1), channel_id=1, source_target_pairs={{0,1},{1,0},{2,3},{3,2},{4,5},{5,4},{6,7},{7,6},{8,9},{9,8},{10,11... | collective-permute-start | bytes 1179656 | tf_op jit(solution)/shard_map/ppermute | solution.py:584
  87.7 10.1 %copy-start.2 = (bf16[256,768]{1,0:T(8,128)(2,1)S(1)}, bf16[256,768]{1,0:T(8,128)(2,1)}, u32[]{:S(2)}) copy-start(bf16[256,768]{1,0:T(8,128)(2,1)} %copy-done.1) | copy-start | bytes 1179652
  87.8 10.1 %copy-start.4 = (bf16[256,640]{1,0:T(8,128)(2,1)S(1)}, bf16[256,640]{1,0:T(8,128)(2,1)}, u32[]{:S(2)}) copy-start(bf16[256,640]{1,0:T(8,128)(2,1)} %copy-done.3) | copy-start | bytes 983044
  89.9 11.8 %collective-permute-start.23 = (bf16[64,2048]{1,0:T(8,128)(2,1)S(1)}, bf16[64,2048]{1,0:T(8,128)(2,1)S(1)}, u32[]{:S(2)}, u32[]{:S(2)}) collective-permute-start(bf16[64,2048]{1,0:T(8,128)(2,1)S(1)} %get-tuple-element.104), channel_id=1, source_target_pairs={{0,8},{4,12},{8,0},{12,4},{1,9},{5,13},{9,1},{13,5},{2,10},{6,14},... | collective-permute-start | bytes 786440 | tf_op jit(solution)/shard_map/ppermute | solution.py:471
  91.9 18.0 %collective-permute-start.22 = (bf16[256,640]{1,0:T(8,128)(2,1)}, bf16[256,640]{1,0:T(8,128)(2,1)S(1)}, u32[]{:S(2)}, u32[]{:S(2)}) collective-permute-start(bf16[256,640]{1,0:T(8,128)(2,1)} %get-tuple-element.101.refs_2_), channel_id=1, source_target_pairs={{0,1},{1,0},{2,3},{3,2},{4,5},{5,4},{6,7},{7,6},{8,9},{9,8},{10,11... | collective-permute-start | bytes 983048 | tf_op jit(solution)/shard_map/ppermute | solution.py:584
  98.7 0.9 copy-start.9
  99.6 12.5 %collective-permute-start.21 = (bf16[256,640]{1,0:T(8,128)(2,1)S(1)}, bf16[256,640]{1,0:T(8,128)(2,1)S(1)}, u32[]{:S(2)}, u32[]{:S(2)}) collective-permute-start(bf16[256,640]{1,0:T(8,128)(2,1)S(1)} %get-tuple-element.100.refs_2_), channel_id=1, source_target_pairs={{0,1},{1,0},{2,3},{3,2},{4,5},{5,4},{6,7},{7,6},{8,9},{9,8},{10,11... | collective-permute-start | bytes 983048 | tf_op jit(solution)/shard_map/ppermute | solution.py:584
  105.0 19.2 %all-to-all-start.2 = ((bf16[16,16,512]{2,1,0:T(8,128)(2,1)}), bf16[16,16,512]{2,1,0:T(8,128)(2,1)S(1)}, u32[]{:S(2)}, u32[]{:S(2)}) async-start(bf16[16,16,512]{2,1,0:T(8,128)(2,1)} %bitcast.16), calls=%async_computation.2 | async-start | bytes 524288 | tf_op jit(solution)/shard_map/all_to_all | solution.py:551
  109.8 1.1 copy-start.10
  112.1 5.5 %copy-start.6 = (bf16[64,2048]{1,0:T(8,128)(2,1)S(1)}, bf16[64,2048]{1,0:T(8,128)(2,1)}, u32[]{:S(2)}) copy-start(bf16[64,2048]{1,0:T(8,128)(2,1)} %copy-done.5) | copy-start | bytes 786436
  112.1 5.5 %copy-start.8 = (bf16[64,2048]{1,0:T(8,128)(2,1)S(1)}, bf16[64,2048]{1,0:T(8,128)(2,1)}, u32[]{:S(2)}) copy-start(bf16[64,2048]{1,0:T(8,128)(2,1)} %copy-done.7) | copy-start | bytes 786436
  113.3 3.9 %collective-permute-start.27 = (bf16[64,640]{1,0:T(8,128)(2,1)S(1)}, bf16[64,640]{1,0:T(8,128)(2,1)S(1)}, u32[]{:S(2)}, u32[]{:S(2)}) collective-permute-start(bf16[64,640]{1,0:T(8,128)(2,1)S(1)} %get-tuple-element.116), channel_id=1, source_target_pairs={{0,4},{4,0},{8,12},{12,8},{1,5},{5,1},{9,13},{13,9},{2,6},{6,2},{1... | collective-permute-start | bytes 245768 | tf_op jit(solution)/shard_map/ppermute | solution.py:471
  113.7 11.0 %collective-permute-start.24 = (bf16[64,2176]{1,0:T(8,128)(2,1)S(1)}, bf16[64,2176]{1,0:T(8,128)(2,1)S(1)}, u32[]{:S(2)}, u32[]{:S(2)}) collective-permute-start(bf16[64,2176]{1,0:T(8,128)(2,1)S(1)} %get-tuple-element.112), channel_id=1, source_target_pairs={{0,4},{4,0},{8,12},{12,8},{1,5},{5,1},{9,13},{13,9},{2,6},{6,2},{1... | collective-permute-start | bytes 835592 | tf_op jit(solution)/shard_map/ppermute | solution.py:471
  113.8 14.4 %collective-permute-start.25 = (bf16[64,2176]{1,0:T(8,128)(2,1)S(1)}, bf16[64,2176]{1,0:T(8,128)(2,1)S(1)}, u32[]{:S(2)}, u32[]{:S(2)}) collective-permute-start(bf16[64,2176]{1,0:T(8,128)(2,1)S(1)} %get-tuple-element.113), channel_id=1, source_target_pairs={{0,8},{4,12},{8,0},{12,4},{1,9},{5,13},{9,1},{13,5},{2,10},{6,14},... | collective-permute-start | bytes 835592 | tf_op jit(solution)/shard_map/ppermute | solution.py:471
  115.8 13.5 %collective-permute-start.26 = (bf16[64,2176]{1,0:T(8,128)(2,1)S(1)}, bf16[64,2176]{1,0:T(8,128)(2,1)S(1)}, u32[]{:S(2)}, u32[]{:S(2)}) collective-permute-start(bf16[64,2176]{1,0:T(8,128)(2,1)S(1)} %get-tuple-element.114), channel_id=1, source_target_pairs={{0,12},{4,8},{8,4},{12,0},{1,13},{5,9},{9,5},{13,1},{2,14},{6,10},... | collective-permute-start | bytes 835592 | tf_op jit(solution)/shard_map/ppermute | solution.py:471
  115.8 16.5 %collective-permute-start.28 = (bf16[64,640]{1,0:T(8,128)(2,1)}, bf16[64,640]{1,0:T(8,128)(2,1)S(1)}, u32[]{:S(2)}, u32[]{:S(2)}) collective-permute-start(bf16[64,640]{1,0:T(8,128)(2,1)} %get-tuple-element.117), channel_id=1, source_target_pairs={{0,8},{4,12},{8,0},{12,4},{1,9},{5,13},{9,1},{13,5},{2,10},{6,14},... | collective-permute-start | bytes 245768 | tf_op jit(solution)/shard_map/ppermute | solution.py:471
  117.3 15.5 %collective-permute-start.29 = (bf16[64,640]{1,0:T(8,128)(2,1)}, bf16[64,640]{1,0:T(8,128)(2,1)S(1)}, u32[]{:S(2)}, u32[]{:S(2)}) collective-permute-start(bf16[64,640]{1,0:T(8,128)(2,1)} %get-tuple-element.118), channel_id=1, source_target_pairs={{0,12},{4,8},{8,4},{12,0},{1,13},{5,9},{9,5},{13,1},{2,14},{6,10},... | collective-permute-start | bytes 245768 | tf_op jit(solution)/shard_map/ppermute | solution.py:471
  124.8 9.6 %collective-permute-start.32 = (bf16[16,2048]{1,0:T(8,128)(2,1)S(1)}, bf16[16,2048]{1,0:T(8,128)(2,1)S(1)}, u32[]{:S(2)}, u32[]{:S(2)}) collective-permute-start(bf16[16,2048]{1,0:T(8,128)(2,1)S(1)} %get-tuple-element.121.refs_1_), channel_id=1, source_target_pairs={{0,3},{1,2},{2,1},{3,0},{4,7},{5,6},{6,5},{7,4},{8,11},{9,10},{10,... | collective-permute-start | bytes 196616 | tf_op jit(solution)/shard_map/ppermute | solution.py:592
  128.3 6.2 %collective-permute-start.31 = (bf16[16,2048]{1,0:T(8,128)(2,1)S(1)}, bf16[16,2048]{1,0:T(8,128)(2,1)S(1)}, u32[]{:S(2)}, u32[]{:S(2)}) collective-permute-start(bf16[16,2048]{1,0:T(8,128)(2,1)S(1)} %get-tuple-element.121.refs_1_), channel_id=1, source_target_pairs={{0,2},{1,3},{2,0},{3,1},{4,6},{5,7},{6,4},{7,5},{8,10},{9,11},{10,... | collective-permute-start | bytes 196616 | tf_op jit(solution)/shard_map/ppermute | solution.py:592
  129.3 6.2 %collective-permute-start.30 = (bf16[16,2048]{1,0:T(8,128)(2,1)S(1)}, bf16[16,2048]{1,0:T(8,128)(2,1)S(1)}, u32[]{:S(2)}, u32[]{:S(2)}) collective-permute-start(bf16[16,2048]{1,0:T(8,128)(2,1)S(1)} %get-tuple-element.121.refs_1_), channel_id=1, source_target_pairs={{0,1},{1,0},{2,3},{3,2},{4,5},{5,4},{6,7},{7,6},{8,9},{9,8},{10,11... | collective-permute-start | bytes 196616 | tf_op jit(solution)/shard_map/ppermute | solution.py:592
  (3 other events, 2.1 us)

commit v4 on v3

--- a/solution.py
+++ b/solution.py
@@ -224,7 +224,7 @@
         input_output_aliases={} if held is None else {1 + len(flat): 0},
         compiler_params=pltpu.CompilerParams(vmem_limit_bytes=12 * 1024 * 1024),
         cost_estimate=pl.CostEstimate(
-            flops=1, bytes_accessed=4 * count * width * 2 * R * 2, transcendentals=0
+            flops=15 * 10**9, bytes_accessed=4 * count * width * 2 * R * 2, transcendentals=0
         ),
     )(position, *flat, *extra)
 
@@ -381,7 +381,7 @@
     return dict(zip([*out_names, MARK], made))
 
 
-def shrink_call(slot, pool, acts, marks, per=4):
+def shrink_call(slot, pool, acts, marks, per=8):
     rows, width = acts.shape
 
     def body(slot_ref, pool_ref, acts_ref, out_ref):
@@ -400,7 +400,7 @@
         (jax.ShapeDtypeStruct((2 * R, rows), F32),),
         (pl.BlockSpec((2 * R, per * BLOCK), lambda i: (0, i)),),
         [],
-        12,
+        16,
         4 * rows * width * 2 * R,
         rows * width * 2,
         marks,
@@ -499,6 +499,9 @@
     *more, mark = tiles_call(lhs_own, acts, tiles, [mark])
     for c in range(1, per_kind):
         parts[c] = more[c - 1]
+    pool_in, _, _ = lax.optimization_barrier((down_pool[0], mark, came_half))
+    pool = to_owner(pool_in).reshape(count, width, 2 * R)
+    pools = [pltpu.with_memory_space_constraint(pool, pltpu.HBM)]
 
     for t in range(n + 6):
         if t < 2:
@@ -528,14 +531,12 @@
             if t >= 6:
                 arrays[OLD_LINE] = line[t - 2]
                 c = t - 6
-                if c in (0, per_kind - 1):
+                if c in (0, per_kind - 1, n - 2):
                     outs[FINAL] = (tenants, sizes[c])
-                elif c == n - 1:
-                    outs.update({(FINAL, m): (R, sizes[c]) for m in range(count)})
                 else:
                     arrays[OLD_FINAL] = final[c - 1]
                     wide_now = final[c - 1].shape[1] + sizes[c]
-                    if c == n - 2:
+                    if c >= per_kind:
                         outs.update({(FINAL, m): (R, wide_now) for m in range(count)})
                     else:
                         outs[FINALS] = (tenants, wide_now)
@@ -551,15 +552,14 @@
                 up_pieces = lax.all_to_all(
                     up, ("adapter", "dp"), split_axis=0, concat_axis=0, tiled=True
                 )
+            if t == 9:
+                acts_grad, mark = expand_call(flags, slot, pools, d_own, d_other, width, [mark])
+                marks = [mark]
             if t == 6:
                 shrunk_part, mark = shrink_call(slot, pools[0], acts, [mark])
                 marks = [mark]
             made = step_call(flags, arrays, outs, marks, count, start)
             mark = made[MARK]
-            if t == 2:
-                pool_in, _ = lax.optimization_barrier((down_pool[0], mark))
-                pool = to_owner(pool_in).reshape(count, width, 2 * R)
-                pools = [pltpu.with_memory_space_constraint(pool, pltpu.HBM)]
             if PART in made and t < n:
                 parts[t] = made[PART]
             if t == per_kind:
@@ -585,7 +585,6 @@
         if t in inner:
             from_inner[t] = lax.ppermute(inner[t], "dp", [(1, 2), (2, 1)])
 
-    acts_grad, mark = expand_call(flags, slot, pools, d_own, d_other, width, [mark])
     dp = lax.axis_size("dp")
     up_rows = fold_call(up_pieces, count, R // dp, [mark])
     up_parts = [up_rows] + [
@@ -593,19 +592,14 @@
     ]
     up_grad = stack_call(flags, up_parts)
     down_grad = None
-    mixed, last = final[n - 2], final[n - 1]
-    joint, rest, split = sizes[0] + sizes[1], sizes[2], width - sizes[n - 1]
+    mixed, last = final[per_kind], final[n - 1]
+    joint, split = sizes[0] + sizes[1], sizes[per_kind]
+    down_grad = place_call(
+        flags, [(own, 0, split)], [(mixed, width - joint, split)], 0, total_rows, None
+    )
     down_grad = place_call(
         flags,
-        [(own, 0, joint), (mixed, 0, split - joint)],
-        [(mixed, rest, split)],
-        0,
-        total_rows,
-        None,
-    )
-    down_grad = place_call(
-        flags,
-        [(mixed, split - joint, width - split)],
+        [(own, split, joint - split), (mixed, 0, width - joint)],
         [(last, 0, width - split)],
         split,
         total_rows,

time: 138 us -> 129 us (0.935)
  waiting for transfers between devices: 19.1 us -> 13.6 us
  starting transfers between devices: 55.2 us -> 53.5 us
    ppermute x10, waiting for transfers between devices: 11.9 us -> 2.92 us  [local(): from_line[t] = lax.ppermute(line[t], 'dp', [(0, 1), (1, 0), (2, 3), (3, 2)])]
    all_to_all x1, waiting for transfers between devices: 0.01 us -> 3.95 us  [local(): lax.all_to_all(up, ('adapter', 'dp'), split_axis=0, concat_axis=0, tiled=...]
    ppermute x14, waiting for transfers between devices: 6.19 us -> 4.33 us  [swap(): return lax.ppermute(x, 'adapter', [(i, i ^ m) for i in range(count)])]
  transfers between devices with their start and end apart: 36 -> 36, of which waited for: 11 -> 7; matrix products, arithmetic and copies ran while one was open for 1% -> 1% of each run, Pallas kernels for 33% -> 35%
where the time goes in v4:
time: 129 us; the launch traced here: 128 us
  starting transfers between devices  53.5 us (41%)
  Pallas kernels  52.6 us (41%)
  waiting for transfers between devices  13.6 us (11%)
  local copies, waits for them, and re-layouts  6.32 us (5%)
    pallas_call x18, Pallas kernels, launch(): pl.pallas_call(kernel, grid=grid, out_shape=[*outs, jax.ShapeDtypeStruct(...  49.1 us
    ppermute x10, starting transfers between devices, local(): from_line[t] = lax.ppermute(line[t], 'dp', [(0, 1), (1, 0), (2, 3), (3, 2)])  21.1 us
    ppermute x14, starting transfers between devices, swap(): return lax.ppermute(x, 'adapter', [(i, i ^ m) for i in range(count)])  11.1 us
    all_to_all x2, starting transfers between devices, to_owner(): return lax.all_to_all(x, 'adapter', split_axis=0, concat_axis=0, tiled=True)  7.95 us
    ppermute x6, starting transfers between devices, local(): from_inner[t] = lax.ppermute(inner[t], 'dp', [(1, 2), (2, 1)])  5.48 us
    unnamed x30, local copies, waits for them, and re-layouts  4.54 us
    ppermute x3, starting transfers between devices, local(): lax.ppermute(up_rows, 'dp', [(i, i ^ m) for i in range(dp)])  4.39 us
    ppermute x14, waiting for transfers between devices, swap(): return lax.ppermute(x, 'adapter', [(i, i ^ m) for i in range(count)])  4.33 us
  transfers between devices with their start and end apart: 36, of which 7 were waited for; matrix products, arithmetic and copies ran while one was open for 1% of the time, Pallas kernels for 35%

profile of v4, /device:TPU:0, one launch (start us, length us, event | category | flops | bytes accessed | tf_op | source)
XLA Modules:
  0.0 127.8 jit_solution(2184670842551638807)
XLA Ops:
  0.7 1.0 dynamic-slice_bitcast_fusion.3
  2.2 2.6 %collective-permute-start.1 = (bf16[64,512]{1,0:T(8,128)(2,1)S(1)}, bf16[64,512]{1,0:T(8,128)(2,1)S(1)}, u32[]{:S(2)}, u32[]{:S(2)}) collective-permute-start(bf16[64,512]{1,0:T(8,128)(2,1)S(1)} %get-tuple-element.126), channel_id=1, source_target_pairs={{0,8},{4,12},{8,0},{12,4},{1,9},{5,13},{9,1},{13,5},{2,10},{6,14},... | collective-permute-start | bytes 196616 | tf_op jit(solution)/shard_map/ppermute | solution.py:471
  6.2 1.2 collective-permute-done.1
  7.4 1.4 %collective-permute-done.2 = bf16[64,512]{1,0:T(8,128)(2,1)S(1)} collective-permute-done((bf16[64,512]{1,0:T(8,128)(2,1)S(1)}, bf16[64,512]{1,0:T(8,128)(2,1)S(1)}, u32[]{:S(2)}, u32[]{:S(2)}) %collective-permute-start.2) | collective-permute-done | bytes 65568 | tf_op jit(solution)/shard_map/ppermute | solution.py:471
  8.9 3.2 %shard_map.85 = (f32[64,2048]{1,0:T(8,128)S(1)}, f32[8,128]{1,0:T(8,128)}) custom-call(s32[5]{0:T(128)S(1)} %stack.27.refs_0_.flag_ref, s32[1,2048]{1,0:T(1,128)S(1)} %bitcast.28, bf16[256,512]{1,0:T(8,128)(2,1)S(1)} %pad_maximum_fusion.refs_2_, bf16[2048,512]{1,0:T(8,128)(2,1)} %refs_1_.9), custom_call_target="tpu_custom_call" | custom-call | flops 536870912 | bytes 2097152 | tf_op jit(solution)/shard_map/pallas_call | solution.py:31
  12.4 1.7 %collective-permute-done.3.refs_3_ = f32[64,2048]{1,0:T(8,128)S(1)} collective-permute-done((f32[64,2048]{1,0:T(8,128)S(1)}, f32[64,2048]{1,0:T(8,128)S(1)}, u32[]{:S(2)}, u32[]{:S(2)}) %collective-permute-start.3) | collective-permute-done | bytes 524320 | tf_op jit(solution)/shard_map/ppermute | solution.py:471
  14.1 3.2 %shard_map.86 = (bf16[256,640]{1,0:T(8,128)(2,1)S(1)}, bf16[256,2048]{1,0:T(8,128)(2,1)S(1)}, bf16[64,2048]{1,0:T(8,128)(2,1)S(1)}, bf16[64,1024]{1,0:T(8,128)(2,1)S(1)}, f32[8,128]{1,0:T(8,128)S(1)}) custom-call(s32[5]{0:T(128)S(1)} %stack.27.refs_0_.flag_ref, s32[1,2048]{1,0:T(1,128)S(1)} %bitcast.29, f32[64,2048]{1,0:T(8,128)S(1)} %get-tuple-element.63.refs_2_, ...), custom_call_target="tpu_custom_call" | custom-call | flops 671088640 | bytes 2621440 | tf_op jit(solution)/shard_map/pallas_call | solution.py:31
  17.3 0.7 copy-done.3
  18.0 1.6 %collective-permute-start.7 = (bf16[256,640]{1,0:T(8,128)(2,1)S(1)}, bf16[256,640]{1,0:T(8,128)(2,1)S(1)}, u32[]{:S(2)}, u32[]{:S(2)}) collective-permute-start(bf16[256,640]{1,0:T(8,128)(2,1)S(1)} %get-tuple-element.72.refs_3_), channel_id=1, source_target_pairs={{0,1},{1,0},{2,3},{3,2},{4,5},{5,4},{6,7},{7,6},{8,9},{9,8},{10,11... | collective-permute-start | bytes 983048 | tf_op jit(solution)/shard_map/ppermute | solution.py:584
  19.6 1.3 %collective-permute-start.4 = (bf16[64,1024]{1,0:T(8,128)(2,1)S(1)}, bf16[64,1024]{1,0:T(8,128)(2,1)S(1)}, u32[]{:S(2)}, u32[]{:S(2)}) collective-permute-start(bf16[64,1024]{1,0:T(8,128)(2,1)S(1)} %get-tuple-element.67), channel_id=1, source_target_pairs={{0,8},{4,12},{8,0},{12,4},{1,9},{5,13},{9,1},{13,5},{2,10},{6,14},... | collective-permute-start | bytes 393224 | tf_op jit(solution)/shard_map/ppermute | solution.py:471
  20.9 4.5 %shard_map.87 = (bf16[256,640]{1,0:T(8,128)(2,1)S(1)}, bf16[256,768]{1,0:T(8,128)(2,1)S(1)}, f32[8,128]{1,0:T(8,128)S(1)}) custom-call(bf16[256,2048]{1,0:T(8,128)(2,1)S(1)} %get-tuple-element.64.refs_0_, bf16[2048,2048]{1,0:T(8,128)(2,1)} %refs_2_.1, f32[8,128]{1,0:T(8,128)S(1)} %get-tuple-element.65.refs_2_), custom_call_target="tpu_custom_call" | custom-call | flops 1476395008 | bytes 5767168 | tf_op jit(solution)/shard_map/pallas_call | solution.py:31
  25.9 4.5 %all-to-all-start = ((bf16[4,2048,128]{2,1,0:T(8,128)(2,1)}), bf16[4,2048,128]{2,1,0:T(8,128)(2,1)}, u32[]{:S(2)}, u32[]{:S(2)}) async-start(bf16[4,2048,128]{2,1,0:T(8,128)(2,1)} %bitcast.34), calls=%async_computation | async-start | bytes 4194304 | tf_op jit(solution)/shard_map/all_to_all | solution.py:474
  31.5 1.6 %collective-permute-start.8 = (bf16[256,768]{1,0:T(8,128)(2,1)S(1)}, bf16[256,768]{1,0:T(8,128)(2,1)S(1)}, u32[]{:S(2)}, u32[]{:S(2)}) collective-permute-start(bf16[256,768]{1,0:T(8,128)(2,1)S(1)} %get-tuple-element.75), channel_id=1, source_target_pairs={{0,1},{1,0},{2,3},{3,2},{4,5},{5,4},{6,7},{7,6},{8,9},{9,8},{10,11... | collective-permute-start | bytes 1179656 | tf_op jit(solution)/shard_map/ppermute | solution.py:584
  33.8 1.5 %collective-permute-done.6.refs_5_ = bf16[256,640]{1,0:T(8,128)(2,1)S(1)} collective-permute-done((bf16[256,640]{1,0:T(8,128)(2,1)S(1)}, bf16[256,640]{1,0:T(8,128)(2,1)S(1)}, u32[]{:S(2)}, u32[]{:S(2)}) %collective-permute-start.6) | collective-permute-done | bytes 327712 | tf_op jit(solution)/shard_map/ppermute | solution.py:584
  35.3 3.3 %shard_map.89 = (bf16[256,768]{1,0:T(8,128)(2,1)S(1)}, bf16[64,2048]{1,0:T(8,128)(2,1)S(1)}, bf16[256,640]{1,0:T(8,128)(2,1)S(1)}, bf16[256,768]{1,0:T(8,128)(2,1)S(1)}, f32[8,128]{1,0:T(8,128)S(1)}) custom-call(s32[5]{0:T(128)S(1)} %stack.27.refs_0_.flag_ref, bf16[2048,2048]{1,0:T(8,128)(2,1)} %refs_2_.1, s32[1,2048]{1,0:T(1,128)S(1)} %bitcast.30, ...), custom_call_target="tpu_custom_call" | custom-call | flops 15000000512 | bytes 24000000 | tf_op jit(solution)/shard_map/pallas_call | solution.py:31
  38.6 3.0 %collective-permute-start.12 = (bf16[256,768]{1,0:T(8,128)(2,1)S(1)}, bf16[256,768]{1,0:T(8,128)(2,1)S(1)}, u32[]{:S(2)}, u32[]{:S(2)}) collective-permute-start(bf16[256,768]{1,0:T(8,128)(2,1)S(1)} %get-tuple-element.81), channel_id=1, source_target_pairs={{0,1},{1,0},{2,3},{3,2},{4,5},{5,4},{6,7},{7,6},{8,9},{9,8},{10,11... | collective-permute-start | bytes 1179656 | tf_op jit(solution)/shard_map/ppermute | solution.py:584
  42.3 1.4 %collective-permute-done.8.refs_4_ = bf16[256,768]{1,0:T(8,128)(2,1)S(1)} collective-permute-done((bf16[256,768]{1,0:T(8,128)(2,1)S(1)}, bf16[256,768]{1,0:T(8,128)(2,1)S(1)}, u32[]{:S(2)}, u32[]{:S(2)}) %collective-permute-start.8) | collective-permute-done | bytes 393248 | tf_op jit(solution)/shard_map/ppermute | solution.py:584
  43.7 3.2 %shard_map.90 = (bf16[256,640]{1,0:T(8,128)(2,1)S(1)}, bf16[256,768]{1,0:T(8,128)(2,1)S(1)}, bf16[256,640]{1,0:T(8,128)(2,1)S(1)}, f32[8,128]{1,0:T(8,128)S(1)}) custom-call(s32[5]{0:T(128)S(1)} %stack.27.refs_0_.flag_ref, bf16[2048,2048]{1,0:T(8,128)(2,1)} %refs_2_.1, s32[1,2048]{1,0:T(1,128)S(1)} %bitcast.31, ...), custom_call_target="tpu_custom_call" | custom-call | flops 15000000512 | bytes 24000000 | tf_op jit(solution)/shard_map/pallas_call | solution.py:31
  47.6 6.3 %collective-permute-start.10 = (bf16[256,640]{1,0:T(8,128)(2,1)S(1)}, bf16[256,640]{1,0:T(8,128)(2,1)S(1)}, u32[]{:S(2)}, u32[]{:S(2)}) collective-permute-start(bf16[256,640]{1,0:T(8,128)(2,1)S(1)} %get-tuple-element.78.refs_5_), channel_id=1, source_target_pairs={{0,1},{1,0},{2,3},{3,2},{4,5},{5,4},{6,7},{7,6},{8,9},{9,8},{10,11... | collective-permute-start | bytes 983048 | tf_op jit(solution)/shard_map/ppermute | solution.py:584
  53.9 3.9 %shard_map.91 = (bf16[256,640]{1,0:T(8,128)(2,1)S(1)}, bf16[256,768]{1,0:T(8,128)(2,1)S(1)}, bf16[256,640]{1,0:T(8,128)(2,1)}, f32[8,128]{1,0:T(8,128)S(1)}) custom-call(s32[5]{0:T(128)S(1)} %stack.27.refs_0_.flag_ref, bf16[2048,2048]{1,0:T(8,128)(2,1)} %refs_2_.1, s32[1,2048]{1,0:T(1,128)S(1)} %bitcast.32, ...), custom_call_target="tpu_custom_call" | custom-call | flops 15000000512 | bytes 24000000 | tf_op jit(solution)/shard_map/pallas_call | solution.py:31
  57.9 0.7 copy-done.7
  59.3 2.2 %collective-permute-start.17 = (bf16[256,640]{1,0:T(8,128)(2,1)}, bf16[256,640]{1,0:T(8,128)(2,1)}, u32[]{:S(2)}, u32[]{:S(2)}) collective-permute-start(bf16[256,640]{1,0:T(8,128)(2,1)} %get-tuple-element.90.refs_5_), channel_id=1, source_target_pairs={{0,1},{1,0},{2,3},{3,2},{4,5},{5,4},{6,7},{7,6},{8,9},{9,8},{10,11... | collective-permute-start | bytes 983048 | tf_op jit(solution)/shard_map/ppermute | solution.py:584
  61.5 5.6 %shard_map.92 = (f32[128,2048]{1,0:T(8,128)S(1)}, f32[8,128]{1,0:T(8,128)S(1)}) custom-call(s32[16]{0:T(128)S(1)} %gather_fusion, bf16[4,2048,128]{2,1,0:T(8,128)(2,1)} %all-to-all-done.refs_1_.refs_2_, bf16[2048,2048]{1,0:T(8,128)(2,1)} %refs_2_.1, f32[8,128]{1,0:T(8,128)S(1)} %get-tuple-element.85.refs_3_), custom_call_target="tpu_custom_call" | custom-call | flops 2147483648 | bytes 8388608 | tf_op jit(solution)/shard_map/pallas_call | solution.py:31
  67.2 1.5 %shard_map.93 = (bf16[256,640]{1,0:T(8,128)(2,1)}, bf16[256,768]{1,0:T(8,128)(2,1)}, bf16[256,640]{1,0:T(8,128)(2,1)S(1)}, f32[8,128]{1,0:T(8,128)S(1)}) custom-call(s32[5]{0:T(128)S(1)} %stack.27.refs_0_.flag_ref, bf16[256,640]{1,0:T(8,128)(2,1)S(1)} %collective-permute-done.10.refs_1_, bf16[256,640]{1,0:T(8,128)(2,1)S(1)} %copy-done.10, ...), custom_call_target="tpu_custom_call" | custom-call | flops 15000000512 | bytes 24000000 | tf_op jit(solution)/shard_map/pallas_call | solution.py:31
  68.8 1.4 %collective-permute-start.15 = (bf16[256,640]{1,0:T(8,128)(2,1)}, bf16[256,640]{1,0:T(8,128)(2,1)}, u32[]{:S(2)}, u32[]{:S(2)}) collective-permute-start(bf16[256,640]{1,0:T(8,128)(2,1)} %get-tuple-element.88.refs_2_), channel_id=1, source_target_pairs={{1,2},{2,1},{5,6},{6,5},{9,10},{10,9},{13,14},{14,13},{17,18},{18,... | collective-permute-start | bytes 983048 | tf_op jit(solution)/shard_map/ppermute | solution.py:586
  70.2 0.7 copy-done.1
  70.9 1.0 copy-done.2
  71.9 2.2 %shard_map.94 = (bf16[256,640]{1,0:T(8,128)(2,1)}, bf16[256,768]{1,0:T(8,128)(2,1)S(1)}, bf16[256,1280]{1,0:T(8,128)(2,1)}, f32[8,128]{1,0:T(8,128)S(1)}) custom-call(s32[5]{0:T(128)S(1)} %stack.27.refs_0_.flag_ref, bf16[256,640]{1,0:T(8,128)(2,1)} %collective-permute-done.17.refs_1_, bf16[256,640]{1,0:T(8,128)(2,1)S(1)} %copy-done.8, ...), custom_call_target="tpu_custom_call" | custom-call | flops 15000000512 | bytes 24000000 | tf_op jit(solution)/shard_map/pallas_call | solution.py:31
  74.1 3.8 %collective-permute-start.19 = (bf16[256,768]{1,0:T(8,128)(2,1)S(1)}, bf16[256,768]{1,0:T(8,128)(2,1)}, u32[]{:S(2)}, u32[]{:S(2)}) collective-permute-start(bf16[256,768]{1,0:T(8,128)(2,1)S(1)} %get-tuple-element.99.refs_4_), channel_id=1, source_target_pairs={{0,1},{1,0},{2,3},{3,2},{4,5},{5,4},{6,7},{7,6},{8,9},{9,8},{10,11... | collective-permute-start | bytes 1179656 | tf_op jit(solution)/shard_map/ppermute | solution.py:584
  77.9 1.4 %collective-permute-start.20 = (bf16[256,640]{1,0:T(8,128)(2,1)}, bf16[256,640]{1,0:T(8,128)(2,1)}, u32[]{:S(2)}, u32[]{:S(2)}) collective-permute-start(bf16[256,640]{1,0:T(8,128)(2,1)} %get-tuple-element.100.refs_2_), channel_id=1, source_target_pairs={{1,2},{2,1},{5,6},{6,5},{9,10},{10,9},{13,14},{14,13},{17,18},{18,... | collective-permute-start | bytes 983048 | tf_op jit(solution)/shard_map/ppermute | solution.py:586
  79.3 3.5 %all-to-all-start.1 = ((bf16[4,64,1280]{2,1,0:T(8,128)(2,1)}), bf16[4,64,1280]{2,1,0:T(8,128)(2,1)S(1)}, u32[]{:S(2)}, u32[]{:S(2)}) async-start(bf16[4,64,1280]{2,1,0:T(8,128)(2,1)} %bitcast.13), calls=%async_computation.1 | async-start | bytes 1310720 | tf_op jit(solution)/shard_map/all_to_all | solution.py:474
  82.8 2.5 %shard_map.95 = (bf16[256,640]{1,0:T(8,128)(2,1)}, bf16[256,768]{1,0:T(8,128)(2,1)S(1)}, f32[64,2048]{1,0:T(8,128)S(1)}, bf16[64,2048]{1,0:T(8,128)(2,1)S(1)}, f32[8,128]{1,0:T(8,128)S(1)}) custom-call(s32[5]{0:T(128)S(1)} %stack.27.refs_0_.flag_ref, bf16[256,768]{1,0:T(8,128)(2,1)} %collective-permute-done.14.refs_1_, ...), custom_call_target="tpu_custom_call" | custom-call | flops 15000000512 | bytes 24000000 | tf_op jit(solution)/shard_map/pallas_call | solution.py:31
  85.3 2.0 %collective-permute-start.26 = (bf16[64,2048]{1,0:T(8,128)(2,1)S(1)}, bf16[64,2048]{1,0:T(8,128)(2,1)S(1)}, u32[]{:S(2)}, u32[]{:S(2)}) collective-permute-start(bf16[64,2048]{1,0:T(8,128)(2,1)S(1)} %get-tuple-element.110), channel_id=1, source_target_pairs={{0,8},{4,12},{8,0},{12,4},{1,9},{5,13},{9,1},{13,5},{2,10},{6,14},... | collective-permute-start | bytes 786440 | tf_op jit(solution)/shard_map/ppermute | solution.py:471
  87.3 1.4 %collective-permute-start.25 = (bf16[256,640]{1,0:T(8,128)(2,1)}, bf16[256,640]{1,0:T(8,128)(2,1)S(1)}, u32[]{:S(2)}, u32[]{:S(2)}) collective-permute-start(bf16[256,640]{1,0:T(8,128)(2,1)} %get-tuple-element.108.refs_2_), channel_id=1, source_target_pairs={{0,1},{1,0},{2,3},{3,2},{4,5},{5,4},{6,7},{7,6},{8,9},{9,8},{10,11... | collective-permute-start | bytes 983048 | tf_op jit(solution)/shard_map/ppermute | solution.py:584
  88.7 6.6 %shard_map.96 = (bf16[2048,2048]{1,0:T(8,128)(2,1)}, f32[8,128]{1,0:T(8,128)S(1)}) custom-call(s32[5]{0:T(128)S(1)} %stack.27.refs_0_.flag_ref, s32[16]{0:T(128)S(1)} %gather_fusion, bf16[4,2048,128]{2,1,0:T(8,128)(2,1)} %all-to-all-done.refs_1_.refs_2_, bf16[64,2048]{1,0:T(8,128)(2,1)S(1)} %copy-done.4, bf16[64,2048]{1,0:T(8,128)(2,1)S(1)} %copy-done.6, ...), custom_call_target="tpu_custom_call" | custom-call | flops 2147483648 | bytes 8388608 | tf_op jit(solution)/shard_map/pallas_call | solution.py:31
  95.3 2.0 %shard_map.97 = (bf16[256,640]{1,0:T(8,128)(2,1)S(1)}, bf16[64,1536]{1,0:T(8,128)(2,1)S(1)}, bf16[64,1536]{1,0:T(8,128)(2,1)}, bf16[64,1536]{1,0:T(8,128)(2,1)S(...) custom-call(s32[5]{0:T(128)S(1)} %stack.27.refs_0_.flag_ref, bf16[256,768]{1,0:T(8,128)(2,1)} %collective-permute-done.19.refs_1_, ...), custom_call_target="tpu_custom_call" | custom-call | flops 15000000512 | bytes 24000000 | tf_op jit(solution)/shard_map/pallas_call | solution.py:31
  98.6 1.8 %collective-permute-start.23 = (bf16[64,1536]{1,0:T(8,128)(2,1)S(1)}, bf16[64,1536]{1,0:T(8,128)(2,1)S(1)}, u32[]{:S(2)}, u32[]{:S(2)}) collective-permute-start(bf16[64,1536]{1,0:T(8,128)(2,1)S(1)} %get-tuple-element.106), channel_id=1, source_target_pairs={{0,12},{4,8},{8,4},{12,0},{1,13},{5,9},{9,5},{13,1},{2,14},{6,10},... | collective-permute-start | bytes 589832 | tf_op jit(solution)/shard_map/ppermute | solution.py:471
  100.4 3.3 %shard_map.98 = (bf16[256,512]{1,0:T(8,128)(2,1)}, f32[8,128]{1,0:T(8,128)S(1)}) custom-call(s32[5]{0:T(128)S(1)} %stack.27.refs_0_.flag_ref, bf16[2048,512]{1,0:T(8,128)(2,1)} %refs_1_.9, f32[64,2048]{1,0:T(8,128)S(1)} %get-tuple-element.109.refs_2_, bf16[64,2048]{1,0:T(8,128)(2,1)S(1)} %collective-permute-done.26.refs_3_, s32[1,2048]{1,0:T(1,128)S(1)} %bitcast.33, ...), custom_call_target="tpu_custom_call" | custom-call | flops 1 | bytes 24000000 | tf_op jit(solution)/shard_map/pallas_call | solution.py:31
  103.8 3.5 %all-to-all-start.2 = ((bf16[16,16,512]{2,1,0:T(8,128)(2,1)}), bf16[16,16,512]{2,1,0:T(8,128)(2,1)S(1)}, u32[]{:S(2)}, u32[]{:S(2)}) async-start(bf16[16,16,512]{2,1,0:T(8,128)(2,1)} %bitcast.16), calls=%async_computation.2 | async-start | bytes 524288 | tf_op jit(solution)/shard_map/all_to_all | solution.py:552
  107.3 1.0 shard_map.99
  110.0 1.7 %collective-permute-start.28 = (bf16[64,1280]{1,0:T(8,128)(2,1)S(1)}, bf16[64,1280]{1,0:T(8,128)(2,1)S(1)}, u32[]{:S(2)}, u32[]{:S(2)}) collective-permute-start(bf16[64,1280]{1,0:T(8,128)(2,1)S(1)} %get-tuple-element.117), channel_id=1, source_target_pairs={{0,8},{4,12},{8,0},{12,4},{1,9},{5,13},{9,1},{13,5},{2,10},{6,14},... | collective-permute-start | bytes 491528 | tf_op jit(solution)/shard_map/ppermute | solution.py:471
  111.7 1.6 %shard_map.101.refs_9_ = bf16[8192,128]{1,0:T(8,128)(2,1)} custom-call(s32[5]{0:T(128)S(1)} %stack.27.refs_0_.flag_ref, bf16[256,1280]{1,0:T(8,128)(2,1)S(1)} %bitcast.26, bf16[64,1536]{1,0:T(8,128)(2,1)S(1)} %copy-done.12, bf16[64,1536]{1,0:T(8,128)(2,1)S(1)} %collective-permute-done.21.refs_2_, bf16[64,1536]{1,0:T(8,128)(2,1)S(1)} %collective-permute-done.22.refs_3_, ...), custom_call_target="tpu_custom_call" | custom-call | flops 15000000512 | bytes 3145728 | tf_op jit(solution)/shard_map/pallas_call | solution.py:213
  113.4 4.0 %all-to-all-done.2 = bf16[16,16,512]{2,1,0:T(8,128)(2,1)S(1)} async-done(((bf16[16,16,512]{2,1,0:T(8,128)(2,1)}), bf16[16,16,512]{2,1,0:T(8,128)(2,1)S(1)}, u32[]{:S(2)}, u32[]{:S(2)}) %all-to-all-start.2) | async-done | bytes 262176 | tf_op jit(solution)/shard_map/all_to_all | solution.py:552
  118.2 1.1 collective-permute-start.31
  119.3 3.0 %collective-permute-start.32 = (bf16[16,2048]{1,0:T(8,128)(2,1)S(1)}, bf16[16,2048]{1,0:T(8,128)(2,1)S(1)}, u32[]{:S(2)}, u32[]{:S(2)}) collective-permute-start(bf16[16,2048]{1,0:T(8,128)(2,1)S(1)} %get-tuple-element.121.refs_1_), channel_id=1, source_target_pairs={{0,3},{1,2},{2,1},{3,0},{4,7},{5,6},{6,5},{7,4},{8,11},{9,10},{10,... | collective-permute-start | bytes 196616 | tf_op jit(solution)/shard_map/ppermute | solution.py:591
  122.3 1.9 %shard_map.102 = bf16[8192,128]{1,0:T(8,128)(2,1)} custom-call(s32[5]{0:T(128)S(1)} %stack.27.refs_0_.flag_ref, bf16[256,1280]{1,0:T(8,128)(2,1)S(1)} %bitcast.27, bf16[64,1536]{1,0:T(8,128)(2,1)S(1)} %copy-done.12, bf16[64,1536]{1,0:T(8,128)(2,1)S(1)} %collective-permute-done.21.refs_2_, ...), custom_call_target="tpu_custom_call", output_to_operand_aliasing={{}: (10, {})} | custom-call | flops 15000000512 | bytes 5242880 | tf_op jit(solution)/shard_map/pallas_call | solution.py:213
  124.2 2.3 %collective-permute-done.31.refs_3_ = bf16[16,2048]{1,0:T(8,128)(2,1)S(1)} collective-permute-done((bf16[16,2048]{1,0:T(8,128)(2,1)S(1)}, bf16[16,2048]{1,0:T(8,128)(2,1)S(1)}, u32[]{:S(2)}, u32[]{:S(2)}) %collective-permute-start.31) | collective-permute-done | bytes 65568 | tf_op jit(solution)/shard_map/ppermute | solution.py:591
  126.6 1.3 shard_map.104
  (81 shorter events, 10.7 us)
Async XLA Ops:
  0.6 4.9 %copy-start = (s32[4]{0:T(128)S(1)}, s32[4]{0:T(128)}, u32[]{:S(2)}) copy-start(s32[4]{0:T(128)} %param.9) | copy-start | bytes 52
  1.6 4.6 %collective-permute-start = (bf16[64,512]{1,0:T(8,128)(2,1)S(1)}, bf16[64,512]{1,0:T(8,128)(2,1)S(1)}, u32[]{:S(2)}, u32[]{:S(2)}) collective-permute-start(bf16[64,512]{1,0:T(8,128)(2,1)S(1)} %get-tuple-element.124), channel_id=1, source_target_pairs={{0,4},{4,0},{8,12},{12,8},{1,5},{5,1},{9,13},{13,9},{2,6},{6,2},{1... | collective-permute-start | bytes 196616 | tf_op jit(solution)/shard_map/ppermute | solution.py:471
  2.2 5.3 %collective-permute-start.1 = (bf16[64,512]{1,0:T(8,128)(2,1)S(1)}, bf16[64,512]{1,0:T(8,128)(2,1)S(1)}, u32[]{:S(2)}, u32[]{:S(2)}) collective-permute-start(bf16[64,512]{1,0:T(8,128)(2,1)S(1)} %get-tuple-element.126), channel_id=1, source_target_pairs={{0,8},{4,12},{8,0},{12,4},{1,9},{5,13},{9,1},{13,5},{2,10},{6,14},... | collective-permute-start | bytes 196616 | tf_op jit(solution)/shard_map/ppermute | solution.py:471
  4.7 4.0 %collective-permute-start.2 = (bf16[64,512]{1,0:T(8,128)(2,1)S(1)}, bf16[64,512]{1,0:T(8,128)(2,1)S(1)}, u32[]{:S(2)}, u32[]{:S(2)}) collective-permute-start(bf16[64,512]{1,0:T(8,128)(2,1)S(1)} %get-tuple-element.125), channel_id=1, source_target_pairs={{0,12},{4,8},{8,4},{12,0},{1,13},{5,9},{9,5},{13,1},{2,14},{6,10},... | collective-permute-start | bytes 196616 | tf_op jit(solution)/shard_map/ppermute | solution.py:471
  12.1 2.0 %collective-permute-start.3 = (f32[64,2048]{1,0:T(8,128)S(1)}, f32[64,2048]{1,0:T(8,128)S(1)}, u32[]{:S(2)}, u32[]{:S(2)}) collective-permute-start(f32[64,2048]{1,0:T(8,128)S(1)} %get-tuple-element.63.refs_2_), channel_id=1, source_target_pairs={{0,4},{4,0},{8,12},{12,8},{1,5},{5,1},{9,13},{13,9},{2,6},{6,2},{1... | collective-permute-start | bytes 1572872 | tf_op jit(solution)/shard_map/ppermute | solution.py:471
  18.0 12.9 %collective-permute-start.7 = (bf16[256,640]{1,0:T(8,128)(2,1)S(1)}, bf16[256,640]{1,0:T(8,128)(2,1)S(1)}, u32[]{:S(2)}, u32[]{:S(2)}) collective-permute-start(bf16[256,640]{1,0:T(8,128)(2,1)S(1)} %get-tuple-element.72.refs_3_), channel_id=1, source_target_pairs={{0,1},{1,0},{2,3},{3,2},{4,5},{5,4},{6,7},{7,6},{8,9},{9,8},{10,11... | collective-permute-start | bytes 983048 | tf_op jit(solution)/shard_map/ppermute | solution.py:584
  19.6 6.3 %collective-permute-start.4 = (bf16[64,1024]{1,0:T(8,128)(2,1)S(1)}, bf16[64,1024]{1,0:T(8,128)(2,1)S(1)}, u32[]{:S(2)}, u32[]{:S(2)}) collective-permute-start(bf16[64,1024]{1,0:T(8,128)(2,1)S(1)} %get-tuple-element.67), channel_id=1, source_target_pairs={{0,8},{4,12},{8,0},{12,4},{1,9},{5,13},{9,1},{13,5},{2,10},{6,14},... | collective-permute-start | bytes 393224 | tf_op jit(solution)/shard_map/ppermute | solution.py:471
  25.4 9.9 %collective-permute-start.6 = (bf16[256,640]{1,0:T(8,128)(2,1)S(1)}, bf16[256,640]{1,0:T(8,128)(2,1)S(1)}, u32[]{:S(2)}, u32[]{:S(2)}) collective-permute-start(bf16[256,640]{1,0:T(8,128)(2,1)S(1)} %get-tuple-element.70.refs_6_), channel_id=1, source_target_pairs={{0,1},{1,0},{2,3},{3,2},{4,5},{5,4},{6,7},{7,6},{8,9},{9,8},{10,11... | collective-permute-start | bytes 983048 | tf_op jit(solution)/shard_map/ppermute | solution.py:584
  25.9 35.6 %all-to-all-start = ((bf16[4,2048,128]{2,1,0:T(8,128)(2,1)}), bf16[4,2048,128]{2,1,0:T(8,128)(2,1)}, u32[]{:S(2)}, u32[]{:S(2)}) async-start(bf16[4,2048,128]{2,1,0:T(8,128)(2,1)} %bitcast.34), calls=%async_computation | async-start | bytes 4194304 | tf_op jit(solution)/shard_map/all_to_all | solution.py:474
  30.4 3.4 %collective-permute-start.5 = (bf16[64,1024]{1,0:T(8,128)(2,1)S(1)}, bf16[64,1024]{1,0:T(8,128)(2,1)S(1)}, u32[]{:S(2)}, u32[]{:S(2)}) collective-permute-start(bf16[64,1024]{1,0:T(8,128)(2,1)S(1)} %collective-permute-done.4.refs_3_), channel_id=1, source_target_pairs={{0,4},{4,0},{8,12},{12,8},{1,5},{5,1},{9,13},{13,9},{2,6},{6,2},{1... | collective-permute-start | bytes 393224 | tf_op jit(solution)/shard_map/ppermute | solution.py:471
  31.5 12.2 %collective-permute-start.8 = (bf16[256,768]{1,0:T(8,128)(2,1)S(1)}, bf16[256,768]{1,0:T(8,128)(2,1)S(1)}, u32[]{:S(2)}, u32[]{:S(2)}) collective-permute-start(bf16[256,768]{1,0:T(8,128)(2,1)S(1)} %get-tuple-element.75), channel_id=1, source_target_pairs={{0,1},{1,0},{2,3},{3,2},{4,5},{5,4},{6,7},{7,6},{8,9},{9,8},{10,11... | collective-permute-start | bytes 1179656 | tf_op jit(solution)/shard_map/ppermute | solution.py:584
  33.1 9.1 %collective-permute-start.9 = (bf16[256,640]{1,0:T(8,128)(2,1)S(1)}, bf16[256,640]{1,0:T(8,128)(2,1)S(1)}, u32[]{:S(2)}, u32[]{:S(2)}) collective-permute-start(bf16[256,640]{1,0:T(8,128)(2,1)S(1)} %get-tuple-element.76.refs_6_), channel_id=1, source_target_pairs={{1,2},{2,1},{5,6},{6,5},{9,10},{10,9},{13,14},{14,13},{17,18},{18,... | collective-permute-start | bytes 983048 | tf_op jit(solution)/shard_map/ppermute | solution.py:586
  38.6 15.4 %copy-start.5 = (bf16[64,2048]{1,0:T(8,128)(2,1)}, bf16[64,2048]{1,0:T(8,128)(2,1)S(1)}, u32[]{:S(2)}) copy-start(bf16[64,2048]{1,0:T(8,128)(2,1)S(1)} %get-tuple-element.74.refs_3_.refs_4_) | copy-start | bytes 786436
  38.6 15.3 %collective-permute-start.12 = (bf16[256,768]{1,0:T(8,128)(2,1)S(1)}, bf16[256,768]{1,0:T(8,128)(2,1)S(1)}, u32[]{:S(2)}, u32[]{:S(2)}) collective-permute-start(bf16[256,768]{1,0:T(8,128)(2,1)S(1)} %get-tuple-element.81), channel_id=1, source_target_pairs={{0,1},{1,0},{2,3},{3,2},{4,5},{5,4},{6,7},{7,6},{8,9},{9,8},{10,11... | collective-permute-start | bytes 1179656 | tf_op jit(solution)/shard_map/ppermute | solution.py:584
  41.6 12.3 %collective-permute-start.13 = (bf16[256,640]{1,0:T(8,128)(2,1)S(1)}, bf16[256,640]{1,0:T(8,128)(2,1)S(1)}, u32[]{:S(2)}, u32[]{:S(2)}) collective-permute-start(bf16[256,640]{1,0:T(8,128)(2,1)S(1)} %get-tuple-element.83.refs_6_), channel_id=1, source_target_pairs={{1,2},{2,1},{5,6},{6,5},{9,10},{10,9},{13,14},{14,13},{17,18},{18,... | collective-permute-start | bytes 983048 | tf_op jit(solution)/shard_map/ppermute | solution.py:586
  46.9 11.0 %copy-start.9 = (bf16[256,640]{1,0:T(8,128)(2,1)}, bf16[256,640]{1,0:T(8,128)(2,1)S(1)}, u32[]{:S(2)}) copy-start(bf16[256,640]{1,0:T(8,128)(2,1)S(1)} %get-tuple-element.79.refs_2_) | copy-start | bytes 983044
  46.9 20.2 %collective-permute-start.11 = (bf16[256,768]{1,0:T(8,128)(2,1)S(1)}, bf16[256,768]{1,0:T(8,128)(2,1)S(1)}, u32[]{:S(2)}, u32[]{:S(2)}) collective-permute-start(bf16[256,768]{1,0:T(8,128)(2,1)S(1)} %get-tuple-element.80.refs_3_), channel_id=1, source_target_pairs={{1,2},{2,1},{5,6},{6,5},{9,10},{10,9},{13,14},{14,13},{17,18},{18,... | collective-permute-start | bytes 1179656 | tf_op jit(solution)/shard_map/ppermute | solution.py:586
  47.6 19.5 %collective-permute-start.10 = (bf16[256,640]{1,0:T(8,128)(2,1)S(1)}, bf16[256,640]{1,0:T(8,128)(2,1)S(1)}, u32[]{:S(2)}, u32[]{:S(2)}) collective-permute-start(bf16[256,640]{1,0:T(8,128)(2,1)S(1)} %get-tuple-element.78.refs_5_), channel_id=1, source_target_pairs={{0,1},{1,0},{2,3},{3,2},{4,5},{5,4},{6,7},{7,6},{8,9},{9,8},{10,11... | collective-permute-start | bytes 983048 | tf_op jit(solution)/shard_map/ppermute | solution.py:584
  57.9 0.7 copy-start.7
  58.6 11.6 %collective-permute-start.18 = (bf16[256,768]{1,0:T(8,128)(2,1)S(1)}, bf16[256,768]{1,0:T(8,128)(2,1)S(1)}, u32[]{:S(2)}, u32[]{:S(2)}) collective-permute-start(bf16[256,768]{1,0:T(8,128)(2,1)S(1)} %get-tuple-element.92.refs_3_), channel_id=1, source_target_pairs={{1,2},{2,1},{5,6},{6,5},{9,10},{10,9},{13,14},{14,13},{17,18},{18,... | collective-permute-start | bytes 1179656 | tf_op jit(solution)/shard_map/ppermute | solution.py:586
  59.3 10.9 %collective-permute-start.17 = (bf16[256,640]{1,0:T(8,128)(2,1)}, bf16[256,640]{1,0:T(8,128)(2,1)}, u32[]{:S(2)}, u32[]{:S(2)}) collective-permute-start(bf16[256,640]{1,0:T(8,128)(2,1)} %get-tuple-element.90.refs_5_), channel_id=1, source_target_pairs={{0,1},{1,0},{2,3},{3,2},{4,5},{5,4},{6,7},{7,6},{8,9},{9,8},{10,11... | collective-permute-start | bytes 983048 | tf_op jit(solution)/shard_map/ppermute | solution.py:584
  61.5 5.7 %copy-start.10 = (bf16[256,640]{1,0:T(8,128)(2,1)S(1)}, bf16[256,640]{1,0:T(8,128)(2,1)}, u32[]{:S(2)}) copy-start(bf16[256,640]{1,0:T(8,128)(2,1)} %copy-done.9) | copy-start | bytes 983044
  67.2 3.7 %copy-start.8 = (bf16[256,640]{1,0:T(8,128)(2,1)S(1)}, bf16[256,640]{1,0:T(8,128)(2,1)}, u32[]{:S(2)}) copy-start(bf16[256,640]{1,0:T(8,128)(2,1)} %copy-done.7) | copy-start | bytes 983044
  68.7 14.1 %collective-permute-start.14 = (bf16[256,768]{1,0:T(8,128)(2,1)}, bf16[256,768]{1,0:T(8,128)(2,1)}, u32[]{:S(2)}, u32[]{:S(2)}) collective-permute-start(bf16[256,768]{1,0:T(8,128)(2,1)} %get-tuple-element.87.refs_4_), channel_id=1, source_target_pairs={{0,1},{1,0},{2,3},{3,2},{4,5},{5,4},{6,7},{7,6},{8,9},{9,8},{10,11... | collective-permute-start | bytes 1179656 | tf_op jit(solution)/shard_map/ppermute | solution.py:584
  68.8 14.0 %collective-permute-start.15 = (bf16[256,640]{1,0:T(8,128)(2,1)}, bf16[256,640]{1,0:T(8,128)(2,1)}, u32[]{:S(2)}, u32[]{:S(2)}) collective-permute-start(bf16[256,640]{1,0:T(8,128)(2,1)} %get-tuple-element.88.refs_2_), channel_id=1, source_target_pairs={{1,2},{2,1},{5,6},{6,5},{9,10},{10,9},{13,14},{14,13},{17,18},{18,... | collective-permute-start | bytes 983048 | tf_op jit(solution)/shard_map/ppermute | solution.py:586
  70.2 12.6 %collective-permute-start.16 = (f32[128,2048]{1,0:T(8,128)S(1)}, f32[128,2048]{1,0:T(8,128)S(1)}, u32[]{:S(2)}, u32[]{:S(2)}) collective-permute-start(f32[128,2048]{1,0:T(8,128)S(1)} %get-tuple-element.89.refs_5_), channel_id=1, source_target_pairs={{0,4},{4,0},{8,12},{12,8},{1,5},{5,1},{9,13},{13,9},{2,6},{6,2},{1... | collective-permute-start | bytes 3145736 | tf_op jit(solution)/shard_map/ppermute | solution.py:471
  70.2 0.7 copy-start.1
  70.9 1.0 copy-start.2
  74.1 21.1 %collective-permute-start.19 = (bf16[256,768]{1,0:T(8,128)(2,1)S(1)}, bf16[256,768]{1,0:T(8,128)(2,1)}, u32[]{:S(2)}, u32[]{:S(2)}) collective-permute-start(bf16[256,768]{1,0:T(8,128)(2,1)S(1)} %get-tuple-element.99.refs_4_), channel_id=1, source_target_pairs={{0,1},{1,0},{2,3},{3,2},{4,5},{5,4},{6,7},{7,6},{8,9},{9,8},{10,11... | collective-permute-start | bytes 1179656 | tf_op jit(solution)/shard_map/ppermute | solution.py:584
  77.9 17.4 %collective-permute-start.20 = (bf16[256,640]{1,0:T(8,128)(2,1)}, bf16[256,640]{1,0:T(8,128)(2,1)}, u32[]{:S(2)}, u32[]{:S(2)}) collective-permute-start(bf16[256,640]{1,0:T(8,128)(2,1)} %get-tuple-element.100.refs_2_), channel_id=1, source_target_pairs={{1,2},{2,1},{5,6},{6,5},{9,10},{10,9},{13,14},{14,13},{17,18},{18,... | collective-permute-start | bytes 983048 | tf_op jit(solution)/shard_map/ppermute | solution.py:586
  79.3 24.5 %all-to-all-start.1 = ((bf16[4,64,1280]{2,1,0:T(8,128)(2,1)}), bf16[4,64,1280]{2,1,0:T(8,128)(2,1)S(1)}, u32[]{:S(2)}, u32[]{:S(2)}) async-start(bf16[4,64,1280]{2,1,0:T(8,128)(2,1)} %bitcast.13), calls=%async_computation.1 | async-start | bytes 1310720 | tf_op jit(solution)/shard_map/all_to_all | solution.py:474
  82.8 5.9 %copy-start.4 = (bf16[64,2048]{1,0:T(8,128)(2,1)S(1)}, bf16[64,2048]{1,0:T(8,128)(2,1)}, u32[]{:S(2)}) copy-start(bf16[64,2048]{1,0:T(8,128)(2,1)} %copy-done.3) | copy-start | bytes 786436
  82.8 5.9 %copy-start.6 = (bf16[64,2048]{1,0:T(8,128)(2,1)S(1)}, bf16[64,2048]{1,0:T(8,128)(2,1)}, u32[]{:S(2)}) copy-start(bf16[64,2048]{1,0:T(8,128)(2,1)} %copy-done.5) | copy-start | bytes 786436
  85.3 13.3 %collective-permute-start.26 = (bf16[64,2048]{1,0:T(8,128)(2,1)S(1)}, bf16[64,2048]{1,0:T(8,128)(2,1)S(1)}, u32[]{:S(2)}, u32[]{:S(2)}) collective-permute-start(bf16[64,2048]{1,0:T(8,128)(2,1)S(1)} %get-tuple-element.110), channel_id=1, source_target_pairs={{0,8},{4,12},{8,0},{12,4},{1,9},{5,13},{9,1},{13,5},{2,10},{6,14},... | collective-permute-start | bytes 786440 | tf_op jit(solution)/shard_map/ppermute | solution.py:471
  87.3 20.0 %collective-permute-start.25 = (bf16[256,640]{1,0:T(8,128)(2,1)}, bf16[256,640]{1,0:T(8,128)(2,1)S(1)}, u32[]{:S(2)}, u32[]{:S(2)}) collective-permute-start(bf16[256,640]{1,0:T(8,128)(2,1)} %get-tuple-element.108.refs_2_), channel_id=1, source_target_pairs={{0,1},{1,0},{2,3},{3,2},{4,5},{5,4},{6,7},{7,6},{8,9},{9,8},{10,11... | collective-permute-start | bytes 983048 | tf_op jit(solution)/shard_map/ppermute | solution.py:584
  97.9 10.4 %collective-permute-start.24 = (bf16[256,640]{1,0:T(8,128)(2,1)S(1)}, bf16[256,640]{1,0:T(8,128)(2,1)S(1)}, u32[]{:S(2)}, u32[]{:S(2)}) collective-permute-start(bf16[256,640]{1,0:T(8,128)(2,1)S(1)} %get-tuple-element.107.refs_2_), channel_id=1, source_target_pairs={{0,1},{1,0},{2,3},{3,2},{4,5},{5,4},{6,7},{7,6},{8,9},{9,8},{10,11... | collective-permute-start | bytes 983048 | tf_op jit(solution)/shard_map/ppermute | solution.py:584
  98.6 13.1 %collective-permute-start.21 = (bf16[64,1536]{1,0:T(8,128)(2,1)}, bf16[64,1536]{1,0:T(8,128)(2,1)S(1)}, u32[]{:S(2)}, u32[]{:S(2)}) collective-permute-start(bf16[64,1536]{1,0:T(8,128)(2,1)} %get-tuple-element.104), channel_id=1, source_target_pairs={{0,4},{4,0},{8,12},{12,8},{1,5},{5,1},{9,13},{13,9},{2,6},{6,2},{1... | collective-permute-start | bytes 589832 | tf_op jit(solution)/shard_map/ppermute | solution.py:471
  98.6 13.1 %collective-permute-start.22 = (bf16[64,1536]{1,0:T(8,128)(2,1)S(1)}, bf16[64,1536]{1,0:T(8,128)(2,1)S(1)}, u32[]{:S(2)}, u32[]{:S(2)}) collective-permute-start(bf16[64,1536]{1,0:T(8,128)(2,1)S(1)} %get-tuple-element.105), channel_id=1, source_target_pairs={{0,8},{4,12},{8,0},{12,4},{1,9},{5,13},{9,1},{13,5},{2,10},{6,14},... | collective-permute-start | bytes 589832 | tf_op jit(solution)/shard_map/ppermute | solution.py:471
  98.6 13.1 %collective-permute-start.23 = (bf16[64,1536]{1,0:T(8,128)(2,1)S(1)}, bf16[64,1536]{1,0:T(8,128)(2,1)S(1)}, u32[]{:S(2)}, u32[]{:S(2)}) collective-permute-start(bf16[64,1536]{1,0:T(8,128)(2,1)S(1)} %get-tuple-element.106), channel_id=1, source_target_pairs={{0,12},{4,8},{8,4},{12,0},{1,13},{5,9},{9,5},{13,1},{2,14},{6,10},... | collective-permute-start | bytes 589832 | tf_op jit(solution)/shard_map/ppermute | solution.py:471
  103.8 13.6 %all-to-all-start.2 = ((bf16[16,16,512]{2,1,0:T(8,128)(2,1)}), bf16[16,16,512]{2,1,0:T(8,128)(2,1)S(1)}, u32[]{:S(2)}, u32[]{:S(2)}) async-start(bf16[16,16,512]{2,1,0:T(8,128)(2,1)} %bitcast.16), calls=%async_computation.2 | async-start | bytes 524288 | tf_op jit(solution)/shard_map/all_to_all | solution.py:552
  108.4 3.4 %copy-start.12 = (bf16[64,1536]{1,0:T(8,128)(2,1)S(1)}, bf16[64,1536]{1,0:T(8,128)(2,1)}, u32[]{:S(2)}) copy-start(bf16[64,1536]{1,0:T(8,128)(2,1)} %copy-done.11) | copy-start | bytes 589828
  109.7 9.7 %collective-permute-start.27 = (bf16[64,1280]{1,0:T(8,128)(2,1)S(1)}, bf16[64,1280]{1,0:T(8,128)(2,1)S(1)}, u32[]{:S(2)}, u32[]{:S(2)}) collective-permute-start(bf16[64,1280]{1,0:T(8,128)(2,1)S(1)} %get-tuple-element.116), channel_id=1, source_target_pairs={{0,4},{4,0},{8,12},{12,8},{1,5},{5,1},{9,13},{13,9},{2,6},{6,2},{1... | collective-permute-start | bytes 491528 | tf_op jit(solution)/shard_map/ppermute | solution.py:471
  110.0 12.4 %collective-permute-start.28 = (bf16[64,1280]{1,0:T(8,128)(2,1)S(1)}, bf16[64,1280]{1,0:T(8,128)(2,1)S(1)}, u32[]{:S(2)}, u32[]{:S(2)}) collective-permute-start(bf16[64,1280]{1,0:T(8,128)(2,1)S(1)} %get-tuple-element.117), channel_id=1, source_target_pairs={{0,8},{4,12},{8,0},{12,4},{1,9},{5,13},{9,1},{13,5},{2,10},{6,14},... | collective-permute-start | bytes 491528 | tf_op jit(solution)/shard_map/ppermute | solution.py:471
  111.7 10.6 %collective-permute-start.29 = (bf16[64,1280]{1,0:T(8,128)(2,1)S(1)}, bf16[64,1280]{1,0:T(8,128)(2,1)S(1)}, u32[]{:S(2)}, u32[]{:S(2)}) collective-permute-start(bf16[64,1280]{1,0:T(8,128)(2,1)S(1)} %get-tuple-element.118), channel_id=1, source_target_pairs={{0,12},{4,8},{8,4},{12,0},{1,13},{5,9},{9,5},{13,1},{2,14},{6,10},... | collective-permute-start | bytes 491528 | tf_op jit(solution)/shard_map/ppermute | solution.py:471
  111.7 10.6 %copy-start.14 = (bf16[64,1280]{1,0:T(8,128)(2,1)S(1)}, bf16[64,1280]{1,0:T(8,128)(2,1)}, u32[]{:S(2)}) copy-start(bf16[64,1280]{1,0:T(8,128)(2,1)} %copy-done.13) | copy-start | bytes 491524
  117.9 6.3 %collective-permute-start.30 = (bf16[16,2048]{1,0:T(8,128)(2,1)S(1)}, bf16[16,2048]{1,0:T(8,128)(2,1)S(1)}, u32[]{:S(2)}, u32[]{:S(2)}) collective-permute-start(bf16[16,2048]{1,0:T(8,128)(2,1)S(1)} %get-tuple-element.121.refs_1_), channel_id=1, source_target_pairs={{0,1},{1,0},{2,3},{3,2},{4,5},{5,4},{6,7},{7,6},{8,9},{9,8},{10,11... | collective-permute-start | bytes 196616 | tf_op jit(solution)/shard_map/ppermute | solution.py:591
  118.2 8.3 %collective-permute-start.31 = (bf16[16,2048]{1,0:T(8,128)(2,1)S(1)}, bf16[16,2048]{1,0:T(8,128)(2,1)S(1)}, u32[]{:S(2)}, u32[]{:S(2)}) collective-permute-start(bf16[16,2048]{1,0:T(8,128)(2,1)S(1)} %get-tuple-element.121.refs_1_), channel_id=1, source_target_pairs={{0,2},{1,3},{2,0},{3,1},{4,6},{5,7},{6,4},{7,5},{8,10},{9,11},{10,... | collective-permute-start | bytes 196616 | tf_op jit(solution)/shard_map/ppermute | solution.py:591
  119.3 7.2 %collective-permute-start.32 = (bf16[16,2048]{1,0:T(8,128)(2,1)S(1)}, bf16[16,2048]{1,0:T(8,128)(2,1)S(1)}, u32[]{:S(2)}, u32[]{:S(2)}) collective-permute-start(bf16[16,2048]{1,0:T(8,128)(2,1)S(1)} %get-tuple-element.121.refs_1_), channel_id=1, source_target_pairs={{0,3},{1,2},{2,1},{3,0},{4,7},{5,6},{6,5},{7,4},{8,11},{9,10},{10,... | collective-permute-start | bytes 196616 | tf_op jit(solution)/shard_map/ppermute | solution.py:591
  (3 other events, 2.1 us)

commit v5 on v4

--- a/solution.py
+++ b/solution.py
@@ -17,8 +17,8 @@
 (
     PART, FROM_LINE, OLD_PART, INNER, OLD_INNER, FROM_INNER, LINE, OLD_LINE, FINAL, FINALS,
     OLD_FINAL, WIDE, KEEP, SEND, SHRUNK_MINE, SHRUNK_THEIRS, KEPT, CAME, SLOT_ROWS,
-    HALF_MINE, HALF_THEIRS, D_OTHER, RANK, MARK,
-) = range(24)
+    MARK,
+) = range(20)
 
 
 def launch(body, args, specs, outs, out_specs, scratch, mib, flops, moved, marks, grid=()):
@@ -138,6 +138,41 @@
         10,
         2 * rows * count * R * width,
         rows * width * 2,
+        marks,
+    )
+
+
+def other_call(flags, slot_rows, mine, theirs, acts, tiles, count, marks):
+    rows = acts.shape[0]
+    n = len(tiles)
+    total = sum(width for _, width in tiles)
+
+    def body(flag_ref, slot_ref, mine_ref, theirs_ref, acts_ref, *refs):
+        rank_ref, lhs = refs[n], refs[n + 1]
+        held, sems = refs[n + 2 :: 2], refs[n + 3 :: 2]
+        copies = [
+            tile_copies(acts_ref, held[i], sems[i], start) for i, (start, _) in enumerate(tiles)
+        ]
+        odd = flag_ref[ODD] == 1
+        a, b = mine_ref[...].astype(F32), theirs_ref[...].astype(F32)
+        rank = jnp.concatenate([jnp.where(odd, b, a), jnp.where(odd, a, b)], axis=1)
+        rank_ref[...] = rank.astype(BF)
+        masked(slot_ref[...], rank, count, lhs)
+        for i in range(n):
+            refs[i][...] = tile_dot(lhs, held[i], copies[i])
+
+    return launch(
+        body,
+        (flags, slot_rows, mine, theirs, acts),
+        (SCALARS, WHOLE, WHOLE, WHOLE, FAR),
+        [jax.ShapeDtypeStruct((count * R, width), BF) for _, width in tiles]
+        + [jax.ShapeDtypeStruct((R, rows), BF)],
+        [WHOLE] * (n + 1),
+        [pltpu.VMEM((count * R, rows), BF)]
+        + [x for _, width in tiles for x in tile_scratch(rows, width)],
+        16,
+        2 * rows * count * R * total,
+        rows * total * 2,
         marks,
     )
 
@@ -336,24 +371,15 @@
             put[SEND][...] = jnp.where(upper, key, value).astype(BF)
         if start is not None:
             lhs = rest[0]
-            if HALF_MINE in got:
-                odd = flag_ref[ODD] == 1
-                a, b = got[HALF_MINE][...].astype(F32), got[HALF_THEIRS][...].astype(F32)
-                rank = jnp.concatenate([jnp.where(odd, b, a), jnp.where(odd, a, b)], axis=1)
-                put[D_OTHER][...] = rank.astype(BF)
-            elif KEPT in got:
-                rank = got[KEPT][...] + got[CAME][...].astype(F32)
-            else:
-                rank = got[RANK][...].astype(F32)
+            rank = got[KEPT][...] + got[CAME][...].astype(F32)
             masked(got[SLOT_ROWS][...], rank, count, lhs)
             put[PART][...] = tile_dot(lhs, held, copies)
         if LINE in put:
-            if OLD_INNER in got and (PART in got or start is not None):
-                part = got[PART] if PART in got else put[PART]
+            if OLD_INNER in got and PART in got:
 
                 @pl.when(edge)
                 def _():
-                    put[LINE][...] = part[...]
+                    put[LINE][...] = got[PART][...]
 
                 @pl.when(inside)
                 def _():
@@ -362,7 +388,7 @@
             elif OLD_INNER in got:
                 put[LINE][...] = add(OLD_INNER, FROM_INNER)
             else:
-                put[LINE][...] = got.get(PART, put.get(PART))[...]
+                put[LINE][...] = got[PART][...]
     made = launch(
         body,
         (flags, *arrays.values()),
@@ -484,7 +510,7 @@
     back_peer = swap(back_part, 1)
 
     unit = width // 16
-    sizes = [5 * unit, 5 * unit, 6 * unit, 6 * unit, 5 * unit, 5 * unit]
+    sizes = [k * unit for k in (6, 5, 5, 5, 6, 5)]
     n = len(sizes)
     per_kind = n // 2
     starts = [sum(sizes[:c]) % width for c in range(n)]
@@ -504,21 +530,19 @@
     pools = [pltpu.with_memory_space_constraint(pool, pltpu.HBM)]
 
     for t in range(n + 6):
+        if t in (per_kind, per_kind + 1):
+            which = range(t, t + 1) if t == per_kind else range(t, n)
+            *more, d_other, mark = other_call(
+                flags, slot_rows, came_half, came_other, acts,
+                [(starts[c], sizes[c]) for c in which], count, [mark],
+            )
+            parts.update(zip(which, more))
         if t < 2:
             line[t] = parts[t]
         else:
             arrays, outs, start = {}, {}, None
             if t < n and t in parts:
                 arrays[PART] = parts[t]
-            elif t < n:
-                start = starts[t]
-                arrays[WIDE], arrays[SLOT_ROWS] = acts, slot_rows
-                outs[PART] = (tenants, sizes[t])
-                if t == per_kind:
-                    arrays[HALF_MINE], arrays[HALF_THEIRS] = came_half, came_other
-                    outs[D_OTHER] = (R, rows)
-                else:
-                    arrays[RANK] = d_other
             arrays[FROM_LINE] = from_line[t - 2]
             if t - 2 < n:
                 arrays[OLD_PART] = parts[t - 2]
@@ -562,8 +586,6 @@
             mark = made[MARK]
             if PART in made and t < n:
                 parts[t] = made[PART]
-            if t == per_kind:
-                d_other = made[D_OTHER]
             if INNER in made:
                 inner[t] = made[INNER]
             if LINE in made:

time: 129 us -> 124 us (0.961)
  local copies, waits for them, and re-layouts: 6.32 us -> 3.51 us
  waiting for transfers between devices: 13.6 us -> 12 us
    unnamed x30 -> x22, local copies, waits for them, and re-layouts: 4.54 us -> 1.73 us
    ppermute x10, waiting for transfers between devices: 2.92 us -> 0.3 us  [local(): from_line[t] = lax.ppermute(line[t], 'dp', [(0, 1), (1, 0), (2, 3), (3, 2)])]
    ppermute x10, starting transfers between devices: 21.1 us -> 19.7 us  [local(): from_line[t] = lax.ppermute(line[t], 'dp', [(0, 1), (1, 0), (2, 3), (3, 2)])]
    pallas_call x18 -> x20, Pallas kernels: 49.1 us -> 49.1 us  [launch(): pl.pallas_call(kernel, grid=grid, out_shape=[*outs, jax.ShapeDtypeStruct(...]
  transfers between devices with their start and end apart: 36 -> 36, of which waited for: 7 -> 6; matrix products, arithmetic and copies ran while one was open for 1% -> 1% of each run, Pallas kernels for 35% -> 36%
where the time goes in v5:
time: 124 us; the launch traced here: 123 us
  starting transfers between devices  53.5 us (43%)
  Pallas kernels  52.6 us (42%)
  waiting for transfers between devices  12 us (10%)
  local copies, waits for them, and re-layouts  3.51 us (3%)
    pallas_call x20, Pallas kernels, launch(): pl.pallas_call(kernel, grid=grid, out_shape=[*outs, jax.ShapeDtypeStruct(...  49.1 us
    ppermute x10, starting transfers between devices, local(): from_line[t] = lax.ppermute(line[t], 'dp', [(0, 1), (1, 0), (2, 3), (3, 2)])  19.7 us
    ppermute x14, starting transfers between devices, swap(): return lax.ppermute(x, 'adapter', [(i, i ^ m) for i in range(count)])  11.1 us
    all_to_all x2, starting transfers between devices, to_owner(): return lax.all_to_all(x, 'adapter', split_axis=0, concat_axis=0, tiled=True)  7.94 us
    ppermute x6, starting transfers between devices, local(): from_inner[t] = lax.ppermute(inner[t], 'dp', [(1, 2), (2, 1)])  6.2 us
    all_to_all x1, waiting for transfers between devices, local(): lax.all_to_all(up, ('adapter', 'dp'), split_axis=0, concat_axis=0, tiled=...  5.05 us
    ppermute x3, starting transfers between devices, local(): lax.ppermute(up_rows, 'dp', [(i, i ^ m) for i in range(dp)])  4.39 us
    ppermute x14, waiting for transfers between devices, swap(): return lax.ppermute(x, 'adapter', [(i, i ^ m) for i in range(count)])  4.33 us
  transfers between devices with their start and end apart: 36, of which 6 were waited for; matrix products, arithmetic and copies ran while one was open for 1% of the time, Pallas kernels for 36%

profile of v5, /device:TPU:0, one launch (start us, length us, event | category | flops | bytes accessed | tf_op | source)
XLA Modules:
  0.0 123.4 jit_solution(1699891178792842707)
XLA Ops:
  0.7 1.0 dynamic-slice_bitcast_fusion.3
  2.2 2.6 %collective-permute-start.1 = (bf16[64,512]{1,0:T(8,128)(2,1)S(1)}, bf16[64,512]{1,0:T(8,128)(2,1)S(1)}, u32[]{:S(2)}, u32[]{:S(2)}) collective-permute-start(bf16[64,512]{1,0:T(8,128)(2,1)S(1)} %get-tuple-element.130), channel_id=1, source_target_pairs={{0,8},{4,12},{8,0},{12,4},{1,9},{5,13},{9,1},{13,5},{2,10},{6,14},... | collective-permute-start | bytes 196616 | tf_op jit(solution)/shard_map/ppermute | solution.py:497
  4.8 0.7 fusion
  5.5 0.7 gather_fusion
  6.2 1.2 collective-permute-done.1
  7.4 1.4 %collective-permute-done.2 = bf16[64,512]{1,0:T(8,128)(2,1)S(1)} collective-permute-done((bf16[64,512]{1,0:T(8,128)(2,1)S(1)}, bf16[64,512]{1,0:T(8,128)(2,1)S(1)}, u32[]{:S(2)}, u32[]{:S(2)}) %collective-permute-start.2) | collective-permute-done | bytes 65568 | tf_op jit(solution)/shard_map/ppermute | solution.py:497
  8.9 3.2 %shard_map.85 = (f32[64,2048]{1,0:T(8,128)S(1)}, f32[8,128]{1,0:T(8,128)}) custom-call(s32[5]{0:T(128)S(1)} %stack.27.refs_0_.flag_ref, s32[1,2048]{1,0:T(1,128)S(1)} %bitcast.28, bf16[256,512]{1,0:T(8,128)(2,1)S(1)} %pad_maximum_fusion.refs_2_, bf16[2048,512]{1,0:T(8,128)(2,1)} %refs_1_.3), custom_call_target="tpu_custom_call" | custom-call | flops 536870912 | bytes 2097152 | tf_op jit(solution)/shard_map/pallas_call | solution.py:31
  12.4 1.7 %collective-permute-done.3.refs_3_ = f32[64,2048]{1,0:T(8,128)S(1)} collective-permute-done((f32[64,2048]{1,0:T(8,128)S(1)}, f32[64,2048]{1,0:T(8,128)S(1)}, u32[]{:S(2)}, u32[]{:S(2)}) %collective-permute-start.3) | collective-permute-done | bytes 524320 | tf_op jit(solution)/shard_map/ppermute | solution.py:497
  14.1 3.3 %shard_map.86 = (bf16[256,768]{1,0:T(8,128)(2,1)S(1)}, bf16[256,2048]{1,0:T(8,128)(2,1)S(1)}, bf16[64,2048]{1,0:T(8,128)(2,1)S(1)}, bf16[64,1024]{1,0:T(8,128)(2,1)S(1)}, f32[8,128]{1,0:T(8,128)S(1)}) custom-call(s32[5]{0:T(128)S(1)} %stack.27.refs_0_.flag_ref, s32[1,2048]{1,0:T(1,128)S(1)} %bitcast.29, f32[64,2048]{1,0:T(8,128)S(1)} %get-tuple-element.65.refs_2_, ...), custom_call_target="tpu_custom_call" | custom-call | flops 805306368 | bytes 3145728 | tf_op jit(solution)/shard_map/pallas_call | solution.py:31
  17.4 1.6 %collective-permute-start.6 = (bf16[256,768]{1,0:T(8,128)(2,1)S(1)}, bf16[256,768]{1,0:T(8,128)(2,1)S(1)}, u32[]{:S(2)}, u32[]{:S(2)}) collective-permute-start(bf16[256,768]{1,0:T(8,128)(2,1)S(1)} %get-tuple-element.73.refs_3_), channel_id=1, source_target_pairs={{0,1},{1,0},{2,3},{3,2},{4,5},{5,4},{6,7},{7,6},{8,9},{9,8},{10,11... | collective-permute-start | bytes 1179656 | tf_op jit(solution)/shard_map/ppermute | solution.py:606
  19.0 1.3 %collective-permute-start.4 = (bf16[64,1024]{1,0:T(8,128)(2,1)S(1)}, bf16[64,1024]{1,0:T(8,128)(2,1)S(1)}, u32[]{:S(2)}, u32[]{:S(2)}) collective-permute-start(bf16[64,1024]{1,0:T(8,128)(2,1)S(1)} %get-tuple-element.69), channel_id=1, source_target_pairs={{0,8},{4,12},{8,0},{12,4},{1,9},{5,13},{9,1},{13,5},{2,10},{6,14},... | collective-permute-start | bytes 393224 | tf_op jit(solution)/shard_map/ppermute | solution.py:497
  20.4 4.3 %shard_map.87 = (bf16[256,640]{1,0:T(8,128)(2,1)S(1)}, bf16[256,640]{1,0:T(8,128)(2,1)S(1)}, f32[8,128]{1,0:T(8,128)S(1)}) custom-call(bf16[256,2048]{1,0:T(8,128)(2,1)S(1)} %get-tuple-element.66.refs_0_, bf16[2048,2048]{1,0:T(8,128)(2,1)} %refs_2_.1, f32[8,128]{1,0:T(8,128)S(1)} %get-tuple-element.67.refs_2_), custom_call_target="tpu_custom_call" | custom-call | flops 1342177280 | bytes 5242880 | tf_op jit(solution)/shard_map/pallas_call | solution.py:31
  25.2 4.5 %all-to-all-start = ((bf16[4,2048,128]{2,1,0:T(8,128)(2,1)}), bf16[4,2048,128]{2,1,0:T(8,128)(2,1)}, u32[]{:S(2)}, u32[]{:S(2)}) async-start(bf16[4,2048,128]{2,1,0:T(8,128)(2,1)} %bitcast.33), calls=%async_computation | async-start | bytes 4194304 | tf_op jit(solution)/shard_map/all_to_all | solution.py:500
  30.8 0.7 collective-permute-start.9
  31.5 4.4 %collective-permute-start.8 = (bf16[256,640]{1,0:T(8,128)(2,1)S(1)}, bf16[256,640]{1,0:T(8,128)(2,1)S(1)}, u32[]{:S(2)}, u32[]{:S(2)}) collective-permute-start(bf16[256,640]{1,0:T(8,128)(2,1)S(1)} %get-tuple-element.81), channel_id=1, source_target_pairs={{0,1},{1,0},{2,3},{3,2},{4,5},{5,4},{6,7},{7,6},{8,9},{9,8},{10,11... | collective-permute-start | bytes 983048 | tf_op jit(solution)/shard_map/ppermute | solution.py:606
  35.9 3.5 %shard_map.89 = (bf16[256,640]{1,0:T(8,128)(2,1)S(1)}, bf16[64,2048]{1,0:T(8,128)(2,1)}, f32[8,128]{1,0:T(8,128)S(1)}) custom-call(s32[5]{0:T(128)S(1)} %stack.27.refs_0_.flag_ref, s32[1,2048]{1,0:T(1,128)S(1)} %bitcast.30, bf16[64,1024]{1,0:T(8,128)(2,1)S(1)} %collective-permute-done.4.refs_2_, bf16[64,1024]{1,0:T(8,128)(2,1)S(1)} %collective-permute-done.5.refs_3_, ...), custom_call_target="tpu_custom_call" | custom-call | flops 671088640 | bytes 2621440 | tf_op jit(solution)/shard_map/pallas_call | solution.py:31
  40.2 0.7 collective-permute-start.13
  40.9 5.2 %shard_map.91 = (bf16[256,768]{1,0:T(8,128)(2,1)S(1)}, bf16[256,640]{1,0:T(8,128)(2,1)S(1)}, bf16[64,2048]{1,0:T(8,128)(2,1)S(1)}, f32[8,128]{1,0:T(8,128)S(1)}) custom-call(s32[5]{0:T(128)S(1)} %stack.27.refs_0_.flag_ref, s32[1,2048]{1,0:T(1,128)S(1)} %bitcast.31, bf16[64,1024]{1,0:T(8,128)(2,1)S(1)} %collective-permute-done.4.refs_2_, ...), custom_call_target="tpu_custom_call" | custom-call | flops 1476395008 | bytes 5767168 | tf_op jit(solution)/shard_map/pallas_call | solution.py:31
  46.8 3.8 %collective-permute-start.10 = (bf16[256,768]{1,0:T(8,128)(2,1)S(1)}, bf16[256,768]{1,0:T(8,128)(2,1)S(1)}, u32[]{:S(2)}, u32[]{:S(2)}) collective-permute-start(bf16[256,768]{1,0:T(8,128)(2,1)S(1)} %get-tuple-element.84.refs_5_), channel_id=1, source_target_pairs={{0,1},{1,0},{2,3},{3,2},{4,5},{5,4},{6,7},{7,6},{8,9},{9,8},{10,11... | collective-permute-start | bytes 1179656 | tf_op jit(solution)/shard_map/ppermute | solution.py:606
  50.6 0.7 collective-permute-start.11
  51.3 1.5 %shard_map.93 = (bf16[256,640]{1,0:T(8,128)(2,1)}, bf16[256,640]{1,0:T(8,128)(2,1)}, f32[8,128]{1,0:T(8,128)S(1)}) custom-call(s32[5]{0:T(128)S(1)} %stack.27.refs_0_.flag_ref, bf16[256,640]{1,0:T(8,128)(2,1)S(1)} %get-tuple-element.86.refs_1_.refs_2_, bf16[256,640]{1,0:T(8,128)(2,1)S(1)} %collective-permute-done.12.refs_2_, ...), custom_call_target="tpu_custom_call" | custom-call | flops 15000000512 | bytes 24000000 | tf_op jit(solution)/shard_map/pallas_call | solution.py:31
  52.8 2.9 %collective-permute-start.17 = (bf16[256,640]{1,0:T(8,128)(2,1)}, bf16[256,640]{1,0:T(8,128)(2,1)}, u32[]{:S(2)}, u32[]{:S(2)}) collective-permute-start(bf16[256,640]{1,0:T(8,128)(2,1)} %get-tuple-element.95.refs_5_), channel_id=1, source_target_pairs={{0,1},{1,0},{2,3},{3,2},{4,5},{5,4},{6,7},{7,6},{8,9},{9,8},{10,11... | collective-permute-start | bytes 983048 | tf_op jit(solution)/shard_map/ppermute | solution.py:606
  55.7 1.4 %collective-permute-start.18 = (bf16[256,640]{1,0:T(8,128)(2,1)}, bf16[256,640]{1,0:T(8,128)(2,1)}, u32[]{:S(2)}, u32[]{:S(2)}) collective-permute-start(bf16[256,640]{1,0:T(8,128)(2,1)} %get-tuple-element.96.refs_3_), channel_id=1, source_target_pairs={{1,2},{2,1},{5,6},{6,5},{9,10},{10,9},{13,14},{14,13},{17,18},{18,... | collective-permute-start | bytes 983048 | tf_op jit(solution)/shard_map/ppermute | solution.py:608
  57.1 5.6 %shard_map.94 = (f32[128,2048]{1,0:T(8,128)S(1)}, f32[8,128]{1,0:T(8,128)S(1)}) custom-call(s32[16]{0:T(128)S(1)} %gather_fusion, bf16[4,2048,128]{2,1,0:T(8,128)(2,1)} %all-to-all-done.refs_1_.refs_2_, bf16[2048,2048]{1,0:T(8,128)(2,1)} %refs_2_.1, f32[8,128]{1,0:T(8,128)S(1)} %get-tuple-element.90.refs_3_), custom_call_target="tpu_custom_call" | custom-call | flops 2147483648 | bytes 8388608 | tf_op jit(solution)/shard_map/pallas_call | solution.py:31
  62.7 1.5 %shard_map.95 = (bf16[256,768]{1,0:T(8,128)(2,1)S(1)}, bf16[256,640]{1,0:T(8,128)(2,1)}, bf16[256,768]{1,0:T(8,128)(2,1)S(1)}, f32[8,128]{1,0:T(8,128)S(1)}) custom-call(s32[5]{0:T(128)S(1)} %stack.27.refs_0_.flag_ref, bf16[256,768]{1,0:T(8,128)(2,1)S(1)} %collective-permute-done.10.refs_1_, bf16[256,768]{1,0:T(8,128)(2,1)S(1)} %get-tuple-element.80.refs_1_.refs_2_, ...), custom_call_target="tpu_custom_call" | custom-call | flops 15000000512 | bytes 24000000 | tf_op jit(solution)/shard_map/pallas_call | solution.py:31
  64.1 1.4 %collective-permute-start.15 = (bf16[256,768]{1,0:T(8,128)(2,1)S(1)}, bf16[256,768]{1,0:T(8,128)(2,1)}, u32[]{:S(2)}, u32[]{:S(2)}) collective-permute-start(bf16[256,768]{1,0:T(8,128)(2,1)S(1)} %get-tuple-element.93.refs_2_), channel_id=1, source_target_pairs={{1,2},{2,1},{5,6},{6,5},{9,10},{10,9},{13,14},{14,13},{17,18},{18,... | collective-permute-start | bytes 1179656 | tf_op jit(solution)/shard_map/ppermute | solution.py:608
  65.5 3.1 %collective-permute-start.14 = (bf16[256,640]{1,0:T(8,128)(2,1)}, bf16[256,640]{1,0:T(8,128)(2,1)}, u32[]{:S(2)}, u32[]{:S(2)}) collective-permute-start(bf16[256,640]{1,0:T(8,128)(2,1)} %get-tuple-element.92.refs_4_), channel_id=1, source_target_pairs={{0,1},{1,0},{2,3},{3,2},{4,5},{5,4},{6,7},{7,6},{8,9},{9,8},{10,11... | collective-permute-start | bytes 983048 | tf_op jit(solution)/shard_map/ppermute | solution.py:606
  68.7 2.5 %shard_map.96 = (bf16[256,640]{1,0:T(8,128)(2,1)}, bf16[256,640]{1,0:T(8,128)(2,1)}, bf16[256,1408]{1,0:T(8,128)(2,1)}, f32[8,128]{1,0:T(8,128)S(1)}) custom-call(s32[5]{0:T(128)S(1)} %stack.27.refs_0_.flag_ref, bf16[256,640]{1,0:T(8,128)(2,1)} %collective-permute-done.17.refs_1_, bf16[256,640]{1,0:T(8,128)(2,1)S(1)} %copy-done.4, ...), custom_call_target="tpu_custom_call" | custom-call | flops 15000000512 | bytes 24000000 | tf_op jit(solution)/shard_map/pallas_call | solution.py:31
  71.3 1.4 %collective-permute-start.20 = (bf16[256,640]{1,0:T(8,128)(2,1)}, bf16[256,640]{1,0:T(8,128)(2,1)}, u32[]{:S(2)}, u32[]{:S(2)}) collective-permute-start(bf16[256,640]{1,0:T(8,128)(2,1)} %get-tuple-element.104.refs_2_), channel_id=1, source_target_pairs={{1,2},{2,1},{5,6},{6,5},{9,10},{10,9},{13,14},{14,13},{17,18},{18,... | collective-permute-start | bytes 983048 | tf_op jit(solution)/shard_map/ppermute | solution.py:608
  72.7 3.5 %all-to-all-start.1 = ((bf16[4,64,1408]{2,1,0:T(8,128)(2,1)}), bf16[4,64,1408]{2,1,0:T(8,128)(2,1)S(1)}, u32[]{:S(2)}, u32[]{:S(2)}) async-start(bf16[4,64,1408]{2,1,0:T(8,128)(2,1)} %bitcast.13), calls=%async_computation.1 | async-start | bytes 1441792 | tf_op jit(solution)/shard_map/all_to_all | solution.py:500
  76.5 1.0 copy-done.2
  77.5 1.7 %shard_map.97 = (bf16[256,768]{1,0:T(8,128)(2,1)S(1)}, bf16[256,640]{1,0:T(8,128)(2,1)S(1)}, f32[64,2048]{1,0:T(8,128)S(1)}, bf16[64,2048]{1,0:T(8,128)(2,1)S(1)}, f32[8,128]{1,0:T(8,128)S(1)}) custom-call(s32[5]{0:T(128)S(1)} %stack.27.refs_0_.flag_ref, bf16[256,640]{1,0:T(8,128)(2,1)} %collective-permute-done.14.refs_1_, bf16[256,768]{1,0:T(8,128)(2,1)S(1)} %copy-done.2, ...), custom_call_target="tpu_custom_call" | custom-call | flops 15000000512 | bytes 24000000 | tf_op jit(solution)/shard_map/pallas_call | solution.py:31
  79.1 1.8 %collective-permute-start.26 = (bf16[64,2048]{1,0:T(8,128)(2,1)S(1)}, bf16[64,2048]{1,0:T(8,128)(2,1)S(1)}, u32[]{:S(2)}, u32[]{:S(2)}) collective-permute-start(bf16[64,2048]{1,0:T(8,128)(2,1)S(1)} %get-tuple-element.114), channel_id=1, source_target_pairs={{0,8},{4,12},{8,0},{12,4},{1,9},{5,13},{9,1},{13,5},{2,10},{6,14},... | collective-permute-start | bytes 786440 | tf_op jit(solution)/shard_map/ppermute | solution.py:497
  81.0 3.1 %collective-permute-start.25 = (bf16[256,768]{1,0:T(8,128)(2,1)S(1)}, bf16[256,768]{1,0:T(8,128)(2,1)S(1)}, u32[]{:S(2)}, u32[]{:S(2)}) collective-permute-start(bf16[256,768]{1,0:T(8,128)(2,1)S(1)} %get-tuple-element.112.refs_2_), channel_id=1, source_target_pairs={{0,1},{1,0},{2,3},{3,2},{4,5},{5,4},{6,7},{7,6},{8,9},{9,8},{10,11... | collective-permute-start | bytes 1179656 | tf_op jit(solution)/shard_map/ppermute | solution.py:606
  84.1 6.6 %shard_map.98 = (bf16[2048,2048]{1,0:T(8,128)(2,1)}, f32[8,128]{1,0:T(8,128)S(1)}) custom-call(s32[5]{0:T(128)S(1)} %stack.27.refs_0_.flag_ref, s32[16]{0:T(128)S(1)} %gather_fusion, bf16[4,2048,128]{2,1,0:T(8,128)(2,1)} %all-to-all-done.refs_1_.refs_2_, bf16[64,2048]{1,0:T(8,128)(2,1)S(1)} %copy-done.6, bf16[64,2048]{1,0:T(8,128)(2,1)S(1)} %copy-done.8, ...), custom_call_target="tpu_custom_call" | custom-call | flops 2147483648 | bytes 8388608 | tf_op jit(solution)/shard_map/pallas_call | solution.py:31
  90.7 2.1 %shard_map.99 = (bf16[256,640]{1,0:T(8,128)(2,1)S(1)}, bf16[64,1280]{1,0:T(8,128)(2,1)S(1)}, bf16[64,1280]{1,0:T(8,128)(2,1)}, bf16[64,1280]{1,0:T(8,128)(2,1)},...) custom-call(s32[5]{0:T(128)S(1)} %stack.27.refs_0_.flag_ref, bf16[256,640]{1,0:T(8,128)(2,1)} %collective-permute-done.19.refs_1_, ...), custom_call_target="tpu_custom_call" | custom-call | flops 15000000512 | bytes 24000000 | tf_op jit(solution)/shard_map/pallas_call | solution.py:31
  92.8 0.7 copy-done.9
  93.6 1.8 %collective-permute-start.23 = (bf16[64,1280]{1,0:T(8,128)(2,1)S(1)}, bf16[64,1280]{1,0:T(8,128)(2,1)S(1)}, u32[]{:S(2)}, u32[]{:S(2)}) collective-permute-start(bf16[64,1280]{1,0:T(8,128)(2,1)S(1)} %get-tuple-element.110), channel_id=1, source_target_pairs={{0,12},{4,8},{8,4},{12,0},{1,13},{5,9},{9,5},{13,1},{2,14},{6,10},... | collective-permute-start | bytes 491528 | tf_op jit(solution)/shard_map/ppermute | solution.py:497
  95.3 3.3 %shard_map.100 = (bf16[256,512]{1,0:T(8,128)(2,1)}, f32[8,128]{1,0:T(8,128)S(1)}) custom-call(s32[5]{0:T(128)S(1)} %stack.27.refs_0_.flag_ref, bf16[2048,512]{1,0:T(8,128)(2,1)} %refs_1_.3, f32[64,2048]{1,0:T(8,128)S(1)} %get-tuple-element.113.refs_2_, bf16[64,2048]{1,0:T(8,128)(2,1)S(1)} %collective-permute-done.26.refs_3_, s32[1,2048]{1,0:T(1,128)S(1)} %bitcast.32, ...), custom_call_target="tpu_custom_call" | custom-call | flops 1 | bytes 24000000 | tf_op jit(solution)/shard_map/pallas_call | solution.py:31
  98.7 4.1 %all-to-all-start.2 = ((bf16[16,16,512]{2,1,0:T(8,128)(2,1)}), bf16[16,16,512]{2,1,0:T(8,128)(2,1)S(1)}, u32[]{:S(2)}, u32[]{:S(2)}) async-start(bf16[16,16,512]{2,1,0:T(8,128)(2,1)} %bitcast.16), calls=%async_computation.2 | async-start | bytes 524288 | tf_op jit(solution)/shard_map/all_to_all | solution.py:576
  104.5 1.7 %collective-permute-start.28 = (bf16[64,1408]{1,0:T(8,128)(2,1)S(1)}, bf16[64,1408]{1,0:T(8,128)(2,1)S(1)}, u32[]{:S(2)}, u32[]{:S(2)}) collective-permute-start(bf16[64,1408]{1,0:T(8,128)(2,1)S(1)} %get-tuple-element.121), channel_id=1, source_target_pairs={{0,8},{4,12},{8,0},{12,4},{1,9},{5,13},{9,1},{13,5},{2,10},{6,14},... | collective-permute-start | bytes 540680 | tf_op jit(solution)/shard_map/ppermute | solution.py:497
  106.2 1.6 %shard_map.103.refs_9_ = bf16[8192,128]{1,0:T(8,128)(2,1)} custom-call(s32[5]{0:T(128)S(1)} %stack.27.refs_0_.flag_ref, bf16[256,1408]{1,0:T(8,128)(2,1)S(1)} %bitcast.26, bf16[64,1280]{1,0:T(8,128)(2,1)S(1)} %copy-done.10, bf16[64,1280]{1,0:T(8,128)(2,1)S(1)} %collective-permute-done.21.refs_2_, bf16[64,1280]{1,0:T(8,128)(2,1)S(1)} %collective-permute-done.22.refs_3_, ...), custom_call_target="tpu_custom_call" | custom-call | flops 15000000512 | bytes 2621440 | tf_op jit(solution)/shard_map/pallas_call | solution.py:248
  107.8 5.0 %all-to-all-done.2 = bf16[16,16,512]{2,1,0:T(8,128)(2,1)S(1)} async-done(((bf16[16,16,512]{2,1,0:T(8,128)(2,1)}), bf16[16,16,512]{2,1,0:T(8,128)(2,1)S(1)}, u32[]{:S(2)}, u32[]{:S(2)}) %all-to-all-start.2) | async-done | bytes 262176 | tf_op jit(solution)/shard_map/all_to_all | solution.py:576
  113.7 1.2 collective-permute-start.31
  114.9 2.9 %collective-permute-start.32 = (bf16[16,2048]{1,0:T(8,128)(2,1)S(1)}, bf16[16,2048]{1,0:T(8,128)(2,1)S(1)}, u32[]{:S(2)}, u32[]{:S(2)}) collective-permute-start(bf16[16,2048]{1,0:T(8,128)(2,1)S(1)} %get-tuple-element.125.refs_1_), channel_id=1, source_target_pairs={{0,3},{1,2},{2,1},{3,0},{4,7},{5,6},{6,5},{7,4},{8,11},{9,10},{10,... | collective-permute-start | bytes 196616 | tf_op jit(solution)/shard_map/ppermute | solution.py:613
  117.8 1.9 %shard_map.104 = bf16[8192,128]{1,0:T(8,128)(2,1)} custom-call(s32[5]{0:T(128)S(1)} %stack.27.refs_0_.flag_ref, bf16[256,1408]{1,0:T(8,128)(2,1)S(1)} %bitcast.27, bf16[64,1280]{1,0:T(8,128)(2,1)S(1)} %copy-done.10, bf16[64,1280]{1,0:T(8,128)(2,1)S(1)} %collective-permute-done.21.refs_2_, ...), custom_call_target="tpu_custom_call", output_to_operand_aliasing={{}: (10, {})} | custom-call | flops 15000000512 | bytes 5767168 | tf_op jit(solution)/shard_map/pallas_call | solution.py:248
  119.8 2.3 %collective-permute-done.31.refs_3_ = bf16[16,2048]{1,0:T(8,128)(2,1)S(1)} collective-permute-done((bf16[16,2048]{1,0:T(8,128)(2,1)S(1)}, bf16[16,2048]{1,0:T(8,128)(2,1)S(1)}, u32[]{:S(2)}, u32[]{:S(2)}) %collective-permute-start.31) | collective-permute-done | bytes 65568 | tf_op jit(solution)/shard_map/ppermute | solution.py:613
  122.1 1.3 %shard_map.106 = (bf16[64,2048]{1,0:T(8,128)(2,1)}, f32[8,128]{1,0:T(8,128)}) custom-call(s32[5]{0:T(128)S(1)} %stack.27.refs_0_.flag_ref, bf16[16,2048]{1,0:T(8,128)(2,1)S(1)} %get-tuple-element.125.refs_1_, bf16[16,2048]{1,0:T(8,128)(2,1)S(1)} %collective-permute-done.30.refs_2_, bf16[16,2048]{1,0:T(8,128)(2,1)S(1)} %collective-permute-done.31.refs_3_, ...), custom_call_target="tpu_custom_call" | custom-call | flops 1 | bytes 524288 | tf_op jit(solution)/shard_map/pallas_call | solution.py:31
  (75 shorter events, 7.2 us)
Async XLA Ops:
  0.6 4.9 %copy-start = (s32[4]{0:T(128)S(1)}, s32[4]{0:T(128)}, u32[]{:S(2)}) copy-start(s32[4]{0:T(128)} %param.9) | copy-start | bytes 52
  1.6 4.6 %collective-permute-start = (bf16[64,512]{1,0:T(8,128)(2,1)S(1)}, bf16[64,512]{1,0:T(8,128)(2,1)S(1)}, u32[]{:S(2)}, u32[]{:S(2)}) collective-permute-start(bf16[64,512]{1,0:T(8,128)(2,1)S(1)} %get-tuple-element.128), channel_id=1, source_target_pairs={{0,4},{4,0},{8,12},{12,8},{1,5},{5,1},{9,13},{13,9},{2,6},{6,2},{1... | collective-permute-start | bytes 196616 | tf_op jit(solution)/shard_map/ppermute | solution.py:497
  2.2 5.3 %collective-permute-start.1 = (bf16[64,512]{1,0:T(8,128)(2,1)S(1)}, bf16[64,512]{1,0:T(8,128)(2,1)S(1)}, u32[]{:S(2)}, u32[]{:S(2)}) collective-permute-start(bf16[64,512]{1,0:T(8,128)(2,1)S(1)} %get-tuple-element.130), channel_id=1, source_target_pairs={{0,8},{4,12},{8,0},{12,4},{1,9},{5,13},{9,1},{13,5},{2,10},{6,14},... | collective-permute-start | bytes 196616 | tf_op jit(solution)/shard_map/ppermute | solution.py:497
  4.7 4.0 %collective-permute-start.2 = (bf16[64,512]{1,0:T(8,128)(2,1)S(1)}, bf16[64,512]{1,0:T(8,128)(2,1)S(1)}, u32[]{:S(2)}, u32[]{:S(2)}) collective-permute-start(bf16[64,512]{1,0:T(8,128)(2,1)S(1)} %get-tuple-element.129), channel_id=1, source_target_pairs={{0,12},{4,8},{8,4},{12,0},{1,13},{5,9},{9,5},{13,1},{2,14},{6,10},... | collective-permute-start | bytes 196616 | tf_op jit(solution)/shard_map/ppermute | solution.py:497
  12.1 2.0 %collective-permute-start.3 = (f32[64,2048]{1,0:T(8,128)S(1)}, f32[64,2048]{1,0:T(8,128)S(1)}, u32[]{:S(2)}, u32[]{:S(2)}) collective-permute-start(f32[64,2048]{1,0:T(8,128)S(1)} %get-tuple-element.65.refs_2_), channel_id=1, source_target_pairs={{0,4},{4,0},{8,12},{12,8},{1,5},{5,1},{9,13},{13,9},{2,6},{6,2},{1... | collective-permute-start | bytes 1572872 | tf_op jit(solution)/shard_map/ppermute | solution.py:497
  17.4 7.3 %copy-start.5 = (bf16[64,2048]{1,0:T(8,128)(2,1)}, bf16[64,2048]{1,0:T(8,128)(2,1)S(1)}, u32[]{:S(2)}) copy-start(bf16[64,2048]{1,0:T(8,128)(2,1)S(1)} %get-tuple-element.71.refs_3_) | copy-start | bytes 786436
  17.4 12.7 %collective-permute-start.6 = (bf16[256,768]{1,0:T(8,128)(2,1)S(1)}, bf16[256,768]{1,0:T(8,128)(2,1)S(1)}, u32[]{:S(2)}, u32[]{:S(2)}) collective-permute-start(bf16[256,768]{1,0:T(8,128)(2,1)S(1)} %get-tuple-element.73.refs_3_), channel_id=1, source_target_pairs={{0,1},{1,0},{2,3},{3,2},{4,5},{5,4},{6,7},{7,6},{8,9},{9,8},{10,11... | collective-permute-start | bytes 1179656 | tf_op jit(solution)/shard_map/ppermute | solution.py:606
  19.0 6.2 %collective-permute-start.4 = (bf16[64,1024]{1,0:T(8,128)(2,1)S(1)}, bf16[64,1024]{1,0:T(8,128)(2,1)S(1)}, u32[]{:S(2)}, u32[]{:S(2)}) collective-permute-start(bf16[64,1024]{1,0:T(8,128)(2,1)S(1)} %get-tuple-element.69), channel_id=1, source_target_pairs={{0,8},{4,12},{8,0},{12,4},{1,9},{5,13},{9,1},{13,5},{2,10},{6,14},... | collective-permute-start | bytes 393224 | tf_op jit(solution)/shard_map/ppermute | solution.py:497
  24.7 14.8 %collective-permute-start.7 = (bf16[256,640]{1,0:T(8,128)(2,1)S(1)}, bf16[256,640]{1,0:T(8,128)(2,1)S(1)}, u32[]{:S(2)}, u32[]{:S(2)}) collective-permute-start(bf16[256,640]{1,0:T(8,128)(2,1)S(1)} %get-tuple-element.76.refs_3_), channel_id=1, source_target_pairs={{0,1},{1,0},{2,3},{3,2},{4,5},{5,4},{6,7},{7,6},{8,9},{9,8},{10,11... | collective-permute-start | bytes 983048 | tf_op jit(solution)/shard_map/ppermute | solution.py:606
  25.2 31.8 %all-to-all-start = ((bf16[4,2048,128]{2,1,0:T(8,128)(2,1)}), bf16[4,2048,128]{2,1,0:T(8,128)(2,1)}, u32[]{:S(2)}, u32[]{:S(2)}) async-start(bf16[4,2048,128]{2,1,0:T(8,128)(2,1)} %bitcast.33), calls=%async_computation | async-start | bytes 4194304 | tf_op jit(solution)/shard_map/all_to_all | solution.py:500
  29.7 6.3 %collective-permute-start.5 = (bf16[64,1024]{1,0:T(8,128)(2,1)S(1)}, bf16[64,1024]{1,0:T(8,128)(2,1)S(1)}, u32[]{:S(2)}, u32[]{:S(2)}) collective-permute-start(bf16[64,1024]{1,0:T(8,128)(2,1)S(1)} %collective-permute-done.4.refs_2_), channel_id=1, source_target_pairs={{0,4},{4,0},{8,12},{12,8},{1,5},{5,1},{9,13},{13,9},{2,6},{6,2},{1... | collective-permute-start | bytes 393224 | tf_op jit(solution)/shard_map/ppermute | solution.py:497
  30.8 15.3 %collective-permute-start.9 = (bf16[256,768]{1,0:T(8,128)(2,1)S(1)}, bf16[256,768]{1,0:T(8,128)(2,1)S(1)}, u32[]{:S(2)}, u32[]{:S(2)}) collective-permute-start(bf16[256,768]{1,0:T(8,128)(2,1)S(1)} %get-tuple-element.82.refs_4_), channel_id=1, source_target_pairs={{1,2},{2,1},{5,6},{6,5},{9,10},{10,9},{13,14},{14,13},{17,18},{18,... | collective-permute-start | bytes 1179656 | tf_op jit(solution)/shard_map/ppermute | solution.py:608
  31.5 14.6 %collective-permute-start.8 = (bf16[256,640]{1,0:T(8,128)(2,1)S(1)}, bf16[256,640]{1,0:T(8,128)(2,1)S(1)}, u32[]{:S(2)}, u32[]{:S(2)}) collective-permute-start(bf16[256,640]{1,0:T(8,128)(2,1)S(1)} %get-tuple-element.81), channel_id=1, source_target_pairs={{0,1},{1,0},{2,3},{3,2},{4,5},{5,4},{6,7},{7,6},{8,9},{9,8},{10,11... | collective-permute-start | bytes 983048 | tf_op jit(solution)/shard_map/ppermute | solution.py:606
  40.1 11.1 %collective-permute-start.12 = (bf16[256,640]{1,0:T(8,128)(2,1)S(1)}, bf16[256,640]{1,0:T(8,128)(2,1)S(1)}, u32[]{:S(2)}, u32[]{:S(2)}) collective-permute-start(bf16[256,640]{1,0:T(8,128)(2,1)S(1)} %get-tuple-element.87), channel_id=1, source_target_pairs={{0,1},{1,0},{2,3},{3,2},{4,5},{5,4},{6,7},{7,6},{8,9},{9,8},{10,11... | collective-permute-start | bytes 983048 | tf_op jit(solution)/shard_map/ppermute | solution.py:606
  40.2 11.1 %collective-permute-start.13 = (bf16[256,640]{1,0:T(8,128)(2,1)S(1)}, bf16[256,640]{1,0:T(8,128)(2,1)S(1)}, u32[]{:S(2)}, u32[]{:S(2)}) collective-permute-start(bf16[256,640]{1,0:T(8,128)(2,1)S(1)} %get-tuple-element.88.refs_4_), channel_id=1, source_target_pairs={{1,2},{2,1},{5,6},{6,5},{9,10},{10,9},{13,14},{14,13},{17,18},{18,... | collective-permute-start | bytes 983048 | tf_op jit(solution)/shard_map/ppermute | solution.py:608
  46.1 0.7 copy-start.7
  46.1 5.2 %copy-start.3 = (bf16[256,640]{1,0:T(8,128)(2,1)}, bf16[256,640]{1,0:T(8,128)(2,1)S(1)}, u32[]{:S(2)}) copy-start(bf16[256,640]{1,0:T(8,128)(2,1)S(1)} %get-tuple-element.86.refs_1_.refs_2_) | copy-start | bytes 983044
  46.8 15.9 %collective-permute-start.10 = (bf16[256,768]{1,0:T(8,128)(2,1)S(1)}, bf16[256,768]{1,0:T(8,128)(2,1)S(1)}, u32[]{:S(2)}, u32[]{:S(2)}) collective-permute-start(bf16[256,768]{1,0:T(8,128)(2,1)S(1)} %get-tuple-element.84.refs_5_), channel_id=1, source_target_pairs={{0,1},{1,0},{2,3},{3,2},{4,5},{5,4},{6,7},{7,6},{8,9},{9,8},{10,11... | collective-permute-start | bytes 1179656 | tf_op jit(solution)/shard_map/ppermute | solution.py:606
  50.6 12.1 %collective-permute-start.11 = (bf16[256,640]{1,0:T(8,128)(2,1)S(1)}, bf16[256,640]{1,0:T(8,128)(2,1)S(1)}, u32[]{:S(2)}, u32[]{:S(2)}) collective-permute-start(bf16[256,640]{1,0:T(8,128)(2,1)S(1)} %get-tuple-element.85.refs_3_), channel_id=1, source_target_pairs={{1,2},{2,1},{5,6},{6,5},{9,10},{10,9},{13,14},{14,13},{17,18},{18,... | collective-permute-start | bytes 983048 | tf_op jit(solution)/shard_map/ppermute | solution.py:608
  52.8 15.9 %collective-permute-start.17 = (bf16[256,640]{1,0:T(8,128)(2,1)}, bf16[256,640]{1,0:T(8,128)(2,1)}, u32[]{:S(2)}, u32[]{:S(2)}) collective-permute-start(bf16[256,640]{1,0:T(8,128)(2,1)} %get-tuple-element.95.refs_5_), channel_id=1, source_target_pairs={{0,1},{1,0},{2,3},{3,2},{4,5},{5,4},{6,7},{7,6},{8,9},{9,8},{10,11... | collective-permute-start | bytes 983048 | tf_op jit(solution)/shard_map/ppermute | solution.py:606
  55.7 13.0 %collective-permute-start.18 = (bf16[256,640]{1,0:T(8,128)(2,1)}, bf16[256,640]{1,0:T(8,128)(2,1)}, u32[]{:S(2)}, u32[]{:S(2)}) collective-permute-start(bf16[256,640]{1,0:T(8,128)(2,1)} %get-tuple-element.96.refs_3_), channel_id=1, source_target_pairs={{1,2},{2,1},{5,6},{6,5},{9,10},{10,9},{13,14},{14,13},{17,18},{18,... | collective-permute-start | bytes 983048 | tf_op jit(solution)/shard_map/ppermute | solution.py:608
  62.7 6.0 %copy-start.4 = (bf16[256,640]{1,0:T(8,128)(2,1)S(1)}, bf16[256,640]{1,0:T(8,128)(2,1)}, u32[]{:S(2)}) copy-start(bf16[256,640]{1,0:T(8,128)(2,1)} %copy-done.3) | copy-start | bytes 983044
  64.1 7.1 %copy-start.1 = (bf16[256,768]{1,0:T(8,128)(2,1)}, bf16[256,768]{1,0:T(8,128)(2,1)S(1)}, u32[]{:S(2)}) copy-start(bf16[256,768]{1,0:T(8,128)(2,1)S(1)} %get-tuple-element.93.refs_2_) | copy-start | bytes 1179652
  64.1 12.3 %collective-permute-start.15 = (bf16[256,768]{1,0:T(8,128)(2,1)S(1)}, bf16[256,768]{1,0:T(8,128)(2,1)}, u32[]{:S(2)}, u32[]{:S(2)}) collective-permute-start(bf16[256,768]{1,0:T(8,128)(2,1)S(1)} %get-tuple-element.93.refs_2_), channel_id=1, source_target_pairs={{1,2},{2,1},{5,6},{6,5},{9,10},{10,9},{13,14},{14,13},{17,18},{18,... | collective-permute-start | bytes 1179656 | tf_op jit(solution)/shard_map/ppermute | solution.py:608
  65.5 10.9 %collective-permute-start.14 = (bf16[256,640]{1,0:T(8,128)(2,1)}, bf16[256,640]{1,0:T(8,128)(2,1)}, u32[]{:S(2)}, u32[]{:S(2)}) collective-permute-start(bf16[256,640]{1,0:T(8,128)(2,1)} %get-tuple-element.92.refs_4_), channel_id=1, source_target_pairs={{0,1},{1,0},{2,3},{3,2},{4,5},{5,4},{6,7},{7,6},{8,9},{9,8},{10,11... | collective-permute-start | bytes 983048 | tf_op jit(solution)/shard_map/ppermute | solution.py:606
  68.7 7.8 %collective-permute-start.16 = (f32[128,2048]{1,0:T(8,128)S(1)}, f32[128,2048]{1,0:T(8,128)S(1)}, u32[]{:S(2)}, u32[]{:S(2)}) collective-permute-start(f32[128,2048]{1,0:T(8,128)S(1)} %get-tuple-element.94.refs_5_), channel_id=1, source_target_pairs={{0,4},{4,0},{8,12},{12,8},{1,5},{5,1},{9,13},{13,9},{2,6},{6,2},{1... | collective-permute-start | bytes 3145736 | tf_op jit(solution)/shard_map/ppermute | solution.py:497
  71.2 19.5 %collective-permute-start.19 = (bf16[256,640]{1,0:T(8,128)(2,1)}, bf16[256,640]{1,0:T(8,128)(2,1)}, u32[]{:S(2)}, u32[]{:S(2)}) collective-permute-start(bf16[256,640]{1,0:T(8,128)(2,1)} %get-tuple-element.103.refs_4_), channel_id=1, source_target_pairs={{0,1},{1,0},{2,3},{3,2},{4,5},{5,4},{6,7},{7,6},{8,9},{9,8},{10,11... | collective-permute-start | bytes 983048 | tf_op jit(solution)/shard_map/ppermute | solution.py:606
  71.3 19.4 %collective-permute-start.20 = (bf16[256,640]{1,0:T(8,128)(2,1)}, bf16[256,640]{1,0:T(8,128)(2,1)}, u32[]{:S(2)}, u32[]{:S(2)}) collective-permute-start(bf16[256,640]{1,0:T(8,128)(2,1)} %get-tuple-element.104.refs_2_), channel_id=1, source_target_pairs={{1,2},{2,1},{5,6},{6,5},{9,10},{10,9},{13,14},{14,13},{17,18},{18,... | collective-permute-start | bytes 983048 | tf_op jit(solution)/shard_map/ppermute | solution.py:608
  72.7 26.0 %all-to-all-start.1 = ((bf16[4,64,1408]{2,1,0:T(8,128)(2,1)}), bf16[4,64,1408]{2,1,0:T(8,128)(2,1)S(1)}, u32[]{:S(2)}, u32[]{:S(2)}) async-start(bf16[4,64,1408]{2,1,0:T(8,128)(2,1)} %bitcast.13), calls=%async_computation.1 | async-start | bytes 1441792 | tf_op jit(solution)/shard_map/all_to_all | solution.py:500
  76.5 1.0 copy-start.2
  77.5 6.6 %copy-start.6 = (bf16[64,2048]{1,0:T(8,128)(2,1)S(1)}, bf16[64,2048]{1,0:T(8,128)(2,1)}, u32[]{:S(2)}) copy-start(bf16[64,2048]{1,0:T(8,128)(2,1)} %copy-done.5) | copy-start | bytes 786436
  77.5 6.6 %copy-start.8 = (bf16[64,2048]{1,0:T(8,128)(2,1)S(1)}, bf16[64,2048]{1,0:T(8,128)(2,1)}, u32[]{:S(2)}) copy-start(bf16[64,2048]{1,0:T(8,128)(2,1)} %copy-done.7) | copy-start | bytes 786436
  79.1 14.4 %collective-permute-start.26 = (bf16[64,2048]{1,0:T(8,128)(2,1)S(1)}, bf16[64,2048]{1,0:T(8,128)(2,1)S(1)}, u32[]{:S(2)}, u32[]{:S(2)}) collective-permute-start(bf16[64,2048]{1,0:T(8,128)(2,1)S(1)} %get-tuple-element.114), channel_id=1, source_target_pairs={{0,8},{4,12},{8,0},{12,4},{1,9},{5,13},{9,1},{13,5},{2,10},{6,14},... | collective-permute-start | bytes 786440 | tf_op jit(solution)/shard_map/ppermute | solution.py:497
  81.0 21.8 %collective-permute-start.25 = (bf16[256,768]{1,0:T(8,128)(2,1)S(1)}, bf16[256,768]{1,0:T(8,128)(2,1)S(1)}, u32[]{:S(2)}, u32[]{:S(2)}) collective-permute-start(bf16[256,768]{1,0:T(8,128)(2,1)S(1)} %get-tuple-element.112.refs_2_), channel_id=1, source_target_pairs={{0,1},{1,0},{2,3},{3,2},{4,5},{5,4},{6,7},{7,6},{8,9},{9,8},{10,11... | collective-permute-start | bytes 1179656 | tf_op jit(solution)/shard_map/ppermute | solution.py:606
  92.8 0.7 copy-start.9
  93.4 9.9 %collective-permute-start.24 = (bf16[256,640]{1,0:T(8,128)(2,1)S(1)}, bf16[256,640]{1,0:T(8,128)(2,1)S(1)}, u32[]{:S(2)}, u32[]{:S(2)}) collective-permute-start(bf16[256,640]{1,0:T(8,128)(2,1)S(1)} %get-tuple-element.111.refs_2_), channel_id=1, source_target_pairs={{0,1},{1,0},{2,3},{3,2},{4,5},{5,4},{6,7},{7,6},{8,9},{9,8},{10,11... | collective-permute-start | bytes 983048 | tf_op jit(solution)/shard_map/ppermute | solution.py:606
  93.4 12.7 %collective-permute-start.21 = (bf16[64,1280]{1,0:T(8,128)(2,1)}, bf16[64,1280]{1,0:T(8,128)(2,1)S(1)}, u32[]{:S(2)}, u32[]{:S(2)}) collective-permute-start(bf16[64,1280]{1,0:T(8,128)(2,1)} %get-tuple-element.108), channel_id=1, source_target_pairs={{0,4},{4,0},{8,12},{12,8},{1,5},{5,1},{9,13},{13,9},{2,6},{6,2},{1... | collective-permute-start | bytes 491528 | tf_op jit(solution)/shard_map/ppermute | solution.py:497
  93.4 12.7 %collective-permute-start.22 = (bf16[64,1280]{1,0:T(8,128)(2,1)}, bf16[64,1280]{1,0:T(8,128)(2,1)S(1)}, u32[]{:S(2)}, u32[]{:S(2)}) collective-permute-start(bf16[64,1280]{1,0:T(8,128)(2,1)} %get-tuple-element.109), channel_id=1, source_target_pairs={{0,8},{4,12},{8,0},{12,4},{1,9},{5,13},{9,1},{13,5},{2,10},{6,14},... | collective-permute-start | bytes 491528 | tf_op jit(solution)/shard_map/ppermute | solution.py:497
  93.6 12.6 %collective-permute-start.23 = (bf16[64,1280]{1,0:T(8,128)(2,1)S(1)}, bf16[64,1280]{1,0:T(8,128)(2,1)S(1)}, u32[]{:S(2)}, u32[]{:S(2)}) collective-permute-start(bf16[64,1280]{1,0:T(8,128)(2,1)S(1)} %get-tuple-element.110), channel_id=1, source_target_pairs={{0,12},{4,8},{8,4},{12,0},{1,13},{5,9},{9,5},{13,1},{2,14},{6,10},... | collective-permute-start | bytes 491528 | tf_op jit(solution)/shard_map/ppermute | solution.py:497
  98.7 14.2 %all-to-all-start.2 = ((bf16[16,16,512]{2,1,0:T(8,128)(2,1)}), bf16[16,16,512]{2,1,0:T(8,128)(2,1)S(1)}, u32[]{:S(2)}, u32[]{:S(2)}) async-start(bf16[16,16,512]{2,1,0:T(8,128)(2,1)} %bitcast.16), calls=%async_computation.2 | async-start | bytes 524288 | tf_op jit(solution)/shard_map/all_to_all | solution.py:576
  103.4 2.8 %copy-start.10 = (bf16[64,1280]{1,0:T(8,128)(2,1)S(1)}, bf16[64,1280]{1,0:T(8,128)(2,1)}, u32[]{:S(2)}) copy-start(bf16[64,1280]{1,0:T(8,128)(2,1)} %copy-done.9) | copy-start | bytes 491524
  104.0 10.9 %collective-permute-start.27 = (bf16[64,1408]{1,0:T(8,128)(2,1)S(1)}, bf16[64,1408]{1,0:T(8,128)(2,1)S(1)}, u32[]{:S(2)}, u32[]{:S(2)}) collective-permute-start(bf16[64,1408]{1,0:T(8,128)(2,1)S(1)} %get-tuple-element.120), channel_id=1, source_target_pairs={{0,4},{4,0},{8,12},{12,8},{1,5},{5,1},{9,13},{13,9},{2,6},{6,2},{1... | collective-permute-start | bytes 540680 | tf_op jit(solution)/shard_map/ppermute | solution.py:497
  104.5 13.4 %collective-permute-start.28 = (bf16[64,1408]{1,0:T(8,128)(2,1)S(1)}, bf16[64,1408]{1,0:T(8,128)(2,1)S(1)}, u32[]{:S(2)}, u32[]{:S(2)}) collective-permute-start(bf16[64,1408]{1,0:T(8,128)(2,1)S(1)} %get-tuple-element.121), channel_id=1, source_target_pairs={{0,8},{4,12},{8,0},{12,4},{1,9},{5,13},{9,1},{13,5},{2,10},{6,14},... | collective-permute-start | bytes 540680 | tf_op jit(solution)/shard_map/ppermute | solution.py:497
  106.2 11.7 %collective-permute-start.29 = (bf16[64,1408]{1,0:T(8,128)(2,1)S(1)}, bf16[64,1408]{1,0:T(8,128)(2,1)S(1)}, u32[]{:S(2)}, u32[]{:S(2)}) collective-permute-start(bf16[64,1408]{1,0:T(8,128)(2,1)S(1)} %get-tuple-element.122), channel_id=1, source_target_pairs={{0,12},{4,8},{8,4},{12,0},{1,13},{5,9},{9,5},{13,1},{2,14},{6,10},... | collective-permute-start | bytes 540680 | tf_op jit(solution)/shard_map/ppermute | solution.py:497
  113.4 6.3 %collective-permute-start.30 = (bf16[16,2048]{1,0:T(8,128)(2,1)S(1)}, bf16[16,2048]{1,0:T(8,128)(2,1)S(1)}, u32[]{:S(2)}, u32[]{:S(2)}) collective-permute-start(bf16[16,2048]{1,0:T(8,128)(2,1)S(1)} %get-tuple-element.125.refs_1_), channel_id=1, source_target_pairs={{0,1},{1,0},{2,3},{3,2},{4,5},{5,4},{6,7},{7,6},{8,9},{9,8},{10,11... | collective-permute-start | bytes 196616 | tf_op jit(solution)/shard_map/ppermute | solution.py:613
  113.7 8.4 %collective-permute-start.31 = (bf16[16,2048]{1,0:T(8,128)(2,1)S(1)}, bf16[16,2048]{1,0:T(8,128)(2,1)S(1)}, u32[]{:S(2)}, u32[]{:S(2)}) collective-permute-start(bf16[16,2048]{1,0:T(8,128)(2,1)S(1)} %get-tuple-element.125.refs_1_), channel_id=1, source_target_pairs={{0,2},{1,3},{2,0},{3,1},{4,6},{5,7},{6,4},{7,5},{8,10},{9,11},{10,... | collective-permute-start | bytes 196616 | tf_op jit(solution)/shard_map/ppermute | solution.py:613
  114.9 7.2 %collective-permute-start.32 = (bf16[16,2048]{1,0:T(8,128)(2,1)S(1)}, bf16[16,2048]{1,0:T(8,128)(2,1)S(1)}, u32[]{:S(2)}, u32[]{:S(2)}) collective-permute-start(bf16[16,2048]{1,0:T(8,128)(2,1)S(1)} %get-tuple-element.125.refs_1_), channel_id=1, source_target_pairs={{0,3},{1,2},{2,1},{3,0},{4,7},{5,6},{6,5},{7,4},{8,11},{9,10},{10,... | collective-permute-start | bytes 196616 | tf_op jit(solution)/shard_map/ppermute | solution.py:613
